TPU v7x, 32 devices: a whole 2x2x4 slice. The times are simulated.
32 devices in a mesh: ctx: 8 (over y, x, core), tp: 4 (over z).
Axes of the slice: x: 2, y: 2, z: 4, core: 2. Of those that a mesh axis runs over, the one named last changes fastest.
Arguments:
- out_grad: bfloat16 [2048, 8192], P('ctx', 'tp'), may hold values from -6 to 6
- query_rows: bfloat16 [2048, 8192], P('ctx', 'tp'), may hold values from -6 to 6
- key_rows: bfloat16 [2048, 8192], P('ctx', 'tp'), may hold values from -6 to 6
- value_rows: bfloat16 [2048, 8192], P('ctx', 'tp'), may hold values from -6 to 6
- conv_rows: bfloat16 [2048, 8192], P('ctx', 'tp'), may hold values from -6 to 6
- long_filter: float32 [768, 8192], P('ctx', 'tp'), may hold values from -0.21650635 to 0.21650635
- block_table: int32 [16], replicated, may hold values from 0 to 15, each once
Outputs:
- q_grad: bfloat16 [2048, 8192], P('ctx', 'tp')
- k_grad: bfloat16 [2048, 8192], P('ctx', 'tp')
- v_grad: bfloat16 [2048, 8192], P('ctx', 'tp')
- filter_grad: float32 [768, 8192], P('ctx', 'tp')
Inputs may be any that keep to these rules, and one draw needn't show every extreme that they name: slot s, block s % 2 of the device with index s // 2 along ctx, holds sequence block block_table[s]; every block appears once.
All inputs are finite; a program needn't handle non-finite values.
Results may differ from a plain program's by a relative error of at most 0.009.
Values may be sent and summed in bfloat16 or wider, within the bound.
No kernel may reach another device: no remote copies, remote signals or barrier semaphores. Data moves between devices by JAX's collectives and lax.ppermute only.
A program may use at most 192 MiB of HBM per device.

v0:
```python
import math

import jax
import jax.numpy as jnp
from jax import lax
from jax.sharding import PartitionSpec as P

BLOCK = 128
LAG_BLOCKS = 6


HIGHEST_PRECISION = lax.Precision.HIGHEST


def dft_tables(length):
    indices = lax.iota(jnp.int32, length)
    phases = indices[:, None] * indices[None, :] % length
    angles = phases.astype(jnp.float32) * (2.0 * math.pi / length)
    return (jnp.cos(angles), jnp.sin(angles))


def forward_exact(blocks, cos_table, sine_table):
    in_rows = blocks.shape[1]
    real_part = jnp.einsum("wt,ntc->nwc", cos_table, blocks, precision=HIGHEST_PRECISION)
    imag_part = -jnp.einsum("wt,ntc->nwc", sine_table, blocks, precision=HIGHEST_PRECISION)
    return (real_part, imag_part)


def forward_low(blocks, cos_low, sine_low):
    in_rows = blocks.shape[1]
    real_part = jnp.einsum(
        "wt,ntc->nwc", cos_low[:, :in_rows], blocks, preferred_element_type=jnp.float32
    )
    imag_part = -jnp.einsum(
        "wt,ntc->nwc", sine_low[:, :in_rows], blocks, preferred_element_type=jnp.float32
    )
    return (real_part, imag_part)


def inverse(real_part, imag_part, cos_table, sine_table, out_rows):
    factor = 1.0 / cos_table.shape[0]
    cosine_part = jnp.einsum(
        "tw,nwc->ntc", cos_table[:out_rows], real_part, precision=HIGHEST_PRECISION
    )
    sine_part = jnp.einsum(
        "tw,nwc->ntc", sine_table[:out_rows], imag_part, precision=HIGHEST_PRECISION
    )
    return (cosine_part - sine_part) * factor


def filter_segments(full_filter, cos_table, sine_table):
    channels = full_filter.shape[1]
    filter_blocks = full_filter.reshape(LAG_BLOCKS, BLOCK, channels)
    zero_block = jnp.zeros((1, BLOCK, channels), jnp.float32)
    upper_half = jnp.concatenate([filter_blocks, zero_block], 0)
    lower_half = jnp.concatenate([zero_block, filter_blocks], 0)
    cyclic = jnp.concatenate([upper_half, lower_half], 1)
    return forward_exact(cyclic, cos_table, sine_table)


def settle_lags(lag_real, lag_imag, cos_table, sine_table, factor):
    times = inverse(lag_real, lag_imag, cos_table, sine_table, 2 * BLOCK)
    lagged = (times[:-1, :BLOCK] + times[1:, BLOCK:]) * factor
    return lagged.reshape(-1, times.shape[2])


def empty_state(slots, channels):
    slot_zeros = jnp.zeros((slots, 2 * BLOCK, channels), jnp.float32)
    lag_zeros = jnp.zeros((LAG_BLOCKS + 1, 2 * BLOCK, channels), jnp.float32)
    return (slot_zeros, slot_zeros, lag_zeros, lag_zeros)


def make_absorb(block_table, local_ids, spectra, cos_low, sine_low):
    prod_real, prod_imag, seg_real, seg_imag = spectra
    last_seg = LAG_BLOCKS

    def absorb(carried, incoming, first_slot):

        def absorb_block(state, member):
            grad_block, offset = member
            lag_index = block_table[offset] - local_ids
            inside_flag = (lag_index >= 0) & (lag_index <= last_seg)

            def update(current):
                grad_real, grad_imag = forward_low(grad_block[None], cos_low, sine_low)
                inside = inside_flag.astype(jnp.float32)[:, None, None]
                chosen = jnp.clip(lag_index, 0, last_seg)
                pick_real = seg_real[chosen]
                pick_imag = seg_imag[chosen]
                du_real, du_imag, lag_real, lag_imag = current
                du_real = du_real + inside * (pick_real * grad_real + pick_imag * grad_imag)
                du_imag = du_imag + inside * (pick_real * grad_imag - pick_imag * grad_real)
                lag_real = lag_real.at[chosen].add(
                    inside * (prod_real * grad_real + prod_imag * grad_imag)
                )
                lag_imag = lag_imag.at[chosen].add(
                    inside * (prod_real * grad_imag - prod_imag * grad_real)
                )
                return (du_real, du_imag, lag_real, lag_imag)

            def unchanged(current):
                return current

            state = lax.cond(jnp.any(inside_flag), update, unchanged, state)
            return (state, None)

        offsets = lax.iota(jnp.int32, incoming.shape[0])
        carried, unused = lax.scan(absorb_block, carried, (incoming, offsets))
        return carried

    return absorb


def on_device(out_grad, query_rows, key_rows, value_rows, conv_rows, long_filter, block_table):
    ranks = lax.axis_size("ctx")
    device = lax.axis_index("ctx")
    channels = out_grad.shape[1]
    factor = (2.0 * BLOCK * ranks) ** (-0.5)
    cos_table, sine_table = dft_tables(2 * BLOCK)
    cos_low = cos_table.astype(jnp.bfloat16)
    sine_low = sine_table.astype(jnp.bfloat16)
    grad_f = out_grad.astype(jnp.float32)
    key_f = key_rows.astype(jnp.float32)
    value_f = value_rows.astype(jnp.float32)
    q_grad = (grad_f * conv_rows.astype(jnp.float32)).astype(jnp.bfloat16)
    weighted = (grad_f * query_rows.astype(jnp.float32)).astype(jnp.bfloat16)
    product = (key_f * value_f).astype(jnp.bfloat16)
    full_filter = lax.all_gather(long_filter, "ctx", axis=0, tiled=True)
    local_ids = lax.dynamic_slice_in_dim(block_table, 2 * device, 2)
    seg_real, seg_imag = filter_segments(full_filter, cos_table, sine_table)
    prod_real, prod_imag = forward_low(product.reshape(2, BLOCK, channels), cos_low, sine_low)
    absorb = make_absorb(
        block_table, local_ids, (prod_real, prod_imag, seg_real, seg_imag), cos_low, sine_low
    )
    carried = absorb(
        empty_state(2, channels),
        lax.all_gather(weighted.reshape(2, BLOCK, channels), "ctx", axis=0, tiled=True),
        jnp.int32(0),
    )
    du_real, du_imag, lag_real, lag_imag = carried
    seq_grad = inverse(du_real, du_imag, cos_table, sine_table, BLOCK).reshape(2 * BLOCK, channels)
    lag_rows = settle_lags(lag_real, lag_imag, cos_table, sine_table, factor)
    own_rows = LAG_BLOCKS * BLOCK // ranks
    summed = lax.psum(lag_rows, "ctx")
    filter_raw = lax.dynamic_slice_in_dim(summed, device * own_rows, own_rows, 0)
    k_grad = (seq_grad * value_f).astype(jnp.bfloat16)
    v_grad = (seq_grad * key_f).astype(jnp.bfloat16)
    return (q_grad, k_grad, v_grad, filter_raw)


def solution(mesh):
    in_specs = (
        P("ctx", "tp"),
        P("ctx", "tp"),
        P("ctx", "tp"),
        P("ctx", "tp"),
        P("ctx", "tp"),
        P("ctx", "tp"),
        P(),
    )
    out_specs = (P("ctx", "tp"), P("ctx", "tp"), P("ctx", "tp"), P("ctx", "tp"))
    return jax.shard_map(
        on_device, mesh=mesh, in_specs=in_specs, out_specs=out_specs, check_vma=False
    )
```

profile of v0, /device:TPU:0, one launch (start us, length us, event | category | flops | bytes accessed | tf_op | source)
XLA Modules:
  0.0 1244.5 jit_solution(18165227531620766185)
XLA Ops:
  31.9 26.2 %all-gather.3.cloned.1.call-done = f32[768,2048]{1,0:T(8,128)} async-done(((f32[96,2048]{1,0:T(8,128)}), f32[768,2048]{1,0:T(8,128)}) %all-gather.3.cloned.1.call-update) | async-done | bytes 6291472 | tf_op jit(solution)/shard_map/all_gather | solution.py:128
  64.7 19.4 %fusion.27 = f32[7,256,2048]{1,2,0:T(8,128)} fusion(f32[6,128,2048]{1,2,0:T(8,128)} %copy.31), kind=kOutput, calls=%fused_computation.50 | convolution fusion | flops 11293556736 | bytes 20971520 | tf_op jit(solution)/shard_map/wt,ntc->nwc/dot_general | solution.py:24
  84.1 16.9 %copy.35 = f32[7,256,2048]{2,1,0:T(8,128)} copy(f32[7,256,2048]{1,2,0:T(8,128)} %fusion.27) | data formatting | bytes 29360128
  101.1 19.7 %negate_bitcast_fusion = f32[7,256,2048]{1,2,0:T(8,128)} fusion(f32[6,128,2048]{1,2,0:T(8,128)} %copy.31), kind=kOutput, calls=%fused_computation.41 | convolution fusion | flops 11297226752 | bytes 20971520 | tf_op jit(solution)/shard_map/wt,ntc->nwc/dot_general | solution.py:25
  120.8 16.9 %copy.36 = f32[7,256,2048]{2,1,0:T(8,128)} copy(f32[7,256,2048]{1,2,0:T(8,128)} %negate_bitcast_fusion) | data formatting | bytes 29360128
  156.7 795.3 %while.17 = (s32[]{:T(128)}, f32[2,256,2048]{2,1,0:T(8,128)}, f32[2,256,2048]{2,1,0:T(8,128)}, f32[7,256,2048]{2,1,0:T(8,128)}, f32[7,256,2048]{2,1,0:T(8,128)},...) while((s32[]{:T(128)}, f32[2,256,2048]{2,1,0:T(8,128)}, ...), condition=%wide.region_6.7_spmd.clone, body=%wide.region_0.6_spmd.clone.sunk | while | flops 290980896 | bytes 102110704 | solution.py:108
  162.9 58.0 %conditional.3 = ((f32[2,256,2048]{2,1,0:T(8,128)}, f32[2,256,2048]{2,1,0:T(8,128)}, f32[7,256,2048]{2,1,0:T(8,128)}, f32[7,256,2048]{2,1,0:T(8,128)})) conditional(s32[]{:T(128)} %convert_element_type.164, (f32[2,256,2048]{2,1,0:T(8,128)}, f32[2,256,2048]{2,1,0:T(8,128)}, f32[7,256,2048]{2,1,0:T(8,128)}, f32[7,256,2048]{2,1,0:T(8,128)}) %tuple.53, ...), branch_computations={%region_2.2_spmd, %region_3.5_spmd} | conditional | flops 289932288 | bytes 101848176 | solution.py:104
  162.9 8.0 gather_fusion
  189.4 15.3 %subtract_multiply_fusion = (f32[2,256,2048]{2,1,0:T(8,128)}, f32[2,256,2048]{2,1,0:T(8,128)}, f32[2,256,2048]{2,1,0:T(8,128)}, f32[2,256,2048]{2,1,0:T(8,128)}) fusion(f32[2,256,2048]{2,1,0:T(8,128)} %get-tuple-element.139, f32[2,256,2048]{2,1,0:T(8,128)} %get-tuple-element.138, f32[256,2048]{1,0:T(8,128)} %copy.30, f32[256,2048]{1,0:T(8,128)S(1)} %copy.29, ...), kind=kLoop, calls=%fused_computation.6 | loop fusion | flops 18874368 | bytes 46137352 | tf_op jit(solution)/shard_map/while/body/eval_jaxpr/cond/branch_1_fun/mul | solution.py:97
  204.7 8.0 scatter_fusion.1
  212.8 8.1 scatter_fusion
  227.1 58.1 %conditional.3 = ((f32[2,256,2048]{2,1,0:T(8,128)}, f32[2,256,2048]{2,1,0:T(8,128)}, f32[7,256,2048]{2,1,0:T(8,128)}, f32[7,256,2048]{2,1,0:T(8,128)})) conditional(s32[]{:T(128)} %convert_element_type.164, (f32[2,256,2048]{2,1,0:T(8,128)}, f32[2,256,2048]{2,1,0:T(8,128)}, f32[7,256,2048]{2,1,0:T(8,128)}, f32[7,256,2048]{2,1,0:T(8,128)}) %tuple.53, ...), branch_computations={%region_2.2_spmd, %region_3.5_spmd} | conditional | flops 289932288 | bytes 101848176 | solution.py:104
  253.6 15.3 %subtract_multiply_fusion = (f32[2,256,2048]{2,1,0:T(8,128)}, f32[2,256,2048]{2,1,0:T(8,128)}, f32[2,256,2048]{2,1,0:T(8,128)}, f32[2,256,2048]{2,1,0:T(8,128)}) fusion(f32[2,256,2048]{2,1,0:T(8,128)} %get-tuple-element.139, f32[2,256,2048]{2,1,0:T(8,128)} %get-tuple-element.138, f32[256,2048]{1,0:T(8,128)} %copy.30, f32[256,2048]{1,0:T(8,128)S(1)} %copy.29, ...), kind=kLoop, calls=%fused_computation.6 | loop fusion | flops 18874368 | bytes 46137352 | tf_op jit(solution)/shard_map/while/body/eval_jaxpr/cond/branch_1_fun/mul | solution.py:97
  268.9 8.1 scatter_fusion.1
  277.0 8.1 scatter_fusion
  291.3 58.0 %conditional.3 = ((f32[2,256,2048]{2,1,0:T(8,128)}, f32[2,256,2048]{2,1,0:T(8,128)}, f32[7,256,2048]{2,1,0:T(8,128)}, f32[7,256,2048]{2,1,0:T(8,128)})) conditional(s32[]{:T(128)} %convert_element_type.164, (f32[2,256,2048]{2,1,0:T(8,128)}, f32[2,256,2048]{2,1,0:T(8,128)}, f32[7,256,2048]{2,1,0:T(8,128)}, f32[7,256,2048]{2,1,0:T(8,128)}) %tuple.53, ...), branch_computations={%region_2.2_spmd, %region_3.5_spmd} | conditional | flops 289932288 | bytes 101848176 | solution.py:104
  291.3 8.0 gather_fusion
  317.9 15.3 %subtract_multiply_fusion = (f32[2,256,2048]{2,1,0:T(8,128)}, f32[2,256,2048]{2,1,0:T(8,128)}, f32[2,256,2048]{2,1,0:T(8,128)}, f32[2,256,2048]{2,1,0:T(8,128)}) fusion(f32[2,256,2048]{2,1,0:T(8,128)} %get-tuple-element.139, f32[2,256,2048]{2,1,0:T(8,128)} %get-tuple-element.138, f32[256,2048]{1,0:T(8,128)} %copy.30, f32[256,2048]{1,0:T(8,128)S(1)} %copy.29, ...), kind=kLoop, calls=%fused_computation.6 | loop fusion | flops 18874368 | bytes 46137352 | tf_op jit(solution)/shard_map/while/body/eval_jaxpr/cond/branch_1_fun/mul | solution.py:97
  333.2 8.0 scatter_fusion.1
  341.2 8.1 scatter_fusion
  355.5 58.0 %conditional.3 = ((f32[2,256,2048]{2,1,0:T(8,128)}, f32[2,256,2048]{2,1,0:T(8,128)}, f32[7,256,2048]{2,1,0:T(8,128)}, f32[7,256,2048]{2,1,0:T(8,128)})) conditional(s32[]{:T(128)} %convert_element_type.164, (f32[2,256,2048]{2,1,0:T(8,128)}, f32[2,256,2048]{2,1,0:T(8,128)}, f32[7,256,2048]{2,1,0:T(8,128)}, f32[7,256,2048]{2,1,0:T(8,128)}) %tuple.53, ...), branch_computations={%region_2.2_spmd, %region_3.5_spmd} | conditional | flops 289932288 | bytes 101848176 | solution.py:104
  355.5 8.0 gather_fusion
  382.0 15.3 %subtract_multiply_fusion = (f32[2,256,2048]{2,1,0:T(8,128)}, f32[2,256,2048]{2,1,0:T(8,128)}, f32[2,256,2048]{2,1,0:T(8,128)}, f32[2,256,2048]{2,1,0:T(8,128)}) fusion(f32[2,256,2048]{2,1,0:T(8,128)} %get-tuple-element.139, f32[2,256,2048]{2,1,0:T(8,128)} %get-tuple-element.138, f32[256,2048]{1,0:T(8,128)} %copy.30, f32[256,2048]{1,0:T(8,128)S(1)} %copy.29, ...), kind=kLoop, calls=%fused_computation.6 | loop fusion | flops 18874368 | bytes 46137352 | tf_op jit(solution)/shard_map/while/body/eval_jaxpr/cond/branch_1_fun/mul | solution.py:97
  397.4 8.0 scatter_fusion.1
  405.4 8.1 scatter_fusion
  425.9 58.0 %conditional.3 = ((f32[2,256,2048]{2,1,0:T(8,128)}, f32[2,256,2048]{2,1,0:T(8,128)}, f32[7,256,2048]{2,1,0:T(8,128)}, f32[7,256,2048]{2,1,0:T(8,128)})) conditional(s32[]{:T(128)} %convert_element_type.164, (f32[2,256,2048]{2,1,0:T(8,128)}, f32[2,256,2048]{2,1,0:T(8,128)}, f32[7,256,2048]{2,1,0:T(8,128)}, f32[7,256,2048]{2,1,0:T(8,128)}) %tuple.53, ...), branch_computations={%region_2.2_spmd, %region_3.5_spmd} | conditional | flops 289932288 | bytes 101848176 | solution.py:104
  452.4 15.3 %subtract_multiply_fusion = (f32[2,256,2048]{2,1,0:T(8,128)}, f32[2,256,2048]{2,1,0:T(8,128)}, f32[2,256,2048]{2,1,0:T(8,128)}, f32[2,256,2048]{2,1,0:T(8,128)}) fusion(f32[2,256,2048]{2,1,0:T(8,128)} %get-tuple-element.139, f32[2,256,2048]{2,1,0:T(8,128)} %get-tuple-element.138, f32[256,2048]{1,0:T(8,128)} %copy.30, f32[256,2048]{1,0:T(8,128)S(1)} %copy.29, ...), kind=kLoop, calls=%fused_computation.6 | loop fusion | flops 18874368 | bytes 46137352 | tf_op jit(solution)/shard_map/while/body/eval_jaxpr/cond/branch_1_fun/mul | solution.py:97
  467.7 8.1 scatter_fusion.1
  475.8 8.1 scatter_fusion
  490.1 58.0 %conditional.3 = ((f32[2,256,2048]{2,1,0:T(8,128)}, f32[2,256,2048]{2,1,0:T(8,128)}, f32[7,256,2048]{2,1,0:T(8,128)}, f32[7,256,2048]{2,1,0:T(8,128)})) conditional(s32[]{:T(128)} %convert_element_type.164, (f32[2,256,2048]{2,1,0:T(8,128)}, f32[2,256,2048]{2,1,0:T(8,128)}, f32[7,256,2048]{2,1,0:T(8,128)}, f32[7,256,2048]{2,1,0:T(8,128)}) %tuple.53, ...), branch_computations={%region_2.2_spmd, %region_3.5_spmd} | conditional | flops 289932288 | bytes 101848176 | solution.py:104
  516.6 15.3 %subtract_multiply_fusion = (f32[2,256,2048]{2,1,0:T(8,128)}, f32[2,256,2048]{2,1,0:T(8,128)}, f32[2,256,2048]{2,1,0:T(8,128)}, f32[2,256,2048]{2,1,0:T(8,128)}) fusion(f32[2,256,2048]{2,1,0:T(8,128)} %get-tuple-element.139, f32[2,256,2048]{2,1,0:T(8,128)} %get-tuple-element.138, f32[256,2048]{1,0:T(8,128)} %copy.30, f32[256,2048]{1,0:T(8,128)S(1)} %copy.29, ...), kind=kLoop, calls=%fused_computation.6 | loop fusion | flops 18874368 | bytes 46137352 | tf_op jit(solution)/shard_map/while/body/eval_jaxpr/cond/branch_1_fun/mul | solution.py:97
  531.9 8.1 scatter_fusion.1
  540.0 8.1 scatter_fusion
  554.3 58.1 %conditional.3 = ((f32[2,256,2048]{2,1,0:T(8,128)}, f32[2,256,2048]{2,1,0:T(8,128)}, f32[7,256,2048]{2,1,0:T(8,128)}, f32[7,256,2048]{2,1,0:T(8,128)})) conditional(s32[]{:T(128)} %convert_element_type.164, (f32[2,256,2048]{2,1,0:T(8,128)}, f32[2,256,2048]{2,1,0:T(8,128)}, f32[7,256,2048]{2,1,0:T(8,128)}, f32[7,256,2048]{2,1,0:T(8,128)}) %tuple.53, ...), branch_computations={%region_2.2_spmd, %region_3.5_spmd} | conditional | flops 289932288 | bytes 101848176 | solution.py:104
  554.3 8.0 gather_fusion
  580.8 15.3 %subtract_multiply_fusion = (f32[2,256,2048]{2,1,0:T(8,128)}, f32[2,256,2048]{2,1,0:T(8,128)}, f32[2,256,2048]{2,1,0:T(8,128)}, f32[2,256,2048]{2,1,0:T(8,128)}) fusion(f32[2,256,2048]{2,1,0:T(8,128)} %get-tuple-element.139, f32[2,256,2048]{2,1,0:T(8,128)} %get-tuple-element.138, f32[256,2048]{1,0:T(8,128)} %copy.30, f32[256,2048]{1,0:T(8,128)S(1)} %copy.29, ...), kind=kLoop, calls=%fused_computation.6 | loop fusion | flops 18874368 | bytes 46137352 | tf_op jit(solution)/shard_map/while/body/eval_jaxpr/cond/branch_1_fun/mul | solution.py:97
  596.1 8.1 scatter_fusion.1
  604.2 8.2 scatter_fusion
  624.7 58.0 %conditional.3 = ((f32[2,256,2048]{2,1,0:T(8,128)}, f32[2,256,2048]{2,1,0:T(8,128)}, f32[7,256,2048]{2,1,0:T(8,128)}, f32[7,256,2048]{2,1,0:T(8,128)})) conditional(s32[]{:T(128)} %convert_element_type.164, (f32[2,256,2048]{2,1,0:T(8,128)}, f32[2,256,2048]{2,1,0:T(8,128)}, f32[7,256,2048]{2,1,0:T(8,128)}, f32[7,256,2048]{2,1,0:T(8,128)}) %tuple.53, ...), branch_computations={%region_2.2_spmd, %region_3.5_spmd} | conditional | flops 289932288 | bytes 101848176 | solution.py:104
  651.3 15.3 %subtract_multiply_fusion = (f32[2,256,2048]{2,1,0:T(8,128)}, f32[2,256,2048]{2,1,0:T(8,128)}, f32[2,256,2048]{2,1,0:T(8,128)}, f32[2,256,2048]{2,1,0:T(8,128)}) fusion(f32[2,256,2048]{2,1,0:T(8,128)} %get-tuple-element.139, f32[2,256,2048]{2,1,0:T(8,128)} %get-tuple-element.138, f32[256,2048]{1,0:T(8,128)} %copy.30, f32[256,2048]{1,0:T(8,128)S(1)} %copy.29, ...), kind=kLoop, calls=%fused_computation.6 | loop fusion | flops 18874368 | bytes 46137352 | tf_op jit(solution)/shard_map/while/body/eval_jaxpr/cond/branch_1_fun/mul | solution.py:97
  666.6 8.1 scatter_fusion.1
  674.7 8.1 scatter_fusion
  688.9 58.0 %conditional.3 = ((f32[2,256,2048]{2,1,0:T(8,128)}, f32[2,256,2048]{2,1,0:T(8,128)}, f32[7,256,2048]{2,1,0:T(8,128)}, f32[7,256,2048]{2,1,0:T(8,128)})) conditional(s32[]{:T(128)} %convert_element_type.164, (f32[2,256,2048]{2,1,0:T(8,128)}, f32[2,256,2048]{2,1,0:T(8,128)}, f32[7,256,2048]{2,1,0:T(8,128)}, f32[7,256,2048]{2,1,0:T(8,128)}) %tuple.53, ...), branch_computations={%region_2.2_spmd, %region_3.5_spmd} | conditional | flops 289932288 | bytes 101848176 | solution.py:104
  688.9 8.0 gather_fusion
  715.4 15.3 %subtract_multiply_fusion = (f32[2,256,2048]{2,1,0:T(8,128)}, f32[2,256,2048]{2,1,0:T(8,128)}, f32[2,256,2048]{2,1,0:T(8,128)}, f32[2,256,2048]{2,1,0:T(8,128)}) fusion(f32[2,256,2048]{2,1,0:T(8,128)} %get-tuple-element.139, f32[2,256,2048]{2,1,0:T(8,128)} %get-tuple-element.138, f32[256,2048]{1,0:T(8,128)} %copy.30, f32[256,2048]{1,0:T(8,128)S(1)} %copy.29, ...), kind=kLoop, calls=%fused_computation.6 | loop fusion | flops 18874368 | bytes 46137352 | tf_op jit(solution)/shard_map/while/body/eval_jaxpr/cond/branch_1_fun/mul | solution.py:97
  730.8 8.0 scatter_fusion.1
  738.8 8.1 scatter_fusion
  753.0 58.1 %conditional.3 = ((f32[2,256,2048]{2,1,0:T(8,128)}, f32[2,256,2048]{2,1,0:T(8,128)}, f32[7,256,2048]{2,1,0:T(8,128)}, f32[7,256,2048]{2,1,0:T(8,128)})) conditional(s32[]{:T(128)} %convert_element_type.164, (f32[2,256,2048]{2,1,0:T(8,128)}, f32[2,256,2048]{2,1,0:T(8,128)}, f32[7,256,2048]{2,1,0:T(8,128)}, f32[7,256,2048]{2,1,0:T(8,128)}) %tuple.53, ...), branch_computations={%region_2.2_spmd, %region_3.5_spmd} | conditional | flops 289932288 | bytes 101848176 | solution.py:104
  753.1 8.0 gather_fusion
  779.6 15.3 %subtract_multiply_fusion = (f32[2,256,2048]{2,1,0:T(8,128)}, f32[2,256,2048]{2,1,0:T(8,128)}, f32[2,256,2048]{2,1,0:T(8,128)}, f32[2,256,2048]{2,1,0:T(8,128)}) fusion(f32[2,256,2048]{2,1,0:T(8,128)} %get-tuple-element.139, f32[2,256,2048]{2,1,0:T(8,128)} %get-tuple-element.138, f32[256,2048]{1,0:T(8,128)} %copy.30, f32[256,2048]{1,0:T(8,128)S(1)} %copy.29, ...), kind=kLoop, calls=%fused_computation.6 | loop fusion | flops 18874368 | bytes 46137352 | tf_op jit(solution)/shard_map/while/body/eval_jaxpr/cond/branch_1_fun/mul | solution.py:97
  794.9 8.1 scatter_fusion.1
  803.0 8.1 scatter_fusion
  817.3 58.1 %conditional.3 = ((f32[2,256,2048]{2,1,0:T(8,128)}, f32[2,256,2048]{2,1,0:T(8,128)}, f32[7,256,2048]{2,1,0:T(8,128)}, f32[7,256,2048]{2,1,0:T(8,128)})) conditional(s32[]{:T(128)} %convert_element_type.164, (f32[2,256,2048]{2,1,0:T(8,128)}, f32[2,256,2048]{2,1,0:T(8,128)}, f32[7,256,2048]{2,1,0:T(8,128)}, f32[7,256,2048]{2,1,0:T(8,128)}) %tuple.53, ...), branch_computations={%region_2.2_spmd, %region_3.5_spmd} | conditional | flops 289932288 | bytes 101848176 | solution.py:104
  843.8 15.3 %subtract_multiply_fusion = (f32[2,256,2048]{2,1,0:T(8,128)}, f32[2,256,2048]{2,1,0:T(8,128)}, f32[2,256,2048]{2,1,0:T(8,128)}, f32[2,256,2048]{2,1,0:T(8,128)}) fusion(f32[2,256,2048]{2,1,0:T(8,128)} %get-tuple-element.139, f32[2,256,2048]{2,1,0:T(8,128)} %get-tuple-element.138, f32[256,2048]{1,0:T(8,128)} %copy.30, f32[256,2048]{1,0:T(8,128)S(1)} %copy.29, ...), kind=kLoop, calls=%fused_computation.6 | loop fusion | flops 18874368 | bytes 46137352 | tf_op jit(solution)/shard_map/while/body/eval_jaxpr/cond/branch_1_fun/mul | solution.py:97
  859.1 8.1 scatter_fusion.1
  867.2 8.1 scatter_fusion
  887.7 58.1 %conditional.3 = ((f32[2,256,2048]{2,1,0:T(8,128)}, f32[2,256,2048]{2,1,0:T(8,128)}, f32[7,256,2048]{2,1,0:T(8,128)}, f32[7,256,2048]{2,1,0:T(8,128)})) conditional(s32[]{:T(128)} %convert_element_type.164, (f32[2,256,2048]{2,1,0:T(8,128)}, f32[2,256,2048]{2,1,0:T(8,128)}, f32[7,256,2048]{2,1,0:T(8,128)}, f32[7,256,2048]{2,1,0:T(8,128)}) %tuple.53, ...), branch_computations={%region_2.2_spmd, %region_3.5_spmd} | conditional | flops 289932288 | bytes 101848176 | solution.py:104
  914.3 15.3 %subtract_multiply_fusion = (f32[2,256,2048]{2,1,0:T(8,128)}, f32[2,256,2048]{2,1,0:T(8,128)}, f32[2,256,2048]{2,1,0:T(8,128)}, f32[2,256,2048]{2,1,0:T(8,128)}) fusion(f32[2,256,2048]{2,1,0:T(8,128)} %get-tuple-element.139, f32[2,256,2048]{2,1,0:T(8,128)} %get-tuple-element.138, f32[256,2048]{1,0:T(8,128)} %copy.30, f32[256,2048]{1,0:T(8,128)S(1)} %copy.29, ...), kind=kLoop, calls=%fused_computation.6 | loop fusion | flops 18874368 | bytes 46137352 | tf_op jit(solution)/shard_map/while/body/eval_jaxpr/cond/branch_1_fun/mul | solution.py:97
  929.6 8.1 scatter_fusion.1
  937.7 8.1 scatter_fusion
  952.0 28.3 %fusion.39 = f32[7,2048,256]{1,2,0:T(8,128)} fusion(f32[7,256,2048]{2,1,0:T(8,128)} %get-tuple-element.171), kind=kOutput, calls=%fused_computation.73 | convolution fusion | flops 11275206656 | bytes 29360128 | tf_op jit(solution)/shard_map/tw,nwc->ntc/dot_general | solution.py:42
  980.3 25.6 %multiply_bitcast_fusion = f32[7,256,2048]{2,1,0:T(8,128)} fusion(f32[7,2048,256]{1,2,0:T(8,128)} %fusion.39, f32[7,256,2048]{2,1,0:T(8,128)} %get-tuple-element.172), kind=kOutput, calls=%fused_computation.40 | convolution fusion | flops 11282546688 | bytes 44040192 | tf_op jit(solution)/shard_map/tw,nwc->ntc/dot_general | solution.py:45
  1006.0 9.2 fusion.26
  1025.9 209.9 %all-reduce.4.cloned.1.call-done = f32[768,2048]{1,0:T(8,128)} async-done(((f32[768,2048]{1,0:T(8,128)}), f32[768,2048]{1,0:T(8,128)}) %all-reduce.4.cloned.1.call-update) | async-done | bytes 6291472 | tf_op jit(solution)/shard_map/psum | solution.py:144
  (232 shorter events, 390.1 us)
Async XLA Ops:
  7.2 5.8 copy-start.1
  7.2 5.8 copy-start.3
  7.2 51.0 %all-gather.3.cloned.1.call-start = ((), (), s32[]{:S(2)}) async-start(), calls=%async_computation | async-start | bytes 7077888 | tf_op jit(solution)/shard_map/all_gather | solution.py:128
  7.9 129.7 %all-gather.5.cloned.1.call-start = ((), (), s32[]{:S(2)}) async-start(), calls=%async_computation.1 | async-start | bytes 9437184 | tf_op jit(solution)/shard_map/all_gather | solution.py:137
  11.9 1223.8 %all-reduce.4.cloned.1.call-start = ((), (), s32[]{:S(2)}) async-start(), calls=%async_computation.2 | async-start | bytes 12582912 | tf_op jit(solution)/shard_map/psum | solution.py:144
  12.9 0.7 copy-start.7
  22.9 0.7 copy-start.5
  26.4 5.4 copy-start.9
  1015.2 0.9 copy-start.8
  1015.2 6.0 copy-start.6
  1015.2 6.0 copy-start
  1021.2 2.7 copy-start.2
  1021.3 2.7 copy-start.4
Sparse Core Ops, SparseCore 0:
  9.9 48.2 all-gather.2
  60.6 54.3 all-gather.4
  1015.3 220.3 all-reduce.3
where the time goes:
time: 1260 us; the launch traced here: 1240 us
  other arithmetic  433 us (34%)
  local copies, waits for them, and re-layouts  342 us (27%)
  waiting for transfers between devices  237 us (19%)
  matrix products  175 us (14%)
  loops' own time  42.5 us (3%)
  between operations  14.2 us (1%)
    psum x1, waiting for transfers between devices, on_device(): summed = lax.psum(lag_rows, 'ctx')  210 us
    mul x12, other arithmetic, update(): inside * (prod_real * grad_imag - prod_imag * grad_real)  184 us
    scatter-add x12, other arithmetic, update(): lag_real.at[chosen]  97.3 us
    scatter-add x12, other arithmetic, update(): lag_imag.at[chosen]  96.9 us
    gather x12, local copies, waits for them, and re-layouts, update(): pick_real = seg_real[chosen]  95.8 us
    gather x12, local copies, waits for them, and re-layouts, update(): pick_imag = seg_imag[chosen]  95.4 us
    mul x24, local copies, waits for them, and re-layouts, update(): du_real = du_real + inside * (pick_real * grad_real + pick_imag * grad_imag)  58 us
    unnamed x24, local copies, waits for them, and re-layouts  46.7 us
  transfers between devices with their start and end apart: 3, of which 2 were waited for; matrix products, arithmetic and copies ran while one was open for 9% of the time, Pallas kernels for 0%

commit v1 on v0

v1 whole, which is shorter than its diff:
```python
import functools
import math

import jax
import jax.numpy as jnp
import ml_dtypes
import numpy as np
from jax import lax
from jax.experimental import pallas as pl
from jax.experimental.pallas import tpu as pltpu
from jax.sharding import PartitionSpec as P

BLOCK = 128
LAG_BLOCKS = 6
SPAN = 2 * BLOCK
LAG_SPANS = LAG_BLOCKS * BLOCK // SPAN
LANES = 128
VMEM_BYTES = 32 * 2**20


def step_orders(ranks):
    if ranks != 8:
        return [list(range(ranks))] * 3
    return [4, 1, 2, 6, 7, 5, 3, 0], [7, 5, 3, 1, 4, 2, 6, 0], [4, 2, 5, 3, 1, 6, 7, 0]


def early_steps(ranks):
    return [6, 7] if ranks == 8 else []


def starts_after(ranks):
    return {4: 8 + 6, 2: 8 + 7, 6: 4, 7: 2} if ranks == 8 else {}


def transform_tables():
    order = np.concatenate([np.arange(0, SPAN, 2), np.arange(1, SPAN, 2)])
    angles = np.outer(order + 0.5, np.arange(SPAN)) * (math.pi / SPAN)
    forward = np.concatenate([np.cos(angles), -np.sin(angles)], 0)
    inverse = forward.T / SPAN
    return forward.astype(ml_dtypes.bfloat16), inverse.astype(ml_dtypes.bfloat16)


def swapped(device, step):
    return jnp.bitwise_xor(device, step)


def prepare_kernel(*refs, ranks, count, after):
    sources, refs = refs[:count], refs[count + after :]
    targets, rest = refs[:ranks], refs[ranks:]
    slabs, in_sems = rest[:count], rest[count]
    rows, half = slabs[0].shape[1:]
    width = 2 * half // ranks
    device = lax.axis_index("ctx")
    upper = lax.shift_right_logical(device, int(math.log2(ranks)) - 1)
    loads = []
    for group in range(2):
        columns = pl.ds(pl.multiple_of(swapped(upper, group) * half, LANES), half)
        loads.append(
            [
                pltpu.make_async_copy(source.at[:, columns], slab.at[group], in_sems.at[group, at])
                for at, (source, slab) in enumerate(zip(sources, slabs))
            ]
        )
        for load in loads[group]:
            load.start()
    for step in range(ranks):
        group, inner = divmod(step, ranks // 2)
        if inner == 0:
            for load in loads[group]:
                load.wait()
        column = jnp.bitwise_and(swapped(device, inner), ranks // 2 - 1) * width
        columns = pl.ds(pl.multiple_of(column, LANES), width)
        targets[step][:rows] = slabs[0][group, :, columns] * slabs[1][group, :, columns]
        if count == 3:
            targets[step][rows:] = slabs[2][group, :, columns].astype(jnp.bfloat16)


def prepare(arrays, ranks, after=()):
    rows, channels = arrays[0].shape
    width = channels // ranks
    out_rows = rows + sum(a.shape[0] for a in arrays[2:])
    if width % LANES:
        left, right, *below = [a.astype(jnp.float32) for a in arrays]
        packed = jnp.concatenate([left * right, *below], 0).astype(jnp.bfloat16)
        packed = packed.reshape(out_rows, ranks, width).transpose(1, 0, 2)
        device = lax.axis_index("ctx")
        return [lax.dynamic_index_in_dim(packed, device ^ m, 0, False) for m in range(ranks)]
    half = channels // 2
    slabs = [pltpu.VMEM((2, a.shape[0], half), a.dtype) for a in arrays]
    return pl.pallas_call(
        functools.partial(prepare_kernel, ranks=ranks, count=len(arrays), after=len(after)),
        in_specs=[pl.BlockSpec(memory_space=pltpu.HBM)] * len(arrays)
        + [pl.BlockSpec(memory_space=pl.ANY)] * len(after),
        out_specs=[pl.BlockSpec(memory_space=pltpu.VMEM)] * ranks,
        out_shape=[jax.ShapeDtypeStruct((out_rows, width), jnp.bfloat16)] * ranks,
        scratch_shapes=slabs + [pltpu.SemaphoreType.DMA((2, len(arrays)))],
        compiler_params=pltpu.CompilerParams(vmem_limit_bytes=VMEM_BYTES),
        cost_estimate=pl.CostEstimate(
            flops=rows * channels, bytes_accessed=8 * out_rows * channels, transcendentals=0
        ),
    )(*(pltpu.with_memory_space_constraint(a, pltpu.HBM) for a in arrays), *after)


class Spans:
    def __init__(self, table_ref, slot_ref, ranks):
        self.slot_ref = slot_ref
        for slot in range(2 * ranks):
            slot_ref[table_ref[slot]] = slot

    def place(self, block):
        slot = self.slot_ref[block]
        start = pl.multiple_of(jnp.bitwise_and(slot, 1) * BLOCK, BLOCK)
        return lax.shift_right_logical(slot, 1), start

    def read(self, ref, span):
        halves = []
        for block in (2 * span, 2 * span + 1):
            source, start = self.place(block)
            halves.append(ref[source, pl.ds(start, BLOCK), :])
        return jnp.concatenate(halves, 0)

    def write(self, ref, span, values):
        for half in range(2):
            source, start = self.place(2 * span + half)
            ref[source, pl.ds(start, BLOCK), :] = values[half * BLOCK : (half + 1) * BLOCK]


def gather_pieces(pieces, recv_ref, message):
    device = lax.axis_index("ctx")
    for step, piece in zip(step_orders(len(pieces))[message], pieces):
        recv_ref[swapped(device, step)] = piece[...]


def added(total, left, right):
    term_real = left[0] * right[0] + left[1] * right[1]
    term_imag = left[0] * right[1] - left[1] * right[0]
    return (term_real, term_imag) if total is None else (total[0] + term_real, total[1] + term_imag)


def settle(ref, index, place, sign, here, beyond):
    if beyond is not None:
        if sign > 0:
            here = here[0] + beyond[1], here[1] - beyond[0]
        else:
            here = here[0] - beyond[1], here[1] + beyond[0]
    store(ref, index, place, here)


def load(ref, index, place):
    real, imag, lanes = place
    return ref[index, real, lanes], ref[index, imag, lanes]


def store(ref, index, place, values):
    real, imag, lanes = place
    ref[index, real, lanes], ref[index, imag, lanes] = values


def each_place(width, combine):
    lane_size = LANES if width % LANES == 0 else width
    for sign in (1, -1):

        def step(index, carry, sign=sign):
            row = index * 8 if sign > 0 else index * 8 + SPAN // 2
            real = pl.ds(pl.multiple_of(row, 8), 8)
            imag = pl.ds(pl.multiple_of(row + SPAN, 8), 8)
            for lane in range(0, width, lane_size):
                combine((real, imag, slice(lane, lane + lane_size)), sign)
            return carry

        lax.fori_loop(0, SPAN // 16, step, 0)


def invert(inverse, spectrum):
    return jnp.dot(inverse, spectrum.astype(jnp.bfloat16), preferred_element_type=jnp.float32)


def weighted_kernel(table_ref, forward_ref, inverse_ref, *refs):
    slot_ref, recv_ref, f_ref, s_ref = refs[-4:]
    ranks, _, width = recv_ref.shape
    pieces, (seq_ref, w_ref, *early_refs) = refs[:ranks], refs[ranks:-4]
    spans = Spans(table_ref, slot_ref, ranks)
    gather_pieces(pieces, recv_ref, 0)
    forward = forward_ref[...]
    taps = jnp.concatenate([recv_ref[source, SPAN:, :] for source in range(ranks)], 0)
    for lag in range(LAG_SPANS):
        rows = taps[lag * SPAN : (lag + 1) * SPAN]
        f_ref[lag] = jnp.dot(forward, rows, preferred_element_type=jnp.float32)
    for span in range(ranks):
        w_ref[span] = jnp.dot(forward, spans.read(recv_ref, span), preferred_element_type=jnp.float32)

    def combine(place, sign):
        filters = [load(f_ref, lag, place) for lag in range(LAG_SPANS)]
        sums = [None] * (ranks + 1)
        for span in range(ranks):
            weighted = load(w_ref, span, place)
            for lag in range(min(LAG_SPANS - 1, span) + 1):
                sums[span - lag] = added(sums[span - lag], filters[lag], weighted)
            done = span - LAG_SPANS
            if done >= 0:
                settle(s_ref, done, place, sign, sums[done], sums[done + 1])
        for span in range(max(0, ranks - LAG_SPANS), ranks):
            settle(s_ref, span, place, sign, sums[span], sums[span + 1])

    each_place(width, combine)
    inverse = inverse_ref[...]
    for span in range(ranks):
        spans.write(seq_ref, span, invert(inverse, s_ref[span]).astype(jnp.bfloat16))
    device = lax.axis_index("ctx")
    for step, early_ref in zip(early_steps(ranks), early_refs):
        early_ref[...] = seq_ref[swapped(device, step)]


def product_kernel(table_ref, forward_ref, inverse_ref, w_ref, seq_ref, *refs):
    slot_ref, recv_ref, u_ref, g_ref = refs[-4:]
    ranks, _, width = recv_ref.shape
    pieces, targets = refs[:ranks], refs[ranks:-4]
    factor = (2.0 * BLOCK * ranks) ** -0.5
    spans = Spans(table_ref, slot_ref, ranks)
    gather_pieces(pieces, recv_ref, 1)
    forward = forward_ref[...]
    for span in range(ranks):
        u_ref[span] = jnp.dot(forward, spans.read(recv_ref, span), preferred_element_type=jnp.float32)

    def combine(place, sign):
        lagged = [None] * (LAG_SPANS + 1)
        products = []
        for span in range(ranks):
            weighted = load(w_ref, span, place)
            products.append(load(u_ref, span, place))
            for lag in range(min(LAG_SPANS, span) + 1):
                lagged[lag] = added(lagged[lag], products[span - lag], weighted)
        for lag in range(LAG_SPANS):
            settle(g_ref, lag, place, sign, lagged[lag], lagged[lag + 1])

    each_place(width, combine)
    inverse = inverse_ref[...]
    lags = [(invert(inverse, g_ref[lag]) * factor).astype(jnp.bfloat16) for lag in range(LAG_SPANS)]
    lag_rows = jnp.concatenate(lags, 0)
    taps = lag_rows.shape[0] // ranks
    device = lax.axis_index("ctx")
    for source in range(ranks):
        recv_ref[source, :taps] = lag_rows[source * taps : (source + 1) * taps]
    for step, target in enumerate(targets):
        owner = swapped(device, step)
        if step not in early_steps(ranks):
            target[:SPAN] = seq_ref[owner]
        target[-taps:] = recv_ref[owner, :taps]


def spectral_call(kernel, operands, out_shape, scratch, flops, ranks):
    whole = pl.BlockSpec(memory_space=pltpu.VMEM)
    return pl.pallas_call(
        kernel,
        in_specs=[pl.BlockSpec(memory_space=pltpu.SMEM)] + [whole] * (len(operands) - 1),
        out_specs=[whole] * len(out_shape),
        out_shape=out_shape,
        scratch_shapes=[pltpu.SMEM((2 * ranks,), jnp.int32)] + scratch,
        compiler_params=pltpu.CompilerParams(vmem_limit_bytes=VMEM_BYTES),
        cost_estimate=pl.CostEstimate(
            flops=flops,
            bytes_accessed=sum(a.size * a.dtype.itemsize for a in (*operands, *out_shape)),
            transcendentals=0,
        ),
    )(*operands)


def weighted_part(received, constants):
    ranks = len(received)
    recv_rows, width = received[0].shape
    return spectral_call(
        weighted_kernel,
        (*constants, *received),
        [
            jax.ShapeDtypeStruct((ranks, SPAN, width), jnp.bfloat16),
            jax.ShapeDtypeStruct((ranks, 2 * SPAN, width), jnp.float32),
        ]
        + [jax.ShapeDtypeStruct((SPAN, width), jnp.bfloat16)] * len(early_steps(ranks)),
        [
            pltpu.VMEM((ranks, recv_rows, width), jnp.bfloat16),
            pltpu.VMEM((LAG_SPANS, 2 * SPAN, width), jnp.float32),
            pltpu.VMEM((ranks, 2 * SPAN, width), jnp.float32),
        ],
        4 * SPAN * SPAN * width * (2 * ranks + LAG_SPANS),
        ranks,
    )


def product_part(received, seq_grad, spectrum, constants):
    ranks = len(received)
    width = received[0].shape[1]
    taps = LAG_SPANS * SPAN // ranks
    early = early_steps(ranks)
    return spectral_call(
        product_kernel,
        (*constants, spectrum, seq_grad, *received),
        [
            jax.ShapeDtypeStruct((taps if step in early else SPAN + taps, width), jnp.bfloat16)
            for step in range(ranks)
        ],
        [
            pltpu.VMEM((ranks, SPAN, width), jnp.bfloat16),
            pltpu.VMEM((ranks, 2 * SPAN, width), jnp.float32),
            pltpu.VMEM((LAG_SPANS, 2 * SPAN, width), jnp.float32),
        ],
        4 * SPAN * SPAN * width * (ranks + LAG_SPANS),
        ranks,
    )


def finish_kernel(*refs, ranks, early):
    received, early_refs, refs = refs[:ranks], refs[ranks : ranks + early], refs[ranks + early :]
    key_ref, value_ref, k_ref, v_ref, filter_ref, k_slab, v_slab, lag_slab, sems = refs
    _, rows, width = k_slab.shape
    taps = lag_slab.shape[1]
    seq_refs = dict(zip(step_orders(ranks)[2], received)) | dict(zip(early_steps(ranks), early_refs))
    lag_refs = dict(zip(step_orders(ranks)[2], received))
    device = lax.axis_index("ctx")
    stores = []
    for step in range(ranks):
        columns = pl.ds(pl.multiple_of(swapped(device, step) * width, LANES), width)
        seq_grad = seq_refs[step][:rows]
        k_slab[step] = seq_grad * value_ref[:, columns]
        v_slab[step] = seq_grad * key_ref[:, columns]
        lag_slab[step] = lag_refs[step][-taps:].astype(jnp.float32)
        for at, (slab, ref) in enumerate(((k_slab, k_ref), (v_slab, v_ref), (lag_slab, filter_ref))):
            stores.append(pltpu.make_async_copy(slab.at[step], ref.at[:, columns], sems.at[step, at]))
            stores[-1].start()
    for copy in stores:
        copy.wait()


def finish(received, early, key_rows, value_rows):
    ranks = len(received)
    width = received[0].shape[1]
    rows, channels = key_rows.shape
    taps = LAG_SPANS * SPAN // ranks
    if width % LANES:
        order = step_orders(ranks)[2]
        pieces = [received[order.index(step)] for step in range(ranks)]
        for step, piece in zip(early_steps(ranks), early):
            pieces[step] = jnp.concatenate([piece, pieces[step]], 0)
        slots = swapped(lax.axis_index("ctx"), lax.iota(jnp.int32, ranks))
        flat = jnp.stack(pieces)[slots].astype(jnp.float32).transpose(1, 0, 2)
        flat = flat.reshape(rows + taps, channels)
        seq_grad = flat[:rows]
        k_grad = (seq_grad * value_rows.astype(jnp.float32)).astype(jnp.bfloat16)
        v_grad = (seq_grad * key_rows.astype(jnp.float32)).astype(jnp.bfloat16)
        return k_grad, v_grad, flat[rows:]
    return pl.pallas_call(
        functools.partial(finish_kernel, ranks=ranks, early=len(early)),
        in_specs=[pl.BlockSpec(memory_space=pltpu.VMEM)] * (ranks + len(early) + 2),
        out_specs=[pl.BlockSpec(memory_space=pltpu.HBM)] * 3,
        out_shape=[
            jax.ShapeDtypeStruct((rows, channels), jnp.bfloat16),
            jax.ShapeDtypeStruct((rows, channels), jnp.bfloat16),
            jax.ShapeDtypeStruct((taps, channels), jnp.float32),
        ],
        scratch_shapes=[pltpu.VMEM((ranks, rows, width), jnp.bfloat16)] * 2
        + [pltpu.VMEM((ranks, taps, width), jnp.float32), pltpu.SemaphoreType.DMA((ranks, 3))],
        compiler_params=pltpu.CompilerParams(vmem_limit_bytes=VMEM_BYTES),
        cost_estimate=pl.CostEstimate(
            flops=2 * rows * channels,
            bytes_accessed=channels * (10 * rows + 6 * taps),
            transcendentals=0,
        ),
    )(*received, *early, key_rows, value_rows)


def on_device(out_grad, query_rows, key_rows, value_rows, conv_rows, long_filter, block_table):
    ranks = lax.axis_size("ctx")
    constants = (block_table, *(jnp.asarray(table) for table in transform_tables()))

    def swap(piece, step):
        pairs = [(rank, rank ^ step) for rank in range(ranks)]
        return lax.ppermute(piece, "ctx", pairs) if step else piece

    def exchange(pieces, message):
        return [swap(pieces[step], step) for step in step_orders(ranks)[message]]

    weighted = exchange(prepare((out_grad, query_rows, long_filter), ranks), 0)
    product = exchange(prepare((key_rows, value_rows), ranks, weighted[:1]), 1)
    q_grad = (out_grad.astype(jnp.float32) * conv_rows.astype(jnp.float32)).astype(jnp.bfloat16)
    seq_grad, spectrum, *early = weighted_part(weighted, constants)
    early = [swap(piece, step) for step, piece in zip(early_steps(ranks), early)]
    pieces = list(product_part(product, seq_grad, spectrum, constants))
    order = step_orders(ranks)[2]
    returned = {step + ranks: piece for step, piece in zip(early_steps(ranks), early)}
    for step in order:
        ahead = starts_after(ranks).get(step)
        if ahead is not None:
            pieces[step], returned[ahead] = lax.optimization_barrier((pieces[step], returned[ahead]))
        returned[step] = swap(pieces[step], step)
    early = [returned[step + ranks] for step in early_steps(ranks)]
    returned = [returned[step] for step in order]
    return (q_grad, *finish(returned, early, key_rows, value_rows))


def solution(mesh):
    in_specs = (P("ctx", "tp"),) * 6 + (P(),)
    out_specs = (P("ctx", "tp"),) * 4
    return jax.shard_map(
        on_device, mesh=mesh, in_specs=in_specs, out_specs=out_specs, check_vma=False
    )
```

time: 1260 us -> 56.6 us (0.04); the launches traced: 1240 us -> 56.4 us
  other arithmetic: 433 us -> 1.36 us
  local copies, waits for them, and re-layouts: 342 us -> 0.04 us
  waiting for transfers between devices: 237 us -> 12.7 us
  matrix products: 175 us -> 0 us
  loops' own time: 42.5 us -> 0 us
  starting transfers between devices: 0.12 us -> 27.8 us
  Pallas kernels: 0 us -> 13.7 us
  between operations: 14.2 us -> 0.78 us
    psum x1 -> x0, waiting for transfers between devices: 210 us -> none  [on_device(): summed = lax.psum(lag_rows, 'ctx')]
    scatter-add x24 -> x0, other arithmetic: 194 us -> none  [the longest x12 97.3 us: update(): lag_real.at[chosen]]
    mul x13 -> x0, other arithmetic: 193 us -> none  [the longest x12 184 us: update(): inside * (prod_real * grad_imag - prod_imag * grad_real)]
    gather x24 -> x0, local copies, waits for them, and re-layouts: 191 us -> none  [the longest x12 95.8 us: update(): pick_real = seg_real[chosen]]
    dot_general x32 -> x0, matrix products: 175 us -> none  [the longest x13 37.2 us: forward_low(): jnp.einsum('wt,ntc->nwc', sine_low[:, :in_rows], blocks, preferred_elemen...]
    mul x24 -> x0, local copies, waits for them, and re-layouts: 58 us -> none  [update(): du_real = du_real + inside * (pick_real * grad_real + pick_imag * grad_imag)]
    unnamed x24 -> x14, local copies, waits for them, and re-layouts: 46.7 us -> 0.04 us
    another operation x17 -> x0, loops' own time: 42.5 us -> none  [the longest x1 41.9 us: absorb(): carried, unused = lax.scan(absorb_block, carried, (incoming, offsets))]
  transfers between devices with their start and end apart: 3 -> 23, of which waited for: 2 -> 9; matrix products, arithmetic and copies ran while one was open for 9% -> 2% of each run, Pallas kernels for 0% -> 18%
where the time goes in v1:
time: 56.6 us; the launch traced here: 56.4 us
  starting transfers between devices  27.8 us (49%)
  Pallas kernels  13.7 us (24%)
  waiting for transfers between devices  12.7 us (22%)
  other arithmetic  1.36 us (2%)
  between operations  0.78 us (1%)
    ppermute x23, starting transfers between devices, swap(): return lax.ppermute(piece, 'ctx', pairs) if step else piece  27.8 us
    ppermute x23, waiting for transfers between devices, swap(): return lax.ppermute(piece, 'ctx', pairs) if step else piece  12.7 us
    pallas_call x2, Pallas kernels, spectral_call(): pl.pallas_call(kernel, in_specs=[pl.BlockSpec(memory_space=pltpu.SMEM)] +...  8.2 us
    pallas_call x2, Pallas kernels, prepare(): pl.pallas_call(functools.partial(prepare_kernel, ranks=ranks, count=len(a...  3.71 us
    pallas_call x1, Pallas kernels, finish(): pl.pallas_call(functools.partial(finish_kernel, ranks=ranks, early=len(ea...  1.81 us
    convert_element_type x1, other arithmetic, on_device(): (out_grad.astype(jnp.float32) * conv_rows.astype(jnp.float32)).astype(jnp...  1.36 us
  transfers between devices with their start and end apart: 23, of which 9 were waited for; matrix products, arithmetic and copies ran while one was open for 2% of the time, Pallas kernels for 18%

profile of v1, /device:TPU:0, one launch (start us, length us, event | category | flops | bytes accessed | tf_op | source)
XLA Modules:
  0.0 56.4 jit_solution(3831653104792693124)
XLA Ops:
  0.6 0.0 copy-start.2
  0.6 0.0 copy-start.3
  0.7 0.0 copy-start.4
  0.7 2.0 %shard_map.120 = (bf16[352,256]{1,0:T(8,128)(2,1)S(1)}, bf16[352,256]{1,0:T(8,128)(2,1)S(1)}, bf16[352,256]{1,0:T(8,128)(2,1)S(1)}, bf16[352,256]{1,0:T(8,128)(2...) custom-call(bf16[256,2048]{1,0:T(8,128)(2,1)} %refs_0_.2, ...), custom_call_target="tpu_custom_call" | custom-call | flops 524288 | bytes 5767168 | tf_op jit(solution)/shard_map/pallas_call | solution.py:90
  2.7 3.0 %collective-permute-start = (bf16[352,256]{1,0:T(8,128)(2,1)S(1)}, bf16[352,256]{1,0:T(8,128)(2,1)S(1)}, u32[]{:S(2)}, u32[]{:S(2)}) collective-permute-start(bf16[352,256]{1,0:T(8,128)(2,1)S(1)} %get-tuple-element.43), channel_id=1, source_target_pairs={{0,16},{4,20},{8,24},{12,28},{16,0},{20,4},{24,8},{28,12},{1,17},{... | collective-permute-start | bytes 540680 | tf_op jit(solution)/shard_map/ppermute | solution.py:376
  5.7 0.0 collective-permute-start.1
  5.7 1.5 %collective-permute-start.2 = (bf16[352,256]{1,0:T(8,128)(2,1)S(1)}, bf16[352,256]{1,0:T(8,128)(2,1)S(1)}, u32[]{:S(2)}, u32[]{:S(2)}) collective-permute-start(bf16[352,256]{1,0:T(8,128)(2,1)S(1)} %get-tuple-element.45), channel_id=1, source_target_pairs={{0,8},{4,12},{8,0},{12,4},{16,24},{20,28},{24,16},{28,20},{1,9},{5... | collective-permute-start | bytes 540680 | tf_op jit(solution)/shard_map/ppermute | solution.py:376
  7.2 0.1 collective-permute-start.3
  7.4 2.4 %collective-permute-start.4 = (bf16[352,256]{1,0:T(8,128)(2,1)S(1)}, bf16[352,256]{1,0:T(8,128)(2,1)S(1)}, u32[]{:S(2)}, u32[]{:S(2)}) collective-permute-start(bf16[352,256]{1,0:T(8,128)(2,1)S(1)} %get-tuple-element.47), channel_id=1, source_target_pairs={{0,28},{4,24},{8,20},{12,16},{16,12},{20,8},{24,4},{28,0},{1,29},{... | collective-permute-start | bytes 540680 | tf_op jit(solution)/shard_map/ppermute | solution.py:376
  9.7 0.6 %collective-permute-done.refs_0_.refs_2_ = bf16[352,256]{1,0:T(8,128)(2,1)S(1)} collective-permute-done((bf16[352,256]{1,0:T(8,128)(2,1)S(1)}, bf16[352,256]{1,0:T(8,128)(2,1)S(1)}, u32[]{:S(2)}, u32[]{:S(2)}) %collective-permute-start) | collective-permute-done | bytes 180256 | tf_op jit(solution)/shard_map/ppermute | solution.py:376
  10.3 0.3 collective-permute-start.5
  10.6 0.0 collective-permute-done.1.refs_1_
  10.6 2.6 %collective-permute-start.6 = (bf16[352,256]{1,0:T(8,128)(2,1)S(1)}, bf16[352,256]{1,0:T(8,128)(2,1)S(1)}, u32[]{:S(2)}, u32[]{:S(2)}) collective-permute-start(bf16[352,256]{1,0:T(8,128)(2,1)S(1)} %get-tuple-element.49), channel_id=1, source_target_pairs={{0,12},{4,8},{8,4},{12,0},{16,28},{20,24},{24,20},{28,16},{1,13},{... | collective-permute-start | bytes 540680 | tf_op jit(solution)/shard_map/ppermute | solution.py:376
  13.2 1.7 %shard_map.122 = (bf16[256,256]{1,0:T(8,128)(2,1)S(1)}, bf16[256,256]{1,0:T(8,128)(2,1)S(1)}, bf16[256,256]{1,0:T(8,128)(2,1)S(1)}, bf16[256,256]{1,0:T(8,128)(2...) custom-call(bf16[256,2048]{1,0:T(8,128)(2,1)} %refs_10_.1, ...), custom_call_target="tpu_custom_call" | custom-call | flops 524288 | bytes 4194304 | tf_op jit(solution)/shard_map/pallas_call | solution.py:90
  14.9 0.0 collective-permute-done.2.refs_2_
  14.9 0.1 collective-permute-start.10
  15.0 1.6 %collective-permute-done.3.refs_3_ = bf16[352,256]{1,0:T(8,128)(2,1)S(1)} collective-permute-done((bf16[352,256]{1,0:T(8,128)(2,1)S(1)}, bf16[352,256]{1,0:T(8,128)(2,1)S(1)}, u32[]{:S(2)}, u32[]{:S(2)}) %collective-permute-start.3) | collective-permute-done | bytes 180256 | tf_op jit(solution)/shard_map/ppermute | solution.py:376
  16.6 1.9 %collective-permute-start.11 = (bf16[256,256]{1,0:T(8,128)(2,1)S(1)}, bf16[256,256]{1,0:T(8,128)(2,1)S(1)}, u32[]{:S(2)}, u32[]{:S(2)}) collective-permute-start(bf16[256,256]{1,0:T(8,128)(2,1)S(1)} %get-tuple-element.57), channel_id=1, source_target_pairs={{0,16},{4,20},{8,24},{12,28},{16,0},{20,4},{24,8},{28,12},{1,17},{... | collective-permute-start | bytes 393224 | tf_op jit(solution)/shard_map/ppermute | solution.py:376
  18.5 1.4 %collective-permute-done.4.refs_4_ = bf16[352,256]{1,0:T(8,128)(2,1)S(1)} collective-permute-done((bf16[352,256]{1,0:T(8,128)(2,1)S(1)}, bf16[352,256]{1,0:T(8,128)(2,1)S(1)}, u32[]{:S(2)}, u32[]{:S(2)}) %collective-permute-start.4) | collective-permute-done | bytes 180256 | tf_op jit(solution)/shard_map/ppermute | solution.py:376
  19.9 1.6 %collective-permute-start.12 = (bf16[256,256]{1,0:T(8,128)(2,1)S(1)}, bf16[256,256]{1,0:T(8,128)(2,1)S(1)}, u32[]{:S(2)}, u32[]{:S(2)}) collective-permute-start(bf16[256,256]{1,0:T(8,128)(2,1)S(1)} %get-tuple-element.58), channel_id=1, source_target_pairs={{0,8},{4,12},{8,0},{12,4},{16,24},{20,28},{24,16},{28,20},{1,9},{5... | collective-permute-start | bytes 393224 | tf_op jit(solution)/shard_map/ppermute | solution.py:376
  21.6 2.4 %collective-permute-done.5.refs_5_ = bf16[352,256]{1,0:T(8,128)(2,1)S(1)} collective-permute-done((bf16[352,256]{1,0:T(8,128)(2,1)S(1)}, bf16[352,256]{1,0:T(8,128)(2,1)S(1)}, u32[]{:S(2)}, u32[]{:S(2)}) %collective-permute-start.5) | collective-permute-done | bytes 180256 | tf_op jit(solution)/shard_map/ppermute | solution.py:376
  24.0 2.8 %collective-permute-start.13 = (bf16[256,256]{1,0:T(8,128)(2,1)S(1)}, bf16[256,256]{1,0:T(8,128)(2,1)S(1)}, u32[]{:S(2)}, u32[]{:S(2)}) collective-permute-start(bf16[256,256]{1,0:T(8,128)(2,1)S(1)} %get-tuple-element.59), channel_id=1, source_target_pairs={{0,24},{4,28},{8,16},{12,20},{16,8},{20,12},{24,0},{28,4},{1,25},{... | collective-permute-start | bytes 393224 | tf_op jit(solution)/shard_map/ppermute | solution.py:376
  26.8 0.0 collective-permute-done.6.refs_6_
  26.8 0.0 collective-permute-start.7
  26.8 0.0 collective-permute-done.10.refs_3_
  26.8 1.7 %collective-permute-start.8 = (bf16[256,256]{1,0:T(8,128)(2,1)S(1)}, bf16[256,256]{1,0:T(8,128)(2,1)S(1)}, u32[]{:S(2)}, u32[]{:S(2)}) collective-permute-start(bf16[256,256]{1,0:T(8,128)(2,1)S(1)} %get-tuple-element.54), channel_id=1, source_target_pairs={{0,20},{4,16},{8,28},{12,24},{16,4},{20,0},{24,12},{28,8},{1,21},{... | collective-permute-start | bytes 393224 | tf_op jit(solution)/shard_map/ppermute | solution.py:376
  28.5 0.0 collective-permute-done.11.refs_4_
  28.5 0.3 collective-permute-start.9
  28.8 0.0 copy-done.2
  28.8 0.0 copy-done.3
  28.9 0.0 copy-done.4
  28.9 4.1 %shard_map.121 = (bf16[8,256,256]{2,1,0:T(8,128)(2,1)S(1)}, f32[8,512,256]{2,1,0:T(8,128)S(1)}, bf16[256,256]{1,0:T(8,128)(2,1)S(1)}, bf16[256,256]{1,0:T(8,128)(2,1)S(1)}) custom-call(s32[16]{0:T(128)S(1)} %copy-done.4, bf16[512,256]{1,0:T(8,128)(2,1)S(1)} %copy-done.2, bf16[256,512]{1,0:T(8,128)(2,1)S(1)} %copy-done.3, ...), custom_call_target="tpu_custom_call" | custom-call | flops 1275068416 | bytes 7471168 | tf_op jit(solution)/shard_map/pallas_call | solution.py:253
  33.0 0.0 collective-permute-done.12.refs_5_
  33.0 1.1 %collective-permute-start.16 = (bf16[256,256]{1,0:T(8,128)(2,1)S(1)}, bf16[256,256]{1,0:T(8,128)(2,1)S(1)}, u32[]{:S(2)}, u32[]{:S(2)}) collective-permute-start(bf16[256,256]{1,0:T(8,128)(2,1)S(1)} %get-tuple-element.68), channel_id=1, source_target_pairs={{0,28},{4,24},{8,20},{12,16},{16,12},{20,8},{24,4},{28,0},{1,29},{... | collective-permute-start | bytes 393224 | tf_op jit(solution)/shard_map/ppermute | solution.py:376
  34.1 0.0 collective-permute-done.13.refs_6_
  34.1 2.8 %collective-permute-start.14 = (bf16[256,256]{1,0:T(8,128)(2,1)S(1)}, bf16[256,256]{1,0:T(8,128)(2,1)S(1)}, u32[]{:S(2)}, u32[]{:S(2)}) collective-permute-start(bf16[256,256]{1,0:T(8,128)(2,1)S(1)} %get-tuple-element.63), channel_id=1, source_target_pairs={{0,24},{4,28},{8,16},{12,20},{16,8},{20,12},{24,0},{28,4},{1,25},{... | collective-permute-start | bytes 393224 | tf_op jit(solution)/shard_map/ppermute | solution.py:376
  36.9 0.0 collective-permute-done.7.refs_0_
  36.9 0.0 collective-permute-done.8.refs_1_
  36.9 0.0 collective-permute-done.9.refs_2_
  36.9 0.0 copy-start.5
  36.9 0.0 copy-start.6
  36.9 4.1 %shard_map.123 = (bf16[352,256]{1,0:T(8,128)(2,1)S(1)}, bf16[352,256]{1,0:T(8,128)(2,1)S(1)}, bf16[352,256]{1,0:T(8,128)(2,1)S(1)}, bf16[352,256]{1,0:T(8,128)(2...) custom-call(s32[16]{0:T(128)S(1)} %copy-done.4, ...), custom_call_target="tpu_custom_call" | custom-call | flops 738197504 | bytes 7995456 | tf_op jit(solution)/shard_map/pallas_call | solution.py:253
  41.0 0.0 copy-start
  41.0 0.0 copy-start.1
  41.0 0.0 collective-permute-done.16.refs_9_
  41.0 0.9 %collective-permute-start.17 = (bf16[352,256]{1,0:T(8,128)(2,1)S(1)}, bf16[352,256]{1,0:T(8,128)(2,1)S(1)}, u32[]{:S(2)}, u32[]{:S(2)}) collective-permute-start(bf16[352,256]{1,0:T(8,128)(2,1)S(1)} %get-tuple-element.69), channel_id=1, source_target_pairs={{0,8},{4,12},{8,0},{12,4},{16,24},{20,28},{24,16},{28,20},{1,9},{5... | collective-permute-start | bytes 540680 | tf_op jit(solution)/shard_map/ppermute | solution.py:376
  41.9 0.7 %collective-permute-done.14.refs_8_ = bf16[256,256]{1,0:T(8,128)(2,1)S(1)} collective-permute-done((bf16[256,256]{1,0:T(8,128)(2,1)S(1)}, bf16[256,256]{1,0:T(8,128)(2,1)S(1)}, u32[]{:S(2)}, u32[]{:S(2)}) %collective-permute-start.14) | collective-permute-done | bytes 131104 | tf_op jit(solution)/shard_map/ppermute | solution.py:376
  42.6 1.2 %collective-permute-start.15 = (bf16[352,256]{1,0:T(8,128)(2,1)S(1)}, bf16[352,256]{1,0:T(8,128)(2,1)S(1)}, u32[]{:S(2)}, u32[]{:S(2)}) collective-permute-start(bf16[352,256]{1,0:T(8,128)(2,1)S(1)} %get-tuple-element.64), channel_id=1, source_target_pairs={{0,16},{4,20},{8,24},{12,28},{16,0},{20,4},{24,8},{28,12},{1,17},{... | collective-permute-start | bytes 540680 | tf_op jit(solution)/shard_map/ppermute | solution.py:376
  43.8 0.0 collective-permute-start.18
  43.8 1.7 %collective-permute-start.19 = (bf16[352,256]{1,0:T(8,128)(2,1)S(1)}, bf16[352,256]{1,0:T(8,128)(2,1)S(1)}, u32[]{:S(2)}, u32[]{:S(2)}) collective-permute-start(bf16[352,256]{1,0:T(8,128)(2,1)S(1)} %get-tuple-element.72), channel_id=1, source_target_pairs={{0,12},{4,8},{8,4},{12,0},{16,28},{20,24},{24,20},{28,16},{1,13},{... | collective-permute-start | bytes 540680 | tf_op jit(solution)/shard_map/ppermute | solution.py:376
  45.5 0.0 collective-permute-start.20
  45.5 2.5 %collective-permute-done.17.refs_1_ = bf16[352,256]{1,0:T(8,128)(2,1)S(1)} collective-permute-done((bf16[352,256]{1,0:T(8,128)(2,1)S(1)}, bf16[352,256]{1,0:T(8,128)(2,1)S(1)}, u32[]{:S(2)}, u32[]{:S(2)}) %collective-permute-start.17) | collective-permute-done | bytes 180256 | tf_op jit(solution)/shard_map/ppermute | solution.py:376
  48.0 0.0 collective-permute-start.22
  48.0 1.5 %collective-permute-done.15.refs_0_ = bf16[352,256]{1,0:T(8,128)(2,1)S(1)} collective-permute-done((bf16[352,256]{1,0:T(8,128)(2,1)S(1)}, bf16[352,256]{1,0:T(8,128)(2,1)S(1)}, u32[]{:S(2)}, u32[]{:S(2)}) %collective-permute-start.15) | collective-permute-done | bytes 180256 | tf_op jit(solution)/shard_map/ppermute | solution.py:376
  49.6 1.7 %collective-permute-start.21 = (bf16[96,256]{1,0:T(8,128)(2,1)S(1)}, bf16[96,256]{1,0:T(8,128)(2,1)S(1)}, u32[]{:S(2)}, u32[]{:S(2)}) collective-permute-start(bf16[96,256]{1,0:T(8,128)(2,1)S(1)} %get-tuple-element.74), channel_id=1, source_target_pairs={{0,24},{4,28},{8,16},{12,20},{16,8},{20,12},{24,0},{28,4},{1,25},{... | collective-permute-start | bytes 147464 | tf_op jit(solution)/shard_map/ppermute | solution.py:376
  51.3 0.0 copy-done.5
  51.3 0.0 copy-done.6
  51.3 1.4 %multiply_convert_fusion = bf16[256,2048]{1,0:T(8,128)(2,1)} fusion(bf16[256,2048]{1,0:T(8,128)(2,1)S(1)} %copy-done.6, bf16[256,2048]{1,0:T(8,128)(2,1)S(1)} %copy-done.5), kind=kLoop, calls=%fused_computation | loop fusion | flops 2097152 | bytes 3145728 | tf_op jit(solution)/shard_map/convert_element_type | solution.py:383
  52.7 0.1 collective-permute-done.18.refs_2_
  52.8 0.0 collective-permute-done.19.refs_3_
  52.8 0.0 collective-permute-done.20.refs_4_
  52.8 0.0 collective-permute-done.22.refs_6_
  52.8 1.8 %collective-permute-done.21.refs_5_ = bf16[96,256]{1,0:T(8,128)(2,1)S(1)} collective-permute-done((bf16[96,256]{1,0:T(8,128)(2,1)S(1)}, bf16[96,256]{1,0:T(8,128)(2,1)S(1)}, u32[]{:S(2)}, u32[]{:S(2)}) %collective-permute-start.21) | collective-permute-done | bytes 49184 | tf_op jit(solution)/shard_map/ppermute | solution.py:376
  54.6 1.8 %shard_map.124 = (bf16[256,2048]{1,0:T(8,128)(2,1)}, bf16[256,2048]{1,0:T(8,128)(2,1)}, f32[96,2048]{1,0:T(8,128)}) custom-call(bf16[352,256]{1,0:T(8,128)(2,1)S(1)} %collective-permute-done.15.refs_0_, bf16[352,256]{1,0:T(8,128)(2,1)S(1)} %collective-permute-done.17.refs_1_, bf16[352,256]{1,0:T(8,128)(2,1)S(1)} %collective-permute-done.18.refs_2_, ...), custom_call_target="tpu_custom_call" | custom-call | flops 1048576 | bytes 6422528 | tf_op jit(solution)/shard_map/pallas_call | solution.py:350
  (2 shorter events, 0.0 us)
Async XLA Ops:
  0.6 28.2 %copy-start.2 = (bf16[512,256]{1,0:T(8,128)(2,1)S(1)}, bf16[512,256]{1,0:T(8,128)(2,1)}, u32[]{:S(2)}) copy-start(bf16[512,256]{1,0:T(8,128)(2,1)} %constant.4.clone.forward_ref) | copy-start | bytes 786436
  0.6 28.2 %copy-start.3 = (bf16[256,512]{1,0:T(8,128)(2,1)S(1)}, bf16[256,512]{1,0:T(8,128)(2,1)}, u32[]{:S(2)}) copy-start(bf16[256,512]{1,0:T(8,128)(2,1)} %constant.5.clone.inverse_ref) | copy-start | bytes 786436
  0.7 28.2 %copy-start.4 = (s32[16]{0:T(128)S(1)}, s32[16]{0:T(128)}, u32[]{:S(2)}) copy-start(s32[16]{0:T(128)} %table_ref.3) | copy-start | bytes 196
  2.7 7.6 %collective-permute-start = (bf16[352,256]{1,0:T(8,128)(2,1)S(1)}, bf16[352,256]{1,0:T(8,128)(2,1)S(1)}, u32[]{:S(2)}, u32[]{:S(2)}) collective-permute-start(bf16[352,256]{1,0:T(8,128)(2,1)S(1)} %get-tuple-element.43), channel_id=1, source_target_pairs={{0,16},{4,20},{8,24},{12,28},{16,0},{20,4},{24,8},{28,12},{1,17},{... | collective-permute-start | bytes 540680 | tf_op jit(solution)/shard_map/ppermute | solution.py:376
  5.7 4.9 %collective-permute-start.1 = (bf16[352,256]{1,0:T(8,128)(2,1)S(1)}, bf16[352,256]{1,0:T(8,128)(2,1)S(1)}, u32[]{:S(2)}, u32[]{:S(2)}) collective-permute-start(bf16[352,256]{1,0:T(8,128)(2,1)S(1)} %get-tuple-element.44), channel_id=1, source_target_pairs={{0,4},{4,0},{8,12},{12,8},{16,20},{20,16},{24,28},{28,24},{1,5},{5... | collective-permute-start | bytes 540680 | tf_op jit(solution)/shard_map/ppermute | solution.py:376
  5.7 9.2 %collective-permute-start.2 = (bf16[352,256]{1,0:T(8,128)(2,1)S(1)}, bf16[352,256]{1,0:T(8,128)(2,1)S(1)}, u32[]{:S(2)}, u32[]{:S(2)}) collective-permute-start(bf16[352,256]{1,0:T(8,128)(2,1)S(1)} %get-tuple-element.45), channel_id=1, source_target_pairs={{0,8},{4,12},{8,0},{12,4},{16,24},{20,28},{24,16},{28,20},{1,9},{5... | collective-permute-start | bytes 540680 | tf_op jit(solution)/shard_map/ppermute | solution.py:376
  7.2 9.4 %collective-permute-start.3 = (bf16[352,256]{1,0:T(8,128)(2,1)S(1)}, bf16[352,256]{1,0:T(8,128)(2,1)S(1)}, u32[]{:S(2)}, u32[]{:S(2)}) collective-permute-start(bf16[352,256]{1,0:T(8,128)(2,1)S(1)} %get-tuple-element.46), channel_id=1, source_target_pairs={{0,24},{4,28},{8,16},{12,20},{16,8},{20,12},{24,0},{28,4},{1,25},{... | collective-permute-start | bytes 540680 | tf_op jit(solution)/shard_map/ppermute | solution.py:376
  7.4 12.6 %collective-permute-start.4 = (bf16[352,256]{1,0:T(8,128)(2,1)S(1)}, bf16[352,256]{1,0:T(8,128)(2,1)S(1)}, u32[]{:S(2)}, u32[]{:S(2)}) collective-permute-start(bf16[352,256]{1,0:T(8,128)(2,1)S(1)} %get-tuple-element.47), channel_id=1, source_target_pairs={{0,28},{4,24},{8,20},{12,16},{16,12},{20,8},{24,4},{28,0},{1,29},{... | collective-permute-start | bytes 540680 | tf_op jit(solution)/shard_map/ppermute | solution.py:376
  10.3 13.7 %collective-permute-start.5 = (bf16[352,256]{1,0:T(8,128)(2,1)S(1)}, bf16[352,256]{1,0:T(8,128)(2,1)S(1)}, u32[]{:S(2)}, u32[]{:S(2)}) collective-permute-start(bf16[352,256]{1,0:T(8,128)(2,1)S(1)} %get-tuple-element.48), channel_id=1, source_target_pairs={{0,20},{4,16},{8,28},{12,24},{16,4},{20,0},{24,12},{28,8},{1,21},{... | collective-permute-start | bytes 540680 | tf_op jit(solution)/shard_map/ppermute | solution.py:376
  10.6 16.2 %collective-permute-start.6 = (bf16[352,256]{1,0:T(8,128)(2,1)S(1)}, bf16[352,256]{1,0:T(8,128)(2,1)S(1)}, u32[]{:S(2)}, u32[]{:S(2)}) collective-permute-start(bf16[352,256]{1,0:T(8,128)(2,1)S(1)} %get-tuple-element.49), channel_id=1, source_target_pairs={{0,12},{4,8},{8,4},{12,0},{16,28},{20,24},{24,20},{28,16},{1,13},{... | collective-permute-start | bytes 540680 | tf_op jit(solution)/shard_map/ppermute | solution.py:376
  14.9 11.8 %collective-permute-start.10 = (bf16[256,256]{1,0:T(8,128)(2,1)S(1)}, bf16[256,256]{1,0:T(8,128)(2,1)S(1)}, u32[]{:S(2)}, u32[]{:S(2)}) collective-permute-start(bf16[256,256]{1,0:T(8,128)(2,1)S(1)} %get-tuple-element.56), channel_id=1, source_target_pairs={{0,4},{4,0},{8,12},{12,8},{16,20},{20,16},{24,28},{28,24},{1,5},{5... | collective-permute-start | bytes 393224 | tf_op jit(solution)/shard_map/ppermute | solution.py:376
  16.6 11.9 %collective-permute-start.11 = (bf16[256,256]{1,0:T(8,128)(2,1)S(1)}, bf16[256,256]{1,0:T(8,128)(2,1)S(1)}, u32[]{:S(2)}, u32[]{:S(2)}) collective-permute-start(bf16[256,256]{1,0:T(8,128)(2,1)S(1)} %get-tuple-element.57), channel_id=1, source_target_pairs={{0,16},{4,20},{8,24},{12,28},{16,0},{20,4},{24,8},{28,12},{1,17},{... | collective-permute-start | bytes 393224 | tf_op jit(solution)/shard_map/ppermute | solution.py:376
  19.9 13.1 %collective-permute-start.12 = (bf16[256,256]{1,0:T(8,128)(2,1)S(1)}, bf16[256,256]{1,0:T(8,128)(2,1)S(1)}, u32[]{:S(2)}, u32[]{:S(2)}) collective-permute-start(bf16[256,256]{1,0:T(8,128)(2,1)S(1)} %get-tuple-element.58), channel_id=1, source_target_pairs={{0,8},{4,12},{8,0},{12,4},{16,24},{20,28},{24,16},{28,20},{1,9},{5... | collective-permute-start | bytes 393224 | tf_op jit(solution)/shard_map/ppermute | solution.py:376
  24.0 10.1 %collective-permute-start.13 = (bf16[256,256]{1,0:T(8,128)(2,1)S(1)}, bf16[256,256]{1,0:T(8,128)(2,1)S(1)}, u32[]{:S(2)}, u32[]{:S(2)}) collective-permute-start(bf16[256,256]{1,0:T(8,128)(2,1)S(1)} %get-tuple-element.59), channel_id=1, source_target_pairs={{0,24},{4,28},{8,16},{12,20},{16,8},{20,12},{24,0},{28,4},{1,25},{... | collective-permute-start | bytes 393224 | tf_op jit(solution)/shard_map/ppermute | solution.py:376
  26.8 10.1 %collective-permute-start.7 = (bf16[256,256]{1,0:T(8,128)(2,1)S(1)}, bf16[256,256]{1,0:T(8,128)(2,1)S(1)}, u32[]{:S(2)}, u32[]{:S(2)}) collective-permute-start(bf16[256,256]{1,0:T(8,128)(2,1)S(1)} %get-tuple-element.53), channel_id=1, source_target_pairs={{0,28},{4,24},{8,20},{12,16},{16,12},{20,8},{24,4},{28,0},{1,29},{... | collective-permute-start | bytes 393224 | tf_op jit(solution)/shard_map/ppermute | solution.py:376
  26.8 10.1 %collective-permute-start.8 = (bf16[256,256]{1,0:T(8,128)(2,1)S(1)}, bf16[256,256]{1,0:T(8,128)(2,1)S(1)}, u32[]{:S(2)}, u32[]{:S(2)}) collective-permute-start(bf16[256,256]{1,0:T(8,128)(2,1)S(1)} %get-tuple-element.54), channel_id=1, source_target_pairs={{0,20},{4,16},{8,28},{12,24},{16,4},{20,0},{24,12},{28,8},{1,21},{... | collective-permute-start | bytes 393224 | tf_op jit(solution)/shard_map/ppermute | solution.py:376
  28.5 8.4 %collective-permute-start.9 = (bf16[256,256]{1,0:T(8,128)(2,1)S(1)}, bf16[256,256]{1,0:T(8,128)(2,1)S(1)}, u32[]{:S(2)}, u32[]{:S(2)}) collective-permute-start(bf16[256,256]{1,0:T(8,128)(2,1)S(1)} %get-tuple-element.55), channel_id=1, source_target_pairs={{0,12},{4,8},{8,4},{12,0},{16,28},{20,24},{24,20},{28,16},{1,13},{... | collective-permute-start | bytes 393224 | tf_op jit(solution)/shard_map/ppermute | solution.py:376
  33.0 8.0 %collective-permute-start.16 = (bf16[256,256]{1,0:T(8,128)(2,1)S(1)}, bf16[256,256]{1,0:T(8,128)(2,1)S(1)}, u32[]{:S(2)}, u32[]{:S(2)}) collective-permute-start(bf16[256,256]{1,0:T(8,128)(2,1)S(1)} %get-tuple-element.68), channel_id=1, source_target_pairs={{0,28},{4,24},{8,20},{12,16},{16,12},{20,8},{24,4},{28,0},{1,29},{... | collective-permute-start | bytes 393224 | tf_op jit(solution)/shard_map/ppermute | solution.py:376
  34.1 8.5 %collective-permute-start.14 = (bf16[256,256]{1,0:T(8,128)(2,1)S(1)}, bf16[256,256]{1,0:T(8,128)(2,1)S(1)}, u32[]{:S(2)}, u32[]{:S(2)}) collective-permute-start(bf16[256,256]{1,0:T(8,128)(2,1)S(1)} %get-tuple-element.63), channel_id=1, source_target_pairs={{0,24},{4,28},{8,16},{12,20},{16,8},{20,12},{24,0},{28,4},{1,25},{... | collective-permute-start | bytes 393224 | tf_op jit(solution)/shard_map/ppermute | solution.py:376
  36.9 14.4 %copy-start.5 = (bf16[256,2048]{1,0:T(8,128)(2,1)S(1)}, bf16[256,2048]{1,0:T(8,128)(2,1)}, u32[]{:S(2)}) copy-start(bf16[256,2048]{1,0:T(8,128)(2,1)} %refs_0_.2) | copy-start | bytes 3145732
  36.9 14.4 %copy-start.6 = (bf16[256,2048]{1,0:T(8,128)(2,1)S(1)}, bf16[256,2048]{1,0:T(8,128)(2,1)}, u32[]{:S(2)}) copy-start(bf16[256,2048]{1,0:T(8,128)(2,1)} %param.13) | copy-start | bytes 3145732
  41.0 13.6 %copy-start = (bf16[256,2048]{1,0:T(8,128)(2,1)S(1)}, bf16[256,2048]{1,0:T(8,128)(2,1)}, u32[]{:S(2)}) copy-start(bf16[256,2048]{1,0:T(8,128)(2,1)} %refs_10_.1) | copy-start | bytes 3145732
  41.0 13.6 %copy-start.1 = (bf16[256,2048]{1,0:T(8,128)(2,1)S(1)}, bf16[256,2048]{1,0:T(8,128)(2,1)}, u32[]{:S(2)}) copy-start(bf16[256,2048]{1,0:T(8,128)(2,1)} %refs_11_.1) | copy-start | bytes 3145732
  41.0 7.0 %collective-permute-start.17 = (bf16[352,256]{1,0:T(8,128)(2,1)S(1)}, bf16[352,256]{1,0:T(8,128)(2,1)S(1)}, u32[]{:S(2)}, u32[]{:S(2)}) collective-permute-start(bf16[352,256]{1,0:T(8,128)(2,1)S(1)} %get-tuple-element.69), channel_id=1, source_target_pairs={{0,8},{4,12},{8,0},{12,4},{16,24},{20,28},{24,16},{28,20},{1,9},{5... | collective-permute-start | bytes 540680 | tf_op jit(solution)/shard_map/ppermute | solution.py:376
  42.6 7.0 %collective-permute-start.15 = (bf16[352,256]{1,0:T(8,128)(2,1)S(1)}, bf16[352,256]{1,0:T(8,128)(2,1)S(1)}, u32[]{:S(2)}, u32[]{:S(2)}) collective-permute-start(bf16[352,256]{1,0:T(8,128)(2,1)S(1)} %get-tuple-element.64), channel_id=1, source_target_pairs={{0,16},{4,20},{8,24},{12,28},{16,0},{20,4},{24,8},{28,12},{1,17},{... | collective-permute-start | bytes 540680 | tf_op jit(solution)/shard_map/ppermute | solution.py:376
  43.8 9.0 %collective-permute-start.18 = (bf16[352,256]{1,0:T(8,128)(2,1)S(1)}, bf16[352,256]{1,0:T(8,128)(2,1)S(1)}, u32[]{:S(2)}, u32[]{:S(2)}) collective-permute-start(bf16[352,256]{1,0:T(8,128)(2,1)S(1)} %get-tuple-element.71), channel_id=1, source_target_pairs={{0,20},{4,16},{8,28},{12,24},{16,4},{20,0},{24,12},{28,8},{1,21},{... | collective-permute-start | bytes 540680 | tf_op jit(solution)/shard_map/ppermute | solution.py:376
  43.8 9.0 %collective-permute-start.19 = (bf16[352,256]{1,0:T(8,128)(2,1)S(1)}, bf16[352,256]{1,0:T(8,128)(2,1)S(1)}, u32[]{:S(2)}, u32[]{:S(2)}) collective-permute-start(bf16[352,256]{1,0:T(8,128)(2,1)S(1)} %get-tuple-element.72), channel_id=1, source_target_pairs={{0,12},{4,8},{8,4},{12,0},{16,28},{20,24},{24,20},{28,16},{1,13},{... | collective-permute-start | bytes 540680 | tf_op jit(solution)/shard_map/ppermute | solution.py:376
  45.5 7.3 %collective-permute-start.20 = (bf16[352,256]{1,0:T(8,128)(2,1)S(1)}, bf16[352,256]{1,0:T(8,128)(2,1)S(1)}, u32[]{:S(2)}, u32[]{:S(2)}) collective-permute-start(bf16[352,256]{1,0:T(8,128)(2,1)S(1)} %get-tuple-element.73), channel_id=1, source_target_pairs={{0,4},{4,0},{8,12},{12,8},{16,20},{20,16},{24,28},{28,24},{1,5},{5... | collective-permute-start | bytes 540680 | tf_op jit(solution)/shard_map/ppermute | solution.py:376
  48.0 4.8 %collective-permute-start.22 = (bf16[96,256]{1,0:T(8,128)(2,1)S(1)}, bf16[96,256]{1,0:T(8,128)(2,1)S(1)}, u32[]{:S(2)}, u32[]{:S(2)}) collective-permute-start(bf16[96,256]{1,0:T(8,128)(2,1)S(1)} %get-tuple-element.75), channel_id=1, source_target_pairs={{0,28},{4,24},{8,20},{12,16},{16,12},{20,8},{24,4},{28,0},{1,29},{... | collective-permute-start | bytes 147464 | tf_op jit(solution)/shard_map/ppermute | solution.py:376
  49.6 5.0 %collective-permute-start.21 = (bf16[96,256]{1,0:T(8,128)(2,1)S(1)}, bf16[96,256]{1,0:T(8,128)(2,1)S(1)}, u32[]{:S(2)}, u32[]{:S(2)}) collective-permute-start(bf16[96,256]{1,0:T(8,128)(2,1)S(1)} %get-tuple-element.74), channel_id=1, source_target_pairs={{0,24},{4,28},{8,16},{12,20},{16,8},{20,12},{24,0},{28,4},{1,25},{... | collective-permute-start | bytes 147464 | tf_op jit(solution)/shard_map/ppermute | solution.py:376

commit v2 on v1

--- a/solution.py
+++ b/solution.py
@@ -21,15 +21,23 @@
 def step_orders(ranks):
     if ranks != 8:
         return [list(range(ranks))] * 3
-    return [4, 1, 2, 6, 7, 5, 3, 0], [7, 5, 3, 1, 4, 2, 6, 0], [4, 2, 5, 3, 1, 6, 7, 0]
+    return [4, 2, 6, 7, 5, 3, 1, 0], [5, 3, 1, 4, 2, 6, 7, 0], [4, 2, 5, 3, 1, 6, 7, 0]
+
+
+def joint_steps(ranks):
+    return [5, 3, 1] if ranks == 8 else []
 
 
 def early_steps(ranks):
     return [6, 7] if ranks == 8 else []
 
 
+def first_steps(ranks):
+    return [0, 2, 4] if ranks == 8 else []
+
+
 def starts_after(ranks):
-    return {4: 8 + 6, 2: 8 + 7, 6: 4, 7: 2} if ranks == 8 else {}
+    return {4: 8 + 6, 2: 8 + 7, 1: 2, 6: 2, 7: 2} if ranks == 8 else {}
 
 
 def transform_tables():
@@ -44,8 +52,8 @@
     return jnp.bitwise_xor(device, step)
 
 
-def prepare_kernel(*refs, ranks, count, after):
-    sources, refs = refs[:count], refs[count + after :]
+def prepare_kernel(*refs, ranks, count, above):
+    sources, above_refs, refs = refs[:count], refs[count : count + len(above)], refs[count + len(above) :]
     targets, rest = refs[:ranks], refs[ranks:]
     slabs, in_sems = rest[:count], rest[count]
     rows, half = slabs[0].shape[1:]
@@ -70,12 +78,18 @@
                 load.wait()
         column = jnp.bitwise_and(swapped(device, inner), ranks // 2 - 1) * width
         columns = pl.ds(pl.multiple_of(column, LANES), width)
-        targets[step][:rows] = slabs[0][group, :, columns] * slabs[1][group, :, columns]
+        target = targets[step]
+        if step in above:
+            first = target.shape[0] - rows
+            target[:first] = above_refs[above.index(step)][...]
+            target = target.at[first:]
+        target[:rows] = slabs[0][group, :, columns] * slabs[1][group, :, columns]
         if count == 3:
-            targets[step][rows:] = slabs[2][group, :, columns].astype(jnp.bfloat16)
-
-
-def prepare(arrays, ranks, after=()):
+            target[rows:] = slabs[2][group, :, columns].astype(jnp.bfloat16)
+
+
+def prepare(arrays, ranks, above=()):
+    above = dict(above)
     rows, channels = arrays[0].shape
     width = channels // ranks
     out_rows = rows + sum(a.shape[0] for a in arrays[2:])
@@ -84,21 +98,23 @@
         packed = jnp.concatenate([left * right, *below], 0).astype(jnp.bfloat16)
         packed = packed.reshape(out_rows, ranks, width).transpose(1, 0, 2)
         device = lax.axis_index("ctx")
-        return [lax.dynamic_index_in_dim(packed, device ^ m, 0, False) for m in range(ranks)]
+        pieces = [lax.dynamic_index_in_dim(packed, device ^ m, 0, False) for m in range(ranks)]
+        return [jnp.concatenate([above[m], p], 0) if m in above else p for m, p in enumerate(pieces)]
+    piece_rows = [out_rows + (above[m].shape[0] if m in above else 0) for m in range(ranks)]
     half = channels // 2
     slabs = [pltpu.VMEM((2, a.shape[0], half), a.dtype) for a in arrays]
     return pl.pallas_call(
-        functools.partial(prepare_kernel, ranks=ranks, count=len(arrays), after=len(after)),
+        functools.partial(prepare_kernel, ranks=ranks, count=len(arrays), above=tuple(above)),
         in_specs=[pl.BlockSpec(memory_space=pltpu.HBM)] * len(arrays)
-        + [pl.BlockSpec(memory_space=pl.ANY)] * len(after),
+        + [pl.BlockSpec(memory_space=pltpu.VMEM)] * len(above),
         out_specs=[pl.BlockSpec(memory_space=pltpu.VMEM)] * ranks,
-        out_shape=[jax.ShapeDtypeStruct((out_rows, width), jnp.bfloat16)] * ranks,
+        out_shape=[jax.ShapeDtypeStruct((r, width), jnp.bfloat16) for r in piece_rows],
         scratch_shapes=slabs + [pltpu.SemaphoreType.DMA((2, len(arrays)))],
         compiler_params=pltpu.CompilerParams(vmem_limit_bytes=VMEM_BYTES),
         cost_estimate=pl.CostEstimate(
             flops=rows * channels, bytes_accessed=8 * out_rows * channels, transcendentals=0
         ),
-    )(*(pltpu.with_memory_space_constraint(a, pltpu.HBM) for a in arrays), *after)
+    )(*(pltpu.with_memory_space_constraint(a, pltpu.HBM) for a in arrays), *above.values())
 
 
 class Spans:
@@ -127,8 +143,9 @@
 
 def gather_pieces(pieces, recv_ref, message):
     device = lax.axis_index("ctx")
+    rows = recv_ref.shape[1]
     for step, piece in zip(step_orders(len(pieces))[message], pieces):
-        recv_ref[swapped(device, step)] = piece[...]
+        recv_ref[swapped(device, step)] = piece[-rows:] if message else piece[:rows]
 
 
 def added(total, left, right):
@@ -267,7 +284,8 @@
 
 def weighted_part(received, constants):
     ranks = len(received)
-    recv_rows, width = received[0].shape
+    width = received[0].shape[1]
+    recv_rows = SPAN + LAG_SPANS * SPAN // ranks
     return spectral_call(
         weighted_kernel,
         (*constants, *received),
@@ -308,63 +326,84 @@
     )
 
 
-def finish_kernel(*refs, ranks, early):
-    received, early_refs, refs = refs[:ranks], refs[ranks : ranks + early], refs[ranks + early :]
-    key_ref, value_ref, k_ref, v_ref, filter_ref, k_slab, v_slab, lag_slab, sems = refs
+def finish_kernel(*refs, steps):
+    pieces, refs = refs[: len(steps)], refs[len(steps) :]
+    (key_ref, value_ref), (k_ref, v_ref, filter_ref, k_slab, v_slab, lag_slab, sems) = refs[:2], refs[-7:]
     _, rows, width = k_slab.shape
     taps = lag_slab.shape[1]
-    seq_refs = dict(zip(step_orders(ranks)[2], received)) | dict(zip(early_steps(ranks), early_refs))
-    lag_refs = dict(zip(step_orders(ranks)[2], received))
     device = lax.axis_index("ctx")
     stores = []
-    for step in range(ranks):
+    for at, (step, piece) in enumerate(zip(steps, pieces)):
         columns = pl.ds(pl.multiple_of(swapped(device, step) * width, LANES), width)
-        seq_grad = seq_refs[step][:rows]
-        k_slab[step] = seq_grad * value_ref[:, columns]
-        v_slab[step] = seq_grad * key_ref[:, columns]
-        lag_slab[step] = lag_refs[step][-taps:].astype(jnp.float32)
-        for at, (slab, ref) in enumerate(((k_slab, k_ref), (v_slab, v_ref), (lag_slab, filter_ref))):
-            stores.append(pltpu.make_async_copy(slab.at[step], ref.at[:, columns], sems.at[step, at]))
+        results = []
+        if piece.shape[0] >= rows:
+            seq_grad = piece[:rows]
+            k_slab[at] = seq_grad * value_ref[:, columns]
+            v_slab[at] = seq_grad * key_ref[:, columns]
+            results += [(k_slab, k_ref), (v_slab, v_ref)]
+        if piece.shape[0] != rows:
+            lag_slab[at] = piece[-taps:].astype(jnp.float32)
+            results.append((lag_slab, filter_ref))
+        for sem, (slab, ref) in enumerate(results):
+            stores.append(pltpu.make_async_copy(slab.at[at], ref.at[:, columns], sems.at[at, sem]))
             stores[-1].start()
     for copy in stores:
         copy.wait()
 
 
-def finish(received, early, key_rows, value_rows):
-    ranks = len(received)
-    width = received[0].shape[1]
+def finish_some(pieces, key_rows, value_rows, ranks, partial):
+    steps = [step for step, _ in pieces]
     rows, channels = key_rows.shape
+    width = channels // ranks
     taps = LAG_SPANS * SPAN // ranks
-    if width % LANES:
-        order = step_orders(ranks)[2]
-        pieces = [received[order.index(step)] for step in range(ranks)]
-        for step, piece in zip(early_steps(ranks), early):
-            pieces[step] = jnp.concatenate([piece, pieces[step]], 0)
-        slots = swapped(lax.axis_index("ctx"), lax.iota(jnp.int32, ranks))
-        flat = jnp.stack(pieces)[slots].astype(jnp.float32).transpose(1, 0, 2)
-        flat = flat.reshape(rows + taps, channels)
-        seq_grad = flat[:rows]
-        k_grad = (seq_grad * value_rows.astype(jnp.float32)).astype(jnp.bfloat16)
-        v_grad = (seq_grad * key_rows.astype(jnp.float32)).astype(jnp.bfloat16)
-        return k_grad, v_grad, flat[rows:]
     return pl.pallas_call(
-        functools.partial(finish_kernel, ranks=ranks, early=len(early)),
-        in_specs=[pl.BlockSpec(memory_space=pltpu.VMEM)] * (ranks + len(early) + 2),
+        functools.partial(finish_kernel, steps=steps),
+        in_specs=[pl.BlockSpec(memory_space=pltpu.VMEM)] * (len(pieces) + 2)
+        + [pl.BlockSpec(memory_space=pltpu.HBM)] * len(partial),
         out_specs=[pl.BlockSpec(memory_space=pltpu.HBM)] * 3,
         out_shape=[
             jax.ShapeDtypeStruct((rows, channels), jnp.bfloat16),
             jax.ShapeDtypeStruct((rows, channels), jnp.bfloat16),
             jax.ShapeDtypeStruct((taps, channels), jnp.float32),
         ],
-        scratch_shapes=[pltpu.VMEM((ranks, rows, width), jnp.bfloat16)] * 2
-        + [pltpu.VMEM((ranks, taps, width), jnp.float32), pltpu.SemaphoreType.DMA((ranks, 3))],
+        scratch_shapes=[pltpu.VMEM((len(pieces), rows, width), jnp.bfloat16)] * 2
+        + [
+            pltpu.VMEM((len(pieces), taps, width), jnp.float32),
+            pltpu.SemaphoreType.DMA((len(pieces), 3)),
+        ],
+        input_output_aliases={len(pieces) + 2 + at: at for at in range(len(partial))},
         compiler_params=pltpu.CompilerParams(vmem_limit_bytes=VMEM_BYTES),
         cost_estimate=pl.CostEstimate(
-            flops=2 * rows * channels,
-            bytes_accessed=channels * (10 * rows + 6 * taps),
+            flops=2 * rows * width * len(pieces),
+            bytes_accessed=width * len(pieces) * (10 * rows + 6 * taps),
             transcendentals=0,
         ),
-    )(*received, *early, key_rows, value_rows)
+    )(*(piece for _, piece in pieces), key_rows, value_rows, *partial)
+
+
+def finish(returned, early, key_rows, value_rows):
+    ranks = len(returned)
+    width = returned[0].shape[1]
+    rows, channels = key_rows.shape
+    if width % LANES:
+        pieces = [returned[step] for step in range(ranks)]
+        for step, piece in early.items():
+            pieces[step] = jnp.concatenate([piece, pieces[step]], 0)
+        slots = swapped(lax.axis_index("ctx"), lax.iota(jnp.int32, ranks))
+        flat = jnp.stack(pieces)[slots].astype(jnp.float32).transpose(1, 0, 2)
+        flat = flat.reshape(-1, channels)
+        seq_grad = flat[:rows]
+        k_grad = (seq_grad * value_rows.astype(jnp.float32)).astype(jnp.bfloat16)
+        v_grad = (seq_grad * key_rows.astype(jnp.float32)).astype(jnp.bfloat16)
+        return k_grad, v_grad, flat[rows:]
+    order = step_orders(ranks)[2]
+    first = first_steps(ranks)
+    outputs = ()
+    if first:
+        pieces = [(step, returned[step]) for step in order if step in first] + list(early.items())
+        outputs = finish_some(pieces, key_rows, value_rows, ranks, outputs)
+    pieces = [(step, returned[step]) for step in order if step not in first]
+    return finish_some(pieces, key_rows, value_rows, ranks, outputs)
 
 
 def on_device(out_grad, query_rows, key_rows, value_rows, conv_rows, long_filter, block_table):
@@ -375,24 +414,30 @@
         pairs = [(rank, rank ^ step) for rank in range(ranks)]
         return lax.ppermute(piece, "ctx", pairs) if step else piece
 
-    def exchange(pieces, message):
-        return [swap(pieces[step], step) for step in step_orders(ranks)[message]]
-
-    weighted = exchange(prepare((out_grad, query_rows, long_filter), ranks), 0)
-    product = exchange(prepare((key_rows, value_rows), ranks, weighted[:1]), 1)
+    def exchange(pieces):
+        return {step: swap(piece, step) for step, piece in pieces.items()}
+
+    def ordered(pieces, message):
+        return [pieces[step] for step in step_orders(ranks)[message]]
+
+    joint = joint_steps(ranks)
+    pieces = prepare((out_grad, query_rows, long_filter), ranks)
+    weighted = exchange({step: pieces[step] for step in range(ranks) if step not in joint})
+    pieces = prepare((key_rows, value_rows), ranks, {step: pieces[step] for step in joint})
+    product = exchange(dict(enumerate(pieces)))
+    weighted |= {step: product[step] for step in joint}
     q_grad = (out_grad.astype(jnp.float32) * conv_rows.astype(jnp.float32)).astype(jnp.bfloat16)
-    seq_grad, spectrum, *early = weighted_part(weighted, constants)
+    seq_grad, spectrum, *early = weighted_part(ordered(weighted, 0), constants)
     early = [swap(piece, step) for step, piece in zip(early_steps(ranks), early)]
-    pieces = list(product_part(product, seq_grad, spectrum, constants))
-    order = step_orders(ranks)[2]
+    pieces = product_part(ordered(product, 1), seq_grad, spectrum, constants)
+    pieces = list(pieces)
     returned = {step + ranks: piece for step, piece in zip(early_steps(ranks), early)}
-    for step in order:
+    for step in step_orders(ranks)[2]:
         ahead = starts_after(ranks).get(step)
         if ahead is not None:
             pieces[step], returned[ahead] = lax.optimization_barrier((pieces[step], returned[ahead]))
         returned[step] = swap(pieces[step], step)
-    early = [returned[step + ranks] for step in early_steps(ranks)]
-    returned = [returned[step] for step in order]
+    early = {step: returned.pop(step + ranks) for step in early_steps(ranks)}
     return (q_grad, *finish(returned, early, key_rows, value_rows))
 
 

time: 56.6 us -> 55.7 us (0.984)
  starting transfers between devices: 27.8 us -> 22.6 us
  waiting for transfers between devices: 12.7 us -> 16.2 us
  Pallas kernels: 13.7 us -> 14.4 us
    ppermute x23 -> x20, starting transfers between devices: 27.8 us -> 22.6 us  [swap(): return lax.ppermute(piece, 'ctx', pairs) if step else piece]
    ppermute x23 -> x20, waiting for transfers between devices: 12.7 us -> 16.2 us  [swap(): return lax.ppermute(piece, 'ctx', pairs) if step else piece]
    pallas_call x1 -> x2, Pallas kernels: 1.81 us -> 2.53 us  [finish_some(): pl.pallas_call(functools.partial(finish_kernel, steps=steps), in_specs=[p...]
  transfers between devices with their start and end apart: 23 -> 20, of which waited for: 9 -> 7; matrix products, arithmetic and copies ran while one was open for 2% -> 2% of each run, Pallas kernels for 18% -> 20%
where the time goes in v2:
time: 55.7 us; the launch traced here: 55.4 us
  starting transfers between devices  22.6 us (41%)
  waiting for transfers between devices  16.2 us (29%)
  Pallas kernels  14.4 us (26%)
  other arithmetic  1.37 us (2%)
  between operations  0.79 us (1%)
    ppermute x20, starting transfers between devices, swap(): return lax.ppermute(piece, 'ctx', pairs) if step else piece  22.6 us
    ppermute x20, waiting for transfers between devices, swap(): return lax.ppermute(piece, 'ctx', pairs) if step else piece  16.2 us
    pallas_call x2, Pallas kernels, spectral_call(): pl.pallas_call(kernel, in_specs=[pl.BlockSpec(memory_space=pltpu.SMEM)] +...  8.19 us
    pallas_call x2, Pallas kernels, prepare(): pl.pallas_call(functools.partial(prepare_kernel, ranks=ranks, count=len(a...  3.72 us
    pallas_call x2, Pallas kernels, finish_some(): pl.pallas_call(functools.partial(finish_kernel, steps=steps), in_specs=[p...  2.53 us
    convert_element_type x1, other arithmetic, on_device(): (out_grad.astype(jnp.float32) * conv_rows.astype(jnp.float32)).astype(jnp...  1.37 us
  transfers between devices with their start and end apart: 20, of which 7 were waited for; matrix products, arithmetic and copies ran while one was open for 2% of the time, Pallas kernels for 20%

profile of v2, /device:TPU:0, one launch (start us, length us, event | category | flops | bytes accessed | tf_op | source)
XLA Modules:
  0.0 55.4 jit_solution(12191369373842331611)
XLA Ops:
  0.6 0.0 copy-start.2
  0.6 0.0 copy-start.3
  0.7 0.0 copy-start.4
  0.7 2.0 %shard_map.120 = (bf16[352,256]{1,0:T(8,128)(2,1)S(1)}, bf16[352,256]{1,0:T(8,128)(2,1)S(1)}, bf16[352,256]{1,0:T(8,128)(2,1)S(1)}, bf16[352,256]{1,0:T(8,128)(2...) custom-call(bf16[256,2048]{1,0:T(8,128)(2,1)} %refs_0_.2, ...), custom_call_target="tpu_custom_call" | custom-call | flops 524288 | bytes 5767168 | tf_op jit(solution)/shard_map/pallas_call | solution.py:106
  2.7 3.0 %collective-permute-start = (bf16[352,256]{1,0:T(8,128)(2,1)S(1)}, bf16[352,256]{1,0:T(8,128)(2,1)S(1)}, u32[]{:S(2)}, u32[]{:S(2)}) collective-permute-start(bf16[352,256]{1,0:T(8,128)(2,1)S(1)} %get-tuple-element.48), channel_id=1, source_target_pairs={{0,16},{4,20},{8,24},{12,28},{16,0},{20,4},{24,8},{28,12},{1,17},{... | collective-permute-start | bytes 540680 | tf_op jit(solution)/shard_map/ppermute | solution.py:415
  5.7 1.5 %collective-permute-start.1 = (bf16[352,256]{1,0:T(8,128)(2,1)S(1)}, bf16[352,256]{1,0:T(8,128)(2,1)S(1)}, u32[]{:S(2)}, u32[]{:S(2)}) collective-permute-start(bf16[352,256]{1,0:T(8,128)(2,1)S(1)} %get-tuple-element.49), channel_id=1, source_target_pairs={{0,8},{4,12},{8,0},{12,4},{16,24},{20,28},{24,16},{28,20},{1,9},{5... | collective-permute-start | bytes 540680 | tf_op jit(solution)/shard_map/ppermute | solution.py:415
  7.2 1.7 %shard_map.121 = (bf16[256,256]{1,0:T(8,128)(2,1)S(1)}, bf16[608,256]{1,0:T(8,128)(2,1)S(1)}, bf16[256,256]{1,0:T(8,128)(2,1)S(1)}, bf16[608,256]{1,0:T(8,128)(2...) custom-call(bf16[256,2048]{1,0:T(8,128)(2,1)} %refs_5_.3, ...), custom_call_target="tpu_custom_call" | custom-call | flops 524288 | bytes 4194304 | tf_op jit(solution)/shard_map/pallas_call | solution.py:106
  8.9 0.1 collective-permute-start.4
  9.0 0.3 collective-permute-start.5
  9.3 0.4 collective-permute-start.6
  9.7 0.6 %collective-permute-done.refs_0_ = bf16[352,256]{1,0:T(8,128)(2,1)S(1)} collective-permute-done((bf16[352,256]{1,0:T(8,128)(2,1)S(1)}, bf16[352,256]{1,0:T(8,128)(2,1)S(1)}, u32[]{:S(2)}, u32[]{:S(2)}) %collective-permute-start) | collective-permute-done | bytes 180256 | tf_op jit(solution)/shard_map/ppermute | solution.py:415
  10.3 3.5 %collective-permute-start.2 = (bf16[352,256]{1,0:T(8,128)(2,1)S(1)}, bf16[352,256]{1,0:T(8,128)(2,1)S(1)}, u32[]{:S(2)}, u32[]{:S(2)}) collective-permute-start(bf16[352,256]{1,0:T(8,128)(2,1)S(1)} %get-tuple-element.50), channel_id=1, source_target_pairs={{0,24},{4,28},{8,16},{12,20},{16,8},{20,12},{24,0},{28,4},{1,25},{... | collective-permute-start | bytes 540680 | tf_op jit(solution)/shard_map/ppermute | solution.py:415
  13.8 0.0 collective-permute-done.1.refs_1_
  13.8 0.0 collective-permute-start.3
  13.8 10.5 %collective-permute-done.2.refs_2_ = bf16[352,256]{1,0:T(8,128)(2,1)S(1)} collective-permute-done((bf16[352,256]{1,0:T(8,128)(2,1)S(1)}, bf16[352,256]{1,0:T(8,128)(2,1)S(1)}, u32[]{:S(2)}, u32[]{:S(2)}) %collective-permute-start.2) | collective-permute-done | bytes 180256 | tf_op jit(solution)/shard_map/ppermute | solution.py:415
  24.3 0.0 collective-permute-start.10
  24.3 0.9 %collective-permute-done.3.refs_3_ = bf16[352,256]{1,0:T(8,128)(2,1)S(1)} collective-permute-done((bf16[352,256]{1,0:T(8,128)(2,1)S(1)}, bf16[352,256]{1,0:T(8,128)(2,1)S(1)}, u32[]{:S(2)}, u32[]{:S(2)}) %collective-permute-start.3) | collective-permute-done | bytes 180256 | tf_op jit(solution)/shard_map/ppermute | solution.py:415
  25.3 2.0 %collective-permute-start.7 = (bf16[256,256]{1,0:T(8,128)(2,1)S(1)}, bf16[256,256]{1,0:T(8,128)(2,1)S(1)}, u32[]{:S(2)}, u32[]{:S(2)}) collective-permute-start(bf16[256,256]{1,0:T(8,128)(2,1)S(1)} %get-tuple-element.61), channel_id=1, source_target_pairs={{0,16},{4,20},{8,24},{12,28},{16,0},{20,4},{24,8},{28,12},{1,17},{... | collective-permute-start | bytes 393224 | tf_op jit(solution)/shard_map/ppermute | solution.py:415
  27.2 0.0 collective-permute-done.4.refs_4_.refs_0_
  27.2 1.3 %collective-permute-start.8 = (bf16[256,256]{1,0:T(8,128)(2,1)S(1)}, bf16[256,256]{1,0:T(8,128)(2,1)S(1)}, u32[]{:S(2)}, u32[]{:S(2)}) collective-permute-start(bf16[256,256]{1,0:T(8,128)(2,1)S(1)} %get-tuple-element.62), channel_id=1, source_target_pairs={{0,8},{4,12},{8,0},{12,4},{16,24},{20,28},{24,16},{28,20},{1,9},{5... | collective-permute-start | bytes 393224 | tf_op jit(solution)/shard_map/ppermute | solution.py:415
  28.5 0.0 collective-permute-done.5.refs_5_.refs_1_
  28.5 0.2 collective-permute-start.9
  28.8 0.0 collective-permute-done.6.refs_6_.refs_2_
  28.8 0.0 copy-done.2
  28.8 0.0 copy-done.3
  28.8 0.0 copy-done.4
  28.8 4.1 %shard_map.122 = (bf16[8,256,256]{2,1,0:T(8,128)(2,1)S(1)}, f32[8,512,256]{2,1,0:T(8,128)S(1)}, bf16[256,256]{1,0:T(8,128)(2,1)S(1)}, bf16[256,256]{1,0:T(8,128)(2,1)S(1)}) custom-call(s32[16]{0:T(128)S(1)} %copy-done.4, bf16[512,256]{1,0:T(8,128)(2,1)S(1)} %copy-done.2, bf16[256,512]{1,0:T(8,128)(2,1)S(1)} %copy-done.3, ...), custom_call_target="tpu_custom_call" | custom-call | flops 1275068416 | bytes 7864384 | tf_op jit(solution)/shard_map/pallas_call | solution.py:270
  32.9 2.0 %collective-permute-start.13 = (bf16[256,256]{1,0:T(8,128)(2,1)S(1)}, bf16[256,256]{1,0:T(8,128)(2,1)S(1)}, u32[]{:S(2)}, u32[]{:S(2)}) collective-permute-start(bf16[256,256]{1,0:T(8,128)(2,1)S(1)} %get-tuple-element.70), channel_id=1, source_target_pairs={{0,28},{4,24},{8,20},{12,16},{16,12},{20,8},{24,4},{28,0},{1,29},{... | collective-permute-start | bytes 393224 | tf_op jit(solution)/shard_map/ppermute | solution.py:415
  34.9 0.0 collective-permute-done.10.refs_6_
  34.9 1.1 %collective-permute-start.18 = (bf16[256,256]{1,0:T(8,128)(2,1)S(1)}, bf16[256,256]{1,0:T(8,128)(2,1)S(1)}, u32[]{:S(2)}, u32[]{:S(2)}) collective-permute-start(bf16[256,256]{1,0:T(8,128)(2,1)S(1)} %get-tuple-element.80), channel_id=1, source_target_pairs={{0,24},{4,28},{8,16},{12,20},{16,8},{20,12},{24,0},{28,4},{1,25},{... | collective-permute-start | bytes 393224 | tf_op jit(solution)/shard_map/ppermute | solution.py:415
  36.0 0.0 collective-permute-done.7.refs_3_
  36.0 0.0 collective-permute-done.8.refs_4_
  36.0 0.0 collective-permute-done.9.refs_5_
  36.0 0.0 copy-start.5
  36.0 0.0 copy-start.6
  36.0 4.1 %shard_map.123 = (bf16[352,256]{1,0:T(8,128)(2,1)S(1)}, bf16[352,256]{1,0:T(8,128)(2,1)S(1)}, bf16[352,256]{1,0:T(8,128)(2,1)S(1)}, bf16[352,256]{1,0:T(8,128)(2...) custom-call(s32[16]{0:T(128)S(1)} %copy-done.4, ...), custom_call_target="tpu_custom_call" | custom-call | flops 738197504 | bytes 8536128 | tf_op jit(solution)/shard_map/pallas_call | solution.py:270
  40.1 0.0 copy-start
  40.1 0.0 copy-start.1
  40.1 0.0 collective-permute-done.13.refs_4_
  40.1 1.4 %collective-permute-start.14 = (bf16[352,256]{1,0:T(8,128)(2,1)S(1)}, bf16[352,256]{1,0:T(8,128)(2,1)S(1)}, u32[]{:S(2)}, u32[]{:S(2)}) collective-permute-start(bf16[352,256]{1,0:T(8,128)(2,1)S(1)} %get-tuple-element.71), channel_id=1, source_target_pairs={{0,8},{4,12},{8,0},{12,4},{16,24},{20,28},{24,16},{28,20},{1,9},{5... | collective-permute-start | bytes 540680 | tf_op jit(solution)/shard_map/ppermute | solution.py:415
  41.5 1.0 %collective-permute-done.18.refs_3_ = bf16[256,256]{1,0:T(8,128)(2,1)S(1)} collective-permute-done((bf16[256,256]{1,0:T(8,128)(2,1)S(1)}, bf16[256,256]{1,0:T(8,128)(2,1)S(1)}, u32[]{:S(2)}, u32[]{:S(2)}) %collective-permute-start.18) | collective-permute-done | bytes 131104 | tf_op jit(solution)/shard_map/ppermute | solution.py:415
  42.5 1.7 %collective-permute-start.19 = (bf16[352,256]{1,0:T(8,128)(2,1)S(1)}, bf16[352,256]{1,0:T(8,128)(2,1)S(1)}, u32[]{:S(2)}, u32[]{:S(2)}) collective-permute-start(bf16[352,256]{1,0:T(8,128)(2,1)S(1)} %get-tuple-element.81), channel_id=1, source_target_pairs={{0,16},{4,20},{8,24},{12,28},{16,0},{20,4},{24,8},{28,12},{1,17},{... | collective-permute-start | bytes 540680 | tf_op jit(solution)/shard_map/ppermute | solution.py:415
  44.1 0.0 collective-permute-start.11
  44.1 1.8 %collective-permute-start.12 = (bf16[352,256]{1,0:T(8,128)(2,1)S(1)}, bf16[352,256]{1,0:T(8,128)(2,1)S(1)}, u32[]{:S(2)}, u32[]{:S(2)}) collective-permute-start(bf16[352,256]{1,0:T(8,128)(2,1)S(1)} %get-tuple-element.67), channel_id=1, source_target_pairs={{0,12},{4,8},{8,4},{12,0},{16,28},{20,24},{24,20},{28,16},{1,13},{... | collective-permute-start | bytes 540680 | tf_op jit(solution)/shard_map/ppermute | solution.py:415
  45.9 0.8 %collective-permute-done.14.refs_1_ = bf16[352,256]{1,0:T(8,128)(2,1)S(1)} collective-permute-done((bf16[352,256]{1,0:T(8,128)(2,1)S(1)}, bf16[352,256]{1,0:T(8,128)(2,1)S(1)}, u32[]{:S(2)}, u32[]{:S(2)}) %collective-permute-start.14) | collective-permute-done | bytes 180256 | tf_op jit(solution)/shard_map/ppermute | solution.py:415
  46.7 1.5 %collective-permute-start.17 = (bf16[96,256]{1,0:T(8,128)(2,1)S(1)}, bf16[96,256]{1,0:T(8,128)(2,1)S(1)}, u32[]{:S(2)}, u32[]{:S(2)}) collective-permute-start(bf16[96,256]{1,0:T(8,128)(2,1)S(1)} %get-tuple-element.78), channel_id=1, source_target_pairs={{0,28},{4,24},{8,20},{12,16},{16,12},{20,8},{24,4},{28,0},{1,29},{... | collective-permute-start | bytes 147464 | tf_op jit(solution)/shard_map/ppermute | solution.py:415
  48.2 1.0 %collective-permute-start.16 = (bf16[96,256]{1,0:T(8,128)(2,1)S(1)}, bf16[96,256]{1,0:T(8,128)(2,1)S(1)}, u32[]{:S(2)}, u32[]{:S(2)}) collective-permute-start(bf16[96,256]{1,0:T(8,128)(2,1)S(1)} %get-tuple-element.75), channel_id=1, source_target_pairs={{0,24},{4,28},{8,16},{12,20},{16,8},{20,12},{24,0},{28,4},{1,25},{... | collective-permute-start | bytes 147464 | tf_op jit(solution)/shard_map/ppermute | solution.py:415
  49.1 0.8 %collective-permute-done.19.refs_0_ = bf16[352,256]{1,0:T(8,128)(2,1)S(1)} collective-permute-done((bf16[352,256]{1,0:T(8,128)(2,1)S(1)}, bf16[352,256]{1,0:T(8,128)(2,1)S(1)}, u32[]{:S(2)}, u32[]{:S(2)}) %collective-permute-start.19) | collective-permute-done | bytes 180256 | tf_op jit(solution)/shard_map/ppermute | solution.py:415
  49.9 0.0 collective-permute-start.15
  49.9 0.0 copy-done.5
  49.9 0.0 copy-done.6
  49.9 1.4 %multiply_convert_fusion = bf16[256,2048]{1,0:T(8,128)(2,1)} fusion(bf16[256,2048]{1,0:T(8,128)(2,1)S(1)} %copy-done.6, bf16[256,2048]{1,0:T(8,128)(2,1)S(1)} %copy-done.5), kind=kLoop, calls=%fused_computation | loop fusion | flops 2097152 | bytes 3145728 | tf_op jit(solution)/shard_map/convert_element_type | solution.py:429
  51.3 0.0 copy-done
  51.3 0.0 copy-done.1
  51.3 1.3 %shard_map.124 = (bf16[256,2048]{1,0:T(8,128)(2,1)}, bf16[256,2048]{1,0:T(8,128)(2,1)}, f32[96,2048]{1,0:T(8,128)}) custom-call(bf16[352,256]{1,0:T(8,128)(2,1)S(1)} %collective-permute-done.19.refs_0_, bf16[352,256]{1,0:T(8,128)(2,1)S(1)} %collective-permute-done.14.refs_1_, bf16[352,256]{1,0:T(8,128)(2,1)S(1)} %get-tuple-element.83.refs_2_, ...), custom_call_target="tpu_custom_call" | custom-call | flops 655360 | bytes 4014080 | tf_op jit(solution)/shard_map/pallas_call | solution.py:359
  52.6 1.6 %collective-permute-done.11.refs_0_ = bf16[352,256]{1,0:T(8,128)(2,1)S(1)} collective-permute-done((bf16[352,256]{1,0:T(8,128)(2,1)S(1)}, bf16[352,256]{1,0:T(8,128)(2,1)S(1)}, u32[]{:S(2)}, u32[]{:S(2)}) %collective-permute-start.11) | collective-permute-done | bytes 180256 | tf_op jit(solution)/shard_map/ppermute | solution.py:415
  54.2 0.0 collective-permute-done.12.refs_1_
  54.2 0.0 collective-permute-done.17.refs_4_
  54.2 0.0 collective-permute-done.16.refs_3_
  54.2 0.0 collective-permute-done.15.refs_2_
  54.2 1.2 %shard_map.125 = (bf16[256,2048]{1,0:T(8,128)(2,1)}, bf16[256,2048]{1,0:T(8,128)(2,1)}, f32[96,2048]{1,0:T(8,128)}) custom-call(bf16[352,256]{1,0:T(8,128)(2,1)S(1)} %collective-permute-done.11.refs_0_, bf16[352,256]{1,0:T(8,128)(2,1)S(1)} %collective-permute-done.12.refs_1_, ...), custom_call_target="tpu_custom_call", output_to_operand_aliasing={{0}: (7, {}), {1}: (8, {}), {2}: (9, {})} | custom-call | flops 655360 | bytes 4014080 | tf_op jit(solution)/shard_map/pallas_call | solution.py:359
Async XLA Ops:
  0.6 28.1 %copy-start.2 = (bf16[512,256]{1,0:T(8,128)(2,1)S(1)}, bf16[512,256]{1,0:T(8,128)(2,1)}, u32[]{:S(2)}) copy-start(bf16[512,256]{1,0:T(8,128)(2,1)} %constant.4.clone.forward_ref) | copy-start | bytes 786436
  0.6 28.1 %copy-start.3 = (bf16[256,512]{1,0:T(8,128)(2,1)S(1)}, bf16[256,512]{1,0:T(8,128)(2,1)}, u32[]{:S(2)}) copy-start(bf16[256,512]{1,0:T(8,128)(2,1)} %constant.5.clone.inverse_ref) | copy-start | bytes 786436
  0.7 28.1 %copy-start.4 = (s32[16]{0:T(128)S(1)}, s32[16]{0:T(128)}, u32[]{:S(2)}) copy-start(s32[16]{0:T(128)} %table_ref.3) | copy-start | bytes 196
  2.7 7.6 %collective-permute-start = (bf16[352,256]{1,0:T(8,128)(2,1)S(1)}, bf16[352,256]{1,0:T(8,128)(2,1)S(1)}, u32[]{:S(2)}, u32[]{:S(2)}) collective-permute-start(bf16[352,256]{1,0:T(8,128)(2,1)S(1)} %get-tuple-element.48), channel_id=1, source_target_pairs={{0,16},{4,20},{8,24},{12,28},{16,0},{20,4},{24,8},{28,12},{1,17},{... | collective-permute-start | bytes 540680 | tf_op jit(solution)/shard_map/ppermute | solution.py:415
  5.7 8.1 %collective-permute-start.1 = (bf16[352,256]{1,0:T(8,128)(2,1)S(1)}, bf16[352,256]{1,0:T(8,128)(2,1)S(1)}, u32[]{:S(2)}, u32[]{:S(2)}) collective-permute-start(bf16[352,256]{1,0:T(8,128)(2,1)S(1)} %get-tuple-element.49), channel_id=1, source_target_pairs={{0,8},{4,12},{8,0},{12,4},{16,24},{20,28},{24,16},{28,20},{1,9},{5... | collective-permute-start | bytes 540680 | tf_op jit(solution)/shard_map/ppermute | solution.py:415
  8.9 18.3 %collective-permute-start.4 = (bf16[608,256]{1,0:T(8,128)(2,1)S(1)}, bf16[608,256]{1,0:T(8,128)(2,1)S(1)}, u32[]{:S(2)}, u32[]{:S(2)}) collective-permute-start(bf16[608,256]{1,0:T(8,128)(2,1)S(1)} %get-tuple-element.55), channel_id=1, source_target_pairs={{0,20},{4,16},{8,28},{12,24},{16,4},{20,0},{24,12},{28,8},{1,21},{... | collective-permute-start | bytes 933896 | tf_op jit(solution)/shard_map/ppermute | solution.py:415
  9.0 19.5 %collective-permute-start.5 = (bf16[608,256]{1,0:T(8,128)(2,1)S(1)}, bf16[608,256]{1,0:T(8,128)(2,1)S(1)}, u32[]{:S(2)}, u32[]{:S(2)}) collective-permute-start(bf16[608,256]{1,0:T(8,128)(2,1)S(1)} %get-tuple-element.56), channel_id=1, source_target_pairs={{0,12},{4,8},{8,4},{12,0},{16,28},{20,24},{24,20},{28,16},{1,13},{... | collective-permute-start | bytes 933896 | tf_op jit(solution)/shard_map/ppermute | solution.py:415
  9.3 19.4 %collective-permute-start.6 = (bf16[608,256]{1,0:T(8,128)(2,1)S(1)}, bf16[608,256]{1,0:T(8,128)(2,1)S(1)}, u32[]{:S(2)}, u32[]{:S(2)}) collective-permute-start(bf16[608,256]{1,0:T(8,128)(2,1)S(1)} %get-tuple-element.57), channel_id=1, source_target_pairs={{0,4},{4,0},{8,12},{12,8},{16,20},{20,16},{24,28},{28,24},{1,5},{5... | collective-permute-start | bytes 933896 | tf_op jit(solution)/shard_map/ppermute | solution.py:415
  10.3 14.0 %collective-permute-start.2 = (bf16[352,256]{1,0:T(8,128)(2,1)S(1)}, bf16[352,256]{1,0:T(8,128)(2,1)S(1)}, u32[]{:S(2)}, u32[]{:S(2)}) collective-permute-start(bf16[352,256]{1,0:T(8,128)(2,1)S(1)} %get-tuple-element.50), channel_id=1, source_target_pairs={{0,24},{4,28},{8,16},{12,20},{16,8},{20,12},{24,0},{28,4},{1,25},{... | collective-permute-start | bytes 540680 | tf_op jit(solution)/shard_map/ppermute | solution.py:415
  13.8 11.5 %collective-permute-start.3 = (bf16[352,256]{1,0:T(8,128)(2,1)S(1)}, bf16[352,256]{1,0:T(8,128)(2,1)S(1)}, u32[]{:S(2)}, u32[]{:S(2)}) collective-permute-start(bf16[352,256]{1,0:T(8,128)(2,1)S(1)} %get-tuple-element.51), channel_id=1, source_target_pairs={{0,28},{4,24},{8,20},{12,16},{16,12},{20,8},{24,4},{28,0},{1,29},{... | collective-permute-start | bytes 540680 | tf_op jit(solution)/shard_map/ppermute | solution.py:415
  24.3 10.5 %collective-permute-start.10 = (bf16[256,256]{1,0:T(8,128)(2,1)S(1)}, bf16[256,256]{1,0:T(8,128)(2,1)S(1)}, u32[]{:S(2)}, u32[]{:S(2)}) collective-permute-start(bf16[256,256]{1,0:T(8,128)(2,1)S(1)} %get-tuple-element.64), channel_id=1, source_target_pairs={{0,28},{4,24},{8,20},{12,16},{16,12},{20,8},{24,4},{28,0},{1,29},{... | collective-permute-start | bytes 393224 | tf_op jit(solution)/shard_map/ppermute | solution.py:415
  25.3 10.7 %collective-permute-start.7 = (bf16[256,256]{1,0:T(8,128)(2,1)S(1)}, bf16[256,256]{1,0:T(8,128)(2,1)S(1)}, u32[]{:S(2)}, u32[]{:S(2)}) collective-permute-start(bf16[256,256]{1,0:T(8,128)(2,1)S(1)} %get-tuple-element.61), channel_id=1, source_target_pairs={{0,16},{4,20},{8,24},{12,28},{16,0},{20,4},{24,8},{28,12},{1,17},{... | collective-permute-start | bytes 393224 | tf_op jit(solution)/shard_map/ppermute | solution.py:415
  27.2 8.7 %collective-permute-start.8 = (bf16[256,256]{1,0:T(8,128)(2,1)S(1)}, bf16[256,256]{1,0:T(8,128)(2,1)S(1)}, u32[]{:S(2)}, u32[]{:S(2)}) collective-permute-start(bf16[256,256]{1,0:T(8,128)(2,1)S(1)} %get-tuple-element.62), channel_id=1, source_target_pairs={{0,8},{4,12},{8,0},{12,4},{16,24},{20,28},{24,16},{28,20},{1,9},{5... | collective-permute-start | bytes 393224 | tf_op jit(solution)/shard_map/ppermute | solution.py:415
  28.5 7.4 %collective-permute-start.9 = (bf16[256,256]{1,0:T(8,128)(2,1)S(1)}, bf16[256,256]{1,0:T(8,128)(2,1)S(1)}, u32[]{:S(2)}, u32[]{:S(2)}) collective-permute-start(bf16[256,256]{1,0:T(8,128)(2,1)S(1)} %get-tuple-element.63), channel_id=1, source_target_pairs={{0,24},{4,28},{8,16},{12,20},{16,8},{20,12},{24,0},{28,4},{1,25},{... | collective-permute-start | bytes 393224 | tf_op jit(solution)/shard_map/ppermute | solution.py:415
  32.9 7.2 %collective-permute-start.13 = (bf16[256,256]{1,0:T(8,128)(2,1)S(1)}, bf16[256,256]{1,0:T(8,128)(2,1)S(1)}, u32[]{:S(2)}, u32[]{:S(2)}) collective-permute-start(bf16[256,256]{1,0:T(8,128)(2,1)S(1)} %get-tuple-element.70), channel_id=1, source_target_pairs={{0,28},{4,24},{8,20},{12,16},{16,12},{20,8},{24,4},{28,0},{1,29},{... | collective-permute-start | bytes 393224 | tf_op jit(solution)/shard_map/ppermute | solution.py:415
  34.9 7.6 %collective-permute-start.18 = (bf16[256,256]{1,0:T(8,128)(2,1)S(1)}, bf16[256,256]{1,0:T(8,128)(2,1)S(1)}, u32[]{:S(2)}, u32[]{:S(2)}) collective-permute-start(bf16[256,256]{1,0:T(8,128)(2,1)S(1)} %get-tuple-element.80), channel_id=1, source_target_pairs={{0,24},{4,28},{8,16},{12,20},{16,8},{20,12},{24,0},{28,4},{1,25},{... | collective-permute-start | bytes 393224 | tf_op jit(solution)/shard_map/ppermute | solution.py:415
  36.0 13.9 %copy-start.5 = (bf16[256,2048]{1,0:T(8,128)(2,1)S(1)}, bf16[256,2048]{1,0:T(8,128)(2,1)}, u32[]{:S(2)}) copy-start(bf16[256,2048]{1,0:T(8,128)(2,1)} %refs_0_.2) | copy-start | bytes 3145732
  36.0 13.9 %copy-start.6 = (bf16[256,2048]{1,0:T(8,128)(2,1)S(1)}, bf16[256,2048]{1,0:T(8,128)(2,1)}, u32[]{:S(2)}) copy-start(bf16[256,2048]{1,0:T(8,128)(2,1)} %param.13) | copy-start | bytes 3145732
  40.1 11.2 %copy-start = (bf16[256,2048]{1,0:T(8,128)(2,1)S(1)}, bf16[256,2048]{1,0:T(8,128)(2,1)}, u32[]{:S(2)}) copy-start(bf16[256,2048]{1,0:T(8,128)(2,1)} %refs_5_.3) | copy-start | bytes 3145732
  40.1 11.2 %copy-start.1 = (bf16[256,2048]{1,0:T(8,128)(2,1)S(1)}, bf16[256,2048]{1,0:T(8,128)(2,1)}, u32[]{:S(2)}) copy-start(bf16[256,2048]{1,0:T(8,128)(2,1)} %refs_6_.3) | copy-start | bytes 3145732
  40.1 6.6 %collective-permute-start.14 = (bf16[352,256]{1,0:T(8,128)(2,1)S(1)}, bf16[352,256]{1,0:T(8,128)(2,1)S(1)}, u32[]{:S(2)}, u32[]{:S(2)}) collective-permute-start(bf16[352,256]{1,0:T(8,128)(2,1)S(1)} %get-tuple-element.71), channel_id=1, source_target_pairs={{0,8},{4,12},{8,0},{12,4},{16,24},{20,28},{24,16},{28,20},{1,9},{5... | collective-permute-start | bytes 540680 | tf_op jit(solution)/shard_map/ppermute | solution.py:415
  42.5 7.4 %collective-permute-start.19 = (bf16[352,256]{1,0:T(8,128)(2,1)S(1)}, bf16[352,256]{1,0:T(8,128)(2,1)S(1)}, u32[]{:S(2)}, u32[]{:S(2)}) collective-permute-start(bf16[352,256]{1,0:T(8,128)(2,1)S(1)} %get-tuple-element.81), channel_id=1, source_target_pairs={{0,16},{4,20},{8,24},{12,28},{16,0},{20,4},{24,8},{28,12},{1,17},{... | collective-permute-start | bytes 540680 | tf_op jit(solution)/shard_map/ppermute | solution.py:415
  44.1 10.1 %collective-permute-start.11 = (bf16[352,256]{1,0:T(8,128)(2,1)S(1)}, bf16[352,256]{1,0:T(8,128)(2,1)S(1)}, u32[]{:S(2)}, u32[]{:S(2)}) collective-permute-start(bf16[352,256]{1,0:T(8,128)(2,1)S(1)} %get-tuple-element.66), channel_id=1, source_target_pairs={{0,20},{4,16},{8,28},{12,24},{16,4},{20,0},{24,12},{28,8},{1,21},{... | collective-permute-start | bytes 540680 | tf_op jit(solution)/shard_map/ppermute | solution.py:415
  44.1 10.1 %collective-permute-start.12 = (bf16[352,256]{1,0:T(8,128)(2,1)S(1)}, bf16[352,256]{1,0:T(8,128)(2,1)S(1)}, u32[]{:S(2)}, u32[]{:S(2)}) collective-permute-start(bf16[352,256]{1,0:T(8,128)(2,1)S(1)} %get-tuple-element.67), channel_id=1, source_target_pairs={{0,12},{4,8},{8,4},{12,0},{16,28},{20,24},{24,20},{28,16},{1,13},{... | collective-permute-start | bytes 540680 | tf_op jit(solution)/shard_map/ppermute | solution.py:415
  46.7 7.5 %collective-permute-start.17 = (bf16[96,256]{1,0:T(8,128)(2,1)S(1)}, bf16[96,256]{1,0:T(8,128)(2,1)S(1)}, u32[]{:S(2)}, u32[]{:S(2)}) collective-permute-start(bf16[96,256]{1,0:T(8,128)(2,1)S(1)} %get-tuple-element.78), channel_id=1, source_target_pairs={{0,28},{4,24},{8,20},{12,16},{16,12},{20,8},{24,4},{28,0},{1,29},{... | collective-permute-start | bytes 147464 | tf_op jit(solution)/shard_map/ppermute | solution.py:415
  48.2 6.0 %collective-permute-start.16 = (bf16[96,256]{1,0:T(8,128)(2,1)S(1)}, bf16[96,256]{1,0:T(8,128)(2,1)S(1)}, u32[]{:S(2)}, u32[]{:S(2)}) collective-permute-start(bf16[96,256]{1,0:T(8,128)(2,1)S(1)} %get-tuple-element.75), channel_id=1, source_target_pairs={{0,24},{4,28},{8,16},{12,20},{16,8},{20,12},{24,0},{28,4},{1,25},{... | collective-permute-start | bytes 147464 | tf_op jit(solution)/shard_map/ppermute | solution.py:415
  49.9 4.3 %collective-permute-start.15 = (bf16[352,256]{1,0:T(8,128)(2,1)S(1)}, bf16[352,256]{1,0:T(8,128)(2,1)S(1)}, u32[]{:S(2)}, u32[]{:S(2)}) collective-permute-start(bf16[352,256]{1,0:T(8,128)(2,1)S(1)} %get-tuple-element.72), channel_id=1, source_target_pairs={{0,4},{4,0},{8,12},{12,8},{16,20},{20,16},{24,28},{28,24},{1,5},{5... | collective-permute-start | bytes 540680 | tf_op jit(solution)/shard_map/ppermute | solution.py:415

commit v3 on v2

--- a/solution.py
+++ b/solution.py
@@ -15,6 +15,7 @@
 SPAN = 2 * BLOCK
 LAG_SPANS = LAG_BLOCKS * BLOCK // SPAN
 LANES = 128
+JOINT_AHEAD = {6: 1}
 VMEM_BYTES = 32 * 2**20
 
 
@@ -421,11 +422,18 @@
         return [pieces[step] for step in step_orders(ranks)[message]]
 
     joint = joint_steps(ranks)
-    pieces = prepare((out_grad, query_rows, long_filter), ranks)
-    weighted = exchange({step: pieces[step] for step in range(ranks) if step not in joint})
-    pieces = prepare((key_rows, value_rows), ranks, {step: pieces[step] for step in joint})
-    product = exchange(dict(enumerate(pieces)))
-    weighted |= {step: product[step] for step in joint}
+    pieces = list(prepare((out_grad, query_rows, long_filter), ranks))
+    below = list(prepare((key_rows, value_rows), ranks, {step: pieces[step] for step in joint}))
+    weighted = {step: swap(below[step], step) for step in joint}
+    product = dict(weighted)
+    for step in range(ranks):
+        if step not in joint:
+            weighted[step] = swap(pieces[step], step)
+            ahead = JOINT_AHEAD.get(step) if joint else None
+            if ahead is not None:
+                below[step], product[ahead] = lax.optimization_barrier((below[step], product[ahead]))
+                weighted[ahead] = product[ahead]
+            product[step] = swap(below[step], step)
     q_grad = (out_grad.astype(jnp.float32) * conv_rows.astype(jnp.float32)).astype(jnp.bfloat16)
     seq_grad, spectrum, *early = weighted_part(ordered(weighted, 0), constants)
     early = [swap(piece, step) for step, piece in zip(early_steps(ranks), early)]

time: 55.7 us -> 56.7 us (1.018)
  waiting for transfers between devices: 16.2 us -> 18.3 us
  starting transfers between devices: 22.6 us -> 21.2 us
    ppermute x20, waiting for transfers between devices: 16.2 us -> 18.3 us  [swap(): return lax.ppermute(piece, 'ctx', pairs) if step else piece]
    ppermute x20, starting transfers between devices: 22.6 us -> 21.2 us  [swap(): return lax.ppermute(piece, 'ctx', pairs) if step else piece]
where the time goes in v3:
time: 56.7 us; the launch traced here: 56.2 us
  starting transfers between devices  21.2 us (37%)
  waiting for transfers between devices  18.3 us (32%)
  Pallas kernels  14.4 us (25%)
  other arithmetic  1.37 us (2%)
  between operations  0.79 us (1%)
    ppermute x20, starting transfers between devices, swap(): return lax.ppermute(piece, 'ctx', pairs) if step else piece  21.2 us
    ppermute x20, waiting for transfers between devices, swap(): return lax.ppermute(piece, 'ctx', pairs) if step else piece  18.3 us
    pallas_call x2, Pallas kernels, spectral_call(): pl.pallas_call(kernel, in_specs=[pl.BlockSpec(memory_space=pltpu.SMEM)] +...  8.19 us
    pallas_call x2, Pallas kernels, prepare(): pl.pallas_call(functools.partial(prepare_kernel, ranks=ranks, count=len(a...  3.72 us
    pallas_call x2, Pallas kernels, finish_some(): pl.pallas_call(functools.partial(finish_kernel, steps=steps), in_specs=[p...  2.53 us
    convert_element_type x1, other arithmetic, on_device(): (out_grad.astype(jnp.float32) * conv_rows.astype(jnp.float32)).astype(jnp...  1.37 us
  transfers between devices with their start and end apart: 20, of which 7 were waited for; matrix products, arithmetic and copies ran while one was open for 2% of the time, Pallas kernels for 20%

profile of v3, /device:TPU:0, one launch (start us, length us, event | category | flops | bytes accessed | tf_op | source)
XLA Modules:
  0.0 56.2 jit_solution(5884744626871303738)
XLA Ops:
  0.6 0.0 copy-start.2
  0.6 0.0 copy-start.3
  0.7 0.0 copy-start.4
  0.7 2.0 %shard_map.120 = (bf16[352,256]{1,0:T(8,128)(2,1)S(1)}, bf16[352,256]{1,0:T(8,128)(2,1)S(1)}, bf16[352,256]{1,0:T(8,128)(2,1)S(1)}, bf16[352,256]{1,0:T(8,128)(2...) custom-call(bf16[256,2048]{1,0:T(8,128)(2,1)} %refs_0_.2, ...), custom_call_target="tpu_custom_call" | custom-call | flops 524288 | bytes 5767168 | tf_op jit(solution)/shard_map/pallas_call | solution.py:107
  2.7 3.0 %collective-permute-start = (bf16[352,256]{1,0:T(8,128)(2,1)S(1)}, bf16[352,256]{1,0:T(8,128)(2,1)S(1)}, u32[]{:S(2)}, u32[]{:S(2)}) collective-permute-start(bf16[352,256]{1,0:T(8,128)(2,1)S(1)} %get-tuple-element.50), channel_id=1, source_target_pairs={{0,16},{4,20},{8,24},{12,28},{16,0},{20,4},{24,8},{28,12},{1,17},{... | collective-permute-start | bytes 540680 | tf_op jit(solution)/shard_map/ppermute | solution.py:416
  5.7 1.5 %collective-permute-start.1 = (bf16[352,256]{1,0:T(8,128)(2,1)S(1)}, bf16[352,256]{1,0:T(8,128)(2,1)S(1)}, u32[]{:S(2)}, u32[]{:S(2)}) collective-permute-start(bf16[352,256]{1,0:T(8,128)(2,1)S(1)} %get-tuple-element.51), channel_id=1, source_target_pairs={{0,8},{4,12},{8,0},{12,4},{16,24},{20,28},{24,16},{28,20},{1,9},{5... | collective-permute-start | bytes 540680 | tf_op jit(solution)/shard_map/ppermute | solution.py:416
  7.2 1.7 %shard_map.121 = (bf16[256,256]{1,0:T(8,128)(2,1)S(1)}, bf16[608,256]{1,0:T(8,128)(2,1)S(1)}, bf16[256,256]{1,0:T(8,128)(2,1)S(1)}, bf16[608,256]{1,0:T(8,128)(2...) custom-call(bf16[256,2048]{1,0:T(8,128)(2,1)} %refs_5_.3, ...), custom_call_target="tpu_custom_call" | custom-call | flops 524288 | bytes 4194304 | tf_op jit(solution)/shard_map/pallas_call | solution.py:107
  8.9 0.1 collective-permute-start.6
  9.0 0.6 %collective-permute-start.4 = (bf16[608,256]{1,0:T(8,128)(2,1)S(1)}, bf16[608,256]{1,0:T(8,128)(2,1)S(1)}, u32[]{:S(2)}, u32[]{:S(2)}) collective-permute-start(bf16[608,256]{1,0:T(8,128)(2,1)S(1)} %get-tuple-element.57), channel_id=1, source_target_pairs={{0,20},{4,16},{8,28},{12,24},{16,4},{20,0},{24,12},{28,8},{1,21},{... | collective-permute-start | bytes 933896 | tf_op jit(solution)/shard_map/ppermute | solution.py:416
  9.6 0.0 collective-permute-start.5
  9.6 0.6 %collective-permute-done.refs_0_ = bf16[352,256]{1,0:T(8,128)(2,1)S(1)} collective-permute-done((bf16[352,256]{1,0:T(8,128)(2,1)S(1)}, bf16[352,256]{1,0:T(8,128)(2,1)S(1)}, u32[]{:S(2)}, u32[]{:S(2)}) %collective-permute-start) | collective-permute-done | bytes 180256 | tf_op jit(solution)/shard_map/ppermute | solution.py:416
  10.3 3.2 %collective-permute-start.2 = (bf16[352,256]{1,0:T(8,128)(2,1)S(1)}, bf16[352,256]{1,0:T(8,128)(2,1)S(1)}, u32[]{:S(2)}, u32[]{:S(2)}) collective-permute-start(bf16[352,256]{1,0:T(8,128)(2,1)S(1)} %get-tuple-element.52), channel_id=1, source_target_pairs={{0,24},{4,28},{8,16},{12,20},{16,8},{20,12},{24,0},{28,4},{1,25},{... | collective-permute-start | bytes 540680 | tf_op jit(solution)/shard_map/ppermute | solution.py:416
  13.5 0.0 collective-permute-done.1.refs_1_
  13.5 0.0 collective-permute-start.3
  13.5 0.0 collective-permute-done.6.refs_6_.refs_2_
  13.5 2.6 %collective-permute-start.10 = (bf16[256,256]{1,0:T(8,128)(2,1)S(1)}, bf16[256,256]{1,0:T(8,128)(2,1)S(1)}, u32[]{:S(2)}, u32[]{:S(2)}) collective-permute-start(bf16[256,256]{1,0:T(8,128)(2,1)S(1)} %get-tuple-element.68), channel_id=1, source_target_pairs={{0,28},{4,24},{8,20},{12,16},{16,12},{20,8},{24,4},{28,0},{1,29},{... | collective-permute-start | bytes 393224 | tf_op jit(solution)/shard_map/ppermute | solution.py:416
  16.1 8.2 %collective-permute-done.2.refs_2_ = bf16[352,256]{1,0:T(8,128)(2,1)S(1)} collective-permute-done((bf16[352,256]{1,0:T(8,128)(2,1)S(1)}, bf16[352,256]{1,0:T(8,128)(2,1)S(1)}, u32[]{:S(2)}, u32[]{:S(2)}) %collective-permute-start.2) | collective-permute-done | bytes 180256 | tf_op jit(solution)/shard_map/ppermute | solution.py:416
  24.3 0.5 collective-permute-start.7
  24.9 3.0 %collective-permute-done.3.refs_3_ = bf16[352,256]{1,0:T(8,128)(2,1)S(1)} collective-permute-done((bf16[352,256]{1,0:T(8,128)(2,1)S(1)}, bf16[352,256]{1,0:T(8,128)(2,1)S(1)}, u32[]{:S(2)}, u32[]{:S(2)}) %collective-permute-start.3) | collective-permute-done | bytes 180256 | tf_op jit(solution)/shard_map/ppermute | solution.py:416
  27.8 0.5 collective-permute-start.8
  28.4 0.0 collective-permute-done.4.refs_4_.refs_0_
  28.4 1.4 %collective-permute-start.9 = (bf16[256,256]{1,0:T(8,128)(2,1)S(1)}, bf16[256,256]{1,0:T(8,128)(2,1)S(1)}, u32[]{:S(2)}, u32[]{:S(2)}) collective-permute-start(bf16[256,256]{1,0:T(8,128)(2,1)S(1)} %get-tuple-element.67), channel_id=1, source_target_pairs={{0,24},{4,28},{8,16},{12,20},{16,8},{20,12},{24,0},{28,4},{1,25},{... | collective-permute-start | bytes 393224 | tf_op jit(solution)/shard_map/ppermute | solution.py:416
  29.8 0.0 collective-permute-done.5.refs_5_.refs_1_
  29.8 0.0 copy-done.2
  29.8 0.0 copy-done.3
  29.8 0.0 copy-done.4
  29.8 4.1 %shard_map.122 = (bf16[8,256,256]{2,1,0:T(8,128)(2,1)S(1)}, f32[8,512,256]{2,1,0:T(8,128)S(1)}, bf16[256,256]{1,0:T(8,128)(2,1)S(1)}, bf16[256,256]{1,0:T(8,128)(2,1)S(1)}) custom-call(s32[16]{0:T(128)S(1)} %copy-done.4, bf16[512,256]{1,0:T(8,128)(2,1)S(1)} %copy-done.2, bf16[256,512]{1,0:T(8,128)(2,1)S(1)} %copy-done.3, ...), custom_call_target="tpu_custom_call" | custom-call | flops 1275068416 | bytes 7864384 | tf_op jit(solution)/shard_map/pallas_call | solution.py:271
  33.9 1.1 %collective-permute-start.13 = (bf16[256,256]{1,0:T(8,128)(2,1)S(1)}, bf16[256,256]{1,0:T(8,128)(2,1)S(1)}, u32[]{:S(2)}, u32[]{:S(2)}) collective-permute-start(bf16[256,256]{1,0:T(8,128)(2,1)S(1)} %get-tuple-element.74), channel_id=1, source_target_pairs={{0,28},{4,24},{8,20},{12,16},{16,12},{20,8},{24,4},{28,0},{1,29},{... | collective-permute-start | bytes 393224 | tf_op jit(solution)/shard_map/ppermute | solution.py:416
  35.1 0.0 collective-permute-done.10.refs_6_
  35.1 1.4 %collective-permute-start.18 = (bf16[256,256]{1,0:T(8,128)(2,1)S(1)}, bf16[256,256]{1,0:T(8,128)(2,1)S(1)}, u32[]{:S(2)}, u32[]{:S(2)}) collective-permute-start(bf16[256,256]{1,0:T(8,128)(2,1)S(1)} %get-tuple-element.84), channel_id=1, source_target_pairs={{0,24},{4,28},{8,16},{12,20},{16,8},{20,12},{24,0},{28,4},{1,25},{... | collective-permute-start | bytes 393224 | tf_op jit(solution)/shard_map/ppermute | solution.py:416
  36.5 0.0 collective-permute-done.7.refs_3_
  36.5 0.0 collective-permute-done.8.refs_4_
  36.5 0.0 collective-permute-done.9.refs_5_
  36.5 0.0 copy-start.5
  36.5 0.0 copy-start.6
  36.6 4.1 %shard_map.123 = (bf16[352,256]{1,0:T(8,128)(2,1)S(1)}, bf16[352,256]{1,0:T(8,128)(2,1)S(1)}, bf16[352,256]{1,0:T(8,128)(2,1)S(1)}, bf16[352,256]{1,0:T(8,128)(2...) custom-call(s32[16]{0:T(128)S(1)} %copy-done.4, ...), custom_call_target="tpu_custom_call" | custom-call | flops 738197504 | bytes 8536128 | tf_op jit(solution)/shard_map/pallas_call | solution.py:271
  40.6 0.0 copy-start
  40.6 0.0 copy-start.1
  40.7 0.0 collective-permute-done.13.refs_4_
  40.7 0.9 %collective-permute-start.14 = (bf16[352,256]{1,0:T(8,128)(2,1)S(1)}, bf16[352,256]{1,0:T(8,128)(2,1)S(1)}, u32[]{:S(2)}, u32[]{:S(2)}) collective-permute-start(bf16[352,256]{1,0:T(8,128)(2,1)S(1)} %get-tuple-element.75), channel_id=1, source_target_pairs={{0,8},{4,12},{8,0},{12,4},{16,24},{20,28},{24,16},{28,20},{1,9},{5... | collective-permute-start | bytes 540680 | tf_op jit(solution)/shard_map/ppermute | solution.py:416
  41.6 2.0 %collective-permute-done.18.refs_3_ = bf16[256,256]{1,0:T(8,128)(2,1)S(1)} collective-permute-done((bf16[256,256]{1,0:T(8,128)(2,1)S(1)}, bf16[256,256]{1,0:T(8,128)(2,1)S(1)}, u32[]{:S(2)}, u32[]{:S(2)}) %collective-permute-start.18) | collective-permute-done | bytes 131104 | tf_op jit(solution)/shard_map/ppermute | solution.py:416
  43.5 1.5 %collective-permute-start.19 = (bf16[352,256]{1,0:T(8,128)(2,1)S(1)}, bf16[352,256]{1,0:T(8,128)(2,1)S(1)}, u32[]{:S(2)}, u32[]{:S(2)}) collective-permute-start(bf16[352,256]{1,0:T(8,128)(2,1)S(1)} %get-tuple-element.85), channel_id=1, source_target_pairs={{0,16},{4,20},{8,24},{12,28},{16,0},{20,4},{24,8},{28,12},{1,17},{... | collective-permute-start | bytes 540680 | tf_op jit(solution)/shard_map/ppermute | solution.py:416
  45.0 0.0 collective-permute-start.11
  45.0 0.7 %collective-permute-start.12 = (bf16[352,256]{1,0:T(8,128)(2,1)S(1)}, bf16[352,256]{1,0:T(8,128)(2,1)S(1)}, u32[]{:S(2)}, u32[]{:S(2)}) collective-permute-start(bf16[352,256]{1,0:T(8,128)(2,1)S(1)} %get-tuple-element.71), channel_id=1, source_target_pairs={{0,12},{4,8},{8,4},{12,0},{16,28},{20,24},{24,20},{28,16},{1,13},{... | collective-permute-start | bytes 540680 | tf_op jit(solution)/shard_map/ppermute | solution.py:416
  45.7 1.7 %collective-permute-done.14.refs_1_ = bf16[352,256]{1,0:T(8,128)(2,1)S(1)} collective-permute-done((bf16[352,256]{1,0:T(8,128)(2,1)S(1)}, bf16[352,256]{1,0:T(8,128)(2,1)S(1)}, u32[]{:S(2)}, u32[]{:S(2)}) %collective-permute-start.14) | collective-permute-done | bytes 180256 | tf_op jit(solution)/shard_map/ppermute | solution.py:416
  47.4 0.6 collective-permute-start.17
  48.0 1.4 %collective-permute-start.16 = (bf16[96,256]{1,0:T(8,128)(2,1)S(1)}, bf16[96,256]{1,0:T(8,128)(2,1)S(1)}, u32[]{:S(2)}, u32[]{:S(2)}) collective-permute-start(bf16[96,256]{1,0:T(8,128)(2,1)S(1)} %get-tuple-element.79), channel_id=1, source_target_pairs={{0,24},{4,28},{8,16},{12,20},{16,8},{20,12},{24,0},{28,4},{1,25},{... | collective-permute-start | bytes 147464 | tf_op jit(solution)/shard_map/ppermute | solution.py:416
  49.4 1.5 %collective-permute-done.19.refs_0_ = bf16[352,256]{1,0:T(8,128)(2,1)S(1)} collective-permute-done((bf16[352,256]{1,0:T(8,128)(2,1)S(1)}, bf16[352,256]{1,0:T(8,128)(2,1)S(1)}, u32[]{:S(2)}, u32[]{:S(2)}) %collective-permute-start.19) | collective-permute-done | bytes 180256 | tf_op jit(solution)/shard_map/ppermute | solution.py:416
  50.9 0.0 collective-permute-start.15
  50.9 0.0 copy-done.5
  50.9 0.0 copy-done.6
  51.0 1.4 %multiply_convert_fusion = bf16[256,2048]{1,0:T(8,128)(2,1)} fusion(bf16[256,2048]{1,0:T(8,128)(2,1)S(1)} %copy-done.6, bf16[256,2048]{1,0:T(8,128)(2,1)S(1)} %copy-done.5), kind=kLoop, calls=%fused_computation | loop fusion | flops 2097152 | bytes 3145728 | tf_op jit(solution)/shard_map/convert_element_type | solution.py:437
  52.3 0.0 copy-done
  52.3 0.0 copy-done.1
  52.3 1.3 %shard_map.124 = (bf16[256,2048]{1,0:T(8,128)(2,1)}, bf16[256,2048]{1,0:T(8,128)(2,1)}, f32[96,2048]{1,0:T(8,128)}) custom-call(bf16[352,256]{1,0:T(8,128)(2,1)S(1)} %collective-permute-done.19.refs_0_, bf16[352,256]{1,0:T(8,128)(2,1)S(1)} %collective-permute-done.14.refs_1_, bf16[352,256]{1,0:T(8,128)(2,1)S(1)} %get-tuple-element.87.refs_2_, ...), custom_call_target="tpu_custom_call" | custom-call | flops 655360 | bytes 4014080 | tf_op jit(solution)/shard_map/pallas_call | solution.py:360
  53.6 1.3 %collective-permute-done.11.refs_0_ = bf16[352,256]{1,0:T(8,128)(2,1)S(1)} collective-permute-done((bf16[352,256]{1,0:T(8,128)(2,1)S(1)}, bf16[352,256]{1,0:T(8,128)(2,1)S(1)}, u32[]{:S(2)}, u32[]{:S(2)}) %collective-permute-start.11) | collective-permute-done | bytes 180256 | tf_op jit(solution)/shard_map/ppermute | solution.py:416
  55.0 0.0 collective-permute-done.12.refs_1_
  55.0 0.0 collective-permute-done.17.refs_4_
  55.0 0.0 collective-permute-done.16.refs_3_
  55.0 0.0 collective-permute-done.15.refs_2_
  55.0 1.2 %shard_map.125 = (bf16[256,2048]{1,0:T(8,128)(2,1)}, bf16[256,2048]{1,0:T(8,128)(2,1)}, f32[96,2048]{1,0:T(8,128)}) custom-call(bf16[352,256]{1,0:T(8,128)(2,1)S(1)} %collective-permute-done.11.refs_0_, bf16[352,256]{1,0:T(8,128)(2,1)S(1)} %collective-permute-done.12.refs_1_, ...), custom_call_target="tpu_custom_call", output_to_operand_aliasing={{0}: (7, {}), {1}: (8, {}), {2}: (9, {})} | custom-call | flops 655360 | bytes 4014080 | tf_op jit(solution)/shard_map/pallas_call | solution.py:360
Async XLA Ops:
  0.6 29.2 %copy-start.2 = (bf16[512,256]{1,0:T(8,128)(2,1)S(1)}, bf16[512,256]{1,0:T(8,128)(2,1)}, u32[]{:S(2)}) copy-start(bf16[512,256]{1,0:T(8,128)(2,1)} %constant.4.clone.forward_ref) | copy-start | bytes 786436
  0.6 29.2 %copy-start.3 = (bf16[256,512]{1,0:T(8,128)(2,1)S(1)}, bf16[256,512]{1,0:T(8,128)(2,1)}, u32[]{:S(2)}) copy-start(bf16[256,512]{1,0:T(8,128)(2,1)} %constant.5.clone.inverse_ref) | copy-start | bytes 786436
  0.7 29.1 %copy-start.4 = (s32[16]{0:T(128)S(1)}, s32[16]{0:T(128)}, u32[]{:S(2)}) copy-start(s32[16]{0:T(128)} %table_ref.3) | copy-start | bytes 196
  2.7 7.6 %collective-permute-start = (bf16[352,256]{1,0:T(8,128)(2,1)S(1)}, bf16[352,256]{1,0:T(8,128)(2,1)S(1)}, u32[]{:S(2)}, u32[]{:S(2)}) collective-permute-start(bf16[352,256]{1,0:T(8,128)(2,1)S(1)} %get-tuple-element.50), channel_id=1, source_target_pairs={{0,16},{4,20},{8,24},{12,28},{16,0},{20,4},{24,8},{28,12},{1,17},{... | collective-permute-start | bytes 540680 | tf_op jit(solution)/shard_map/ppermute | solution.py:416
  5.7 7.8 %collective-permute-start.1 = (bf16[352,256]{1,0:T(8,128)(2,1)S(1)}, bf16[352,256]{1,0:T(8,128)(2,1)S(1)}, u32[]{:S(2)}, u32[]{:S(2)}) collective-permute-start(bf16[352,256]{1,0:T(8,128)(2,1)S(1)} %get-tuple-element.51), channel_id=1, source_target_pairs={{0,8},{4,12},{8,0},{12,4},{16,24},{20,28},{24,16},{28,20},{1,9},{5... | collective-permute-start | bytes 540680 | tf_op jit(solution)/shard_map/ppermute | solution.py:416
  8.9 4.6 %collective-permute-start.6 = (bf16[608,256]{1,0:T(8,128)(2,1)S(1)}, bf16[608,256]{1,0:T(8,128)(2,1)S(1)}, u32[]{:S(2)}, u32[]{:S(2)}) collective-permute-start(bf16[608,256]{1,0:T(8,128)(2,1)S(1)} %get-tuple-element.60), channel_id=1, source_target_pairs={{0,4},{4,0},{8,12},{12,8},{16,20},{20,16},{24,28},{28,24},{1,5},{5... | collective-permute-start | bytes 933896 | tf_op jit(solution)/shard_map/ppermute | solution.py:416
  9.0 19.4 %collective-permute-start.4 = (bf16[608,256]{1,0:T(8,128)(2,1)S(1)}, bf16[608,256]{1,0:T(8,128)(2,1)S(1)}, u32[]{:S(2)}, u32[]{:S(2)}) collective-permute-start(bf16[608,256]{1,0:T(8,128)(2,1)S(1)} %get-tuple-element.57), channel_id=1, source_target_pairs={{0,20},{4,16},{8,28},{12,24},{16,4},{20,0},{24,12},{28,8},{1,21},{... | collective-permute-start | bytes 933896 | tf_op jit(solution)/shard_map/ppermute | solution.py:416
  9.6 20.2 %collective-permute-start.5 = (bf16[608,256]{1,0:T(8,128)(2,1)S(1)}, bf16[608,256]{1,0:T(8,128)(2,1)S(1)}, u32[]{:S(2)}, u32[]{:S(2)}) collective-permute-start(bf16[608,256]{1,0:T(8,128)(2,1)S(1)} %get-tuple-element.58), channel_id=1, source_target_pairs={{0,12},{4,8},{8,4},{12,0},{16,28},{20,24},{24,20},{28,16},{1,13},{... | collective-permute-start | bytes 933896 | tf_op jit(solution)/shard_map/ppermute | solution.py:416
  10.3 14.1 %collective-permute-start.2 = (bf16[352,256]{1,0:T(8,128)(2,1)S(1)}, bf16[352,256]{1,0:T(8,128)(2,1)S(1)}, u32[]{:S(2)}, u32[]{:S(2)}) collective-permute-start(bf16[352,256]{1,0:T(8,128)(2,1)S(1)} %get-tuple-element.52), channel_id=1, source_target_pairs={{0,24},{4,28},{8,16},{12,20},{16,8},{20,12},{24,0},{28,4},{1,25},{... | collective-permute-start | bytes 540680 | tf_op jit(solution)/shard_map/ppermute | solution.py:416
  13.5 14.3 %collective-permute-start.3 = (bf16[352,256]{1,0:T(8,128)(2,1)S(1)}, bf16[352,256]{1,0:T(8,128)(2,1)S(1)}, u32[]{:S(2)}, u32[]{:S(2)}) collective-permute-start(bf16[352,256]{1,0:T(8,128)(2,1)S(1)} %get-tuple-element.53), channel_id=1, source_target_pairs={{0,28},{4,24},{8,20},{12,16},{16,12},{20,8},{24,4},{28,0},{1,29},{... | collective-permute-start | bytes 540680 | tf_op jit(solution)/shard_map/ppermute | solution.py:416
  13.5 21.6 %collective-permute-start.10 = (bf16[256,256]{1,0:T(8,128)(2,1)S(1)}, bf16[256,256]{1,0:T(8,128)(2,1)S(1)}, u32[]{:S(2)}, u32[]{:S(2)}) collective-permute-start(bf16[256,256]{1,0:T(8,128)(2,1)S(1)} %get-tuple-element.68), channel_id=1, source_target_pairs={{0,28},{4,24},{8,20},{12,16},{16,12},{20,8},{24,4},{28,0},{1,29},{... | collective-permute-start | bytes 393224 | tf_op jit(solution)/shard_map/ppermute | solution.py:416
  24.3 12.2 %collective-permute-start.7 = (bf16[256,256]{1,0:T(8,128)(2,1)S(1)}, bf16[256,256]{1,0:T(8,128)(2,1)S(1)}, u32[]{:S(2)}, u32[]{:S(2)}) collective-permute-start(bf16[256,256]{1,0:T(8,128)(2,1)S(1)} %get-tuple-element.65), channel_id=1, source_target_pairs={{0,16},{4,20},{8,24},{12,28},{16,0},{20,4},{24,8},{28,12},{1,17},{... | collective-permute-start | bytes 393224 | tf_op jit(solution)/shard_map/ppermute | solution.py:416
  27.8 8.7 %collective-permute-start.8 = (bf16[256,256]{1,0:T(8,128)(2,1)S(1)}, bf16[256,256]{1,0:T(8,128)(2,1)S(1)}, u32[]{:S(2)}, u32[]{:S(2)}) collective-permute-start(bf16[256,256]{1,0:T(8,128)(2,1)S(1)} %get-tuple-element.66), channel_id=1, source_target_pairs={{0,8},{4,12},{8,0},{12,4},{16,24},{20,28},{24,16},{28,20},{1,9},{5... | collective-permute-start | bytes 393224 | tf_op jit(solution)/shard_map/ppermute | solution.py:416
  28.4 8.2 %collective-permute-start.9 = (bf16[256,256]{1,0:T(8,128)(2,1)S(1)}, bf16[256,256]{1,0:T(8,128)(2,1)S(1)}, u32[]{:S(2)}, u32[]{:S(2)}) collective-permute-start(bf16[256,256]{1,0:T(8,128)(2,1)S(1)} %get-tuple-element.67), channel_id=1, source_target_pairs={{0,24},{4,28},{8,16},{12,20},{16,8},{20,12},{24,0},{28,4},{1,25},{... | collective-permute-start | bytes 393224 | tf_op jit(solution)/shard_map/ppermute | solution.py:416
  33.9 6.7 %collective-permute-start.13 = (bf16[256,256]{1,0:T(8,128)(2,1)S(1)}, bf16[256,256]{1,0:T(8,128)(2,1)S(1)}, u32[]{:S(2)}, u32[]{:S(2)}) collective-permute-start(bf16[256,256]{1,0:T(8,128)(2,1)S(1)} %get-tuple-element.74), channel_id=1, source_target_pairs={{0,28},{4,24},{8,20},{12,16},{16,12},{20,8},{24,4},{28,0},{1,29},{... | collective-permute-start | bytes 393224 | tf_op jit(solution)/shard_map/ppermute | solution.py:416
  35.1 8.4 %collective-permute-start.18 = (bf16[256,256]{1,0:T(8,128)(2,1)S(1)}, bf16[256,256]{1,0:T(8,128)(2,1)S(1)}, u32[]{:S(2)}, u32[]{:S(2)}) collective-permute-start(bf16[256,256]{1,0:T(8,128)(2,1)S(1)} %get-tuple-element.84), channel_id=1, source_target_pairs={{0,24},{4,28},{8,16},{12,20},{16,8},{20,12},{24,0},{28,4},{1,25},{... | collective-permute-start | bytes 393224 | tf_op jit(solution)/shard_map/ppermute | solution.py:416
  36.5 14.4 %copy-start.5 = (bf16[256,2048]{1,0:T(8,128)(2,1)S(1)}, bf16[256,2048]{1,0:T(8,128)(2,1)}, u32[]{:S(2)}) copy-start(bf16[256,2048]{1,0:T(8,128)(2,1)} %refs_0_.2) | copy-start | bytes 3145732
  36.5 14.4 %copy-start.6 = (bf16[256,2048]{1,0:T(8,128)(2,1)S(1)}, bf16[256,2048]{1,0:T(8,128)(2,1)}, u32[]{:S(2)}) copy-start(bf16[256,2048]{1,0:T(8,128)(2,1)} %param.13) | copy-start | bytes 3145732
  40.6 11.7 %copy-start = (bf16[256,2048]{1,0:T(8,128)(2,1)S(1)}, bf16[256,2048]{1,0:T(8,128)(2,1)}, u32[]{:S(2)}) copy-start(bf16[256,2048]{1,0:T(8,128)(2,1)} %refs_5_.3) | copy-start | bytes 3145732
  40.6 11.7 %copy-start.1 = (bf16[256,2048]{1,0:T(8,128)(2,1)S(1)}, bf16[256,2048]{1,0:T(8,128)(2,1)}, u32[]{:S(2)}) copy-start(bf16[256,2048]{1,0:T(8,128)(2,1)} %refs_6_.3) | copy-start | bytes 3145732
  40.7 6.8 %collective-permute-start.14 = (bf16[352,256]{1,0:T(8,128)(2,1)S(1)}, bf16[352,256]{1,0:T(8,128)(2,1)S(1)}, u32[]{:S(2)}, u32[]{:S(2)}) collective-permute-start(bf16[352,256]{1,0:T(8,128)(2,1)S(1)} %get-tuple-element.75), channel_id=1, source_target_pairs={{0,8},{4,12},{8,0},{12,4},{16,24},{20,28},{24,16},{28,20},{1,9},{5... | collective-permute-start | bytes 540680 | tf_op jit(solution)/shard_map/ppermute | solution.py:416
  43.5 7.4 %collective-permute-start.19 = (bf16[352,256]{1,0:T(8,128)(2,1)S(1)}, bf16[352,256]{1,0:T(8,128)(2,1)S(1)}, u32[]{:S(2)}, u32[]{:S(2)}) collective-permute-start(bf16[352,256]{1,0:T(8,128)(2,1)S(1)} %get-tuple-element.85), channel_id=1, source_target_pairs={{0,16},{4,20},{8,24},{12,28},{16,0},{20,4},{24,8},{28,12},{1,17},{... | collective-permute-start | bytes 540680 | tf_op jit(solution)/shard_map/ppermute | solution.py:416
  45.0 9.9 %collective-permute-start.11 = (bf16[352,256]{1,0:T(8,128)(2,1)S(1)}, bf16[352,256]{1,0:T(8,128)(2,1)S(1)}, u32[]{:S(2)}, u32[]{:S(2)}) collective-permute-start(bf16[352,256]{1,0:T(8,128)(2,1)S(1)} %get-tuple-element.70), channel_id=1, source_target_pairs={{0,20},{4,16},{8,28},{12,24},{16,4},{20,0},{24,12},{28,8},{1,21},{... | collective-permute-start | bytes 540680 | tf_op jit(solution)/shard_map/ppermute | solution.py:416
  45.0 9.9 %collective-permute-start.12 = (bf16[352,256]{1,0:T(8,128)(2,1)S(1)}, bf16[352,256]{1,0:T(8,128)(2,1)S(1)}, u32[]{:S(2)}, u32[]{:S(2)}) collective-permute-start(bf16[352,256]{1,0:T(8,128)(2,1)S(1)} %get-tuple-element.71), channel_id=1, source_target_pairs={{0,12},{4,8},{8,4},{12,0},{16,28},{20,24},{24,20},{28,16},{1,13},{... | collective-permute-start | bytes 540680 | tf_op jit(solution)/shard_map/ppermute | solution.py:416
  47.4 7.5 %collective-permute-start.17 = (bf16[96,256]{1,0:T(8,128)(2,1)S(1)}, bf16[96,256]{1,0:T(8,128)(2,1)S(1)}, u32[]{:S(2)}, u32[]{:S(2)}) collective-permute-start(bf16[96,256]{1,0:T(8,128)(2,1)S(1)} %get-tuple-element.82), channel_id=1, source_target_pairs={{0,28},{4,24},{8,20},{12,16},{16,12},{20,8},{24,4},{28,0},{1,29},{... | collective-permute-start | bytes 147464 | tf_op jit(solution)/shard_map/ppermute | solution.py:416
  48.0 7.0 %collective-permute-start.16 = (bf16[96,256]{1,0:T(8,128)(2,1)S(1)}, bf16[96,256]{1,0:T(8,128)(2,1)S(1)}, u32[]{:S(2)}, u32[]{:S(2)}) collective-permute-start(bf16[96,256]{1,0:T(8,128)(2,1)S(1)} %get-tuple-element.79), channel_id=1, source_target_pairs={{0,24},{4,28},{8,16},{12,20},{16,8},{20,12},{24,0},{28,4},{1,25},{... | collective-permute-start | bytes 147464 | tf_op jit(solution)/shard_map/ppermute | solution.py:416
  50.9 4.0 %collective-permute-start.15 = (bf16[352,256]{1,0:T(8,128)(2,1)S(1)}, bf16[352,256]{1,0:T(8,128)(2,1)S(1)}, u32[]{:S(2)}, u32[]{:S(2)}) collective-permute-start(bf16[352,256]{1,0:T(8,128)(2,1)S(1)} %get-tuple-element.76), channel_id=1, source_target_pairs={{0,4},{4,0},{8,12},{12,8},{16,20},{20,16},{24,28},{28,24},{1,5},{5... | collective-permute-start | bytes 540680 | tf_op jit(solution)/shard_map/ppermute | solution.py:416

commit v4 on v2

--- a/solution.py
+++ b/solution.py
@@ -15,13 +15,14 @@
 SPAN = 2 * BLOCK
 LAG_SPANS = LAG_BLOCKS * BLOCK // SPAN
 LANES = 128
+GROUPS = 4
 VMEM_BYTES = 32 * 2**20
 
 
 def step_orders(ranks):
     if ranks != 8:
         return [list(range(ranks))] * 3
-    return [4, 2, 6, 7, 5, 3, 1, 0], [5, 3, 1, 4, 2, 6, 7, 0], [4, 2, 5, 3, 1, 6, 7, 0]
+    return [4, 2, 6, 7, 5, 3, 1, 0], [5, 3, 1, 2, 6, 7, 4, 0], [4, 2, 5, 3, 1, 6, 7, 0]
 
 
 def joint_steps(ranks):
@@ -56,13 +57,14 @@
     sources, above_refs, refs = refs[:count], refs[count : count + len(above)], refs[count + len(above) :]
     targets, rest = refs[:ranks], refs[ranks:]
     slabs, in_sems = rest[:count], rest[count]
-    rows, half = slabs[0].shape[1:]
-    width = 2 * half // ranks
+    groups, rows, total = slabs[0].shape
+    owners = ranks // groups
+    width = total // owners
     device = lax.axis_index("ctx")
-    upper = lax.shift_right_logical(device, int(math.log2(ranks)) - 1)
+    upper = lax.shift_right_logical(device, int(math.log2(owners)))
     loads = []
-    for group in range(2):
-        columns = pl.ds(pl.multiple_of(swapped(upper, group) * half, LANES), half)
+    for group in range(groups):
+        columns = pl.ds(pl.multiple_of(swapped(upper, group) * total, LANES), total)
         loads.append(
             [
                 pltpu.make_async_copy(source.at[:, columns], slab.at[group], in_sems.at[group, at])
@@ -72,11 +74,11 @@
         for load in loads[group]:
             load.start()
     for step in range(ranks):
-        group, inner = divmod(step, ranks // 2)
+        group, inner = divmod(step, owners)
         if inner == 0:
             for load in loads[group]:
                 load.wait()
-        column = jnp.bitwise_and(swapped(device, inner), ranks // 2 - 1) * width
+        column = jnp.bitwise_and(swapped(device, inner), owners - 1) * width
         columns = pl.ds(pl.multiple_of(column, LANES), width)
         target = targets[step]
         if step in above:
@@ -101,15 +103,14 @@
         pieces = [lax.dynamic_index_in_dim(packed, device ^ m, 0, False) for m in range(ranks)]
         return [jnp.concatenate([above[m], p], 0) if m in above else p for m, p in enumerate(pieces)]
     piece_rows = [out_rows + (above[m].shape[0] if m in above else 0) for m in range(ranks)]
-    half = channels // 2
-    slabs = [pltpu.VMEM((2, a.shape[0], half), a.dtype) for a in arrays]
+    slabs = [pltpu.VMEM((GROUPS, a.shape[0], channels // GROUPS), a.dtype) for a in arrays]
     return pl.pallas_call(
         functools.partial(prepare_kernel, ranks=ranks, count=len(arrays), above=tuple(above)),
         in_specs=[pl.BlockSpec(memory_space=pltpu.HBM)] * len(arrays)
         + [pl.BlockSpec(memory_space=pltpu.VMEM)] * len(above),
         out_specs=[pl.BlockSpec(memory_space=pltpu.VMEM)] * ranks,
         out_shape=[jax.ShapeDtypeStruct((r, width), jnp.bfloat16) for r in piece_rows],
-        scratch_shapes=slabs + [pltpu.SemaphoreType.DMA((2, len(arrays)))],
+        scratch_shapes=slabs + [pltpu.SemaphoreType.DMA((GROUPS, len(arrays)))],
         compiler_params=pltpu.CompilerParams(vmem_limit_bytes=VMEM_BYTES),
         cost_estimate=pl.CostEstimate(
             flops=rows * channels, bytes_accessed=8 * out_rows * channels, transcendentals=0

time: 55.7 us -> 57 us (1.023)
  starting transfers between devices: 22.6 us -> 23.8 us
    ppermute x20, starting transfers between devices: 22.6 us -> 23.8 us  [swap(): return lax.ppermute(piece, 'ctx', pairs) if step else piece]
where the time goes in v4:
time: 57 us; the launch traced here: 56.7 us
  starting transfers between devices  23.8 us (42%)
  waiting for transfers between devices  16.4 us (29%)
  Pallas kernels  14.3 us (25%)
  other arithmetic  1.37 us (2%)
  between operations  0.78 us (1%)
    ppermute x20, starting transfers between devices, swap(): return lax.ppermute(piece, 'ctx', pairs) if step else piece  23.8 us
    ppermute x20, waiting for transfers between devices, swap(): return lax.ppermute(piece, 'ctx', pairs) if step else piece  16.4 us
    pallas_call x2, Pallas kernels, spectral_call(): pl.pallas_call(kernel, in_specs=[pl.BlockSpec(memory_space=pltpu.SMEM)] +...  8.19 us
    pallas_call x2, Pallas kernels, prepare(): pl.pallas_call(functools.partial(prepare_kernel, ranks=ranks, count=len(a...  3.59 us
    pallas_call x2, Pallas kernels, finish_some(): pl.pallas_call(functools.partial(finish_kernel, steps=steps), in_specs=[p...  2.52 us
    convert_element_type x1, other arithmetic, on_device(): (out_grad.astype(jnp.float32) * conv_rows.astype(jnp.float32)).astype(jnp...  1.37 us
  transfers between devices with their start and end apart: 20, of which 7 were waited for; matrix products, arithmetic and copies ran while one was open for 2% of the time, Pallas kernels for 20%

profile of v4, /device:TPU:0, one launch (start us, length us, event | category | flops | bytes accessed | tf_op | source)
XLA Modules:
  0.0 56.7 jit_solution(5356254155419897337)
XLA Ops:
  0.6 0.0 copy-start.2
  0.6 0.0 copy-start.3
  0.7 0.0 copy-start.4
  0.7 2.0 %shard_map.120 = (bf16[352,256]{1,0:T(8,128)(2,1)S(1)}, bf16[352,256]{1,0:T(8,128)(2,1)S(1)}, bf16[352,256]{1,0:T(8,128)(2,1)S(1)}, bf16[352,256]{1,0:T(8,128)(2...) custom-call(bf16[256,2048]{1,0:T(8,128)(2,1)} %refs_0_.2, ...), custom_call_target="tpu_custom_call" | custom-call | flops 524288 | bytes 5767168 | tf_op jit(solution)/shard_map/pallas_call | solution.py:107
  2.6 3.0 %collective-permute-start = (bf16[352,256]{1,0:T(8,128)(2,1)S(1)}, bf16[352,256]{1,0:T(8,128)(2,1)S(1)}, u32[]{:S(2)}, u32[]{:S(2)}) collective-permute-start(bf16[352,256]{1,0:T(8,128)(2,1)S(1)} %get-tuple-element.48), channel_id=1, source_target_pairs={{0,16},{4,20},{8,24},{12,28},{16,0},{20,4},{24,8},{28,12},{1,17},{... | collective-permute-start | bytes 540680 | tf_op jit(solution)/shard_map/ppermute | solution.py:416
  5.7 1.5 %collective-permute-start.1 = (bf16[352,256]{1,0:T(8,128)(2,1)S(1)}, bf16[352,256]{1,0:T(8,128)(2,1)S(1)}, u32[]{:S(2)}, u32[]{:S(2)}) collective-permute-start(bf16[352,256]{1,0:T(8,128)(2,1)S(1)} %get-tuple-element.49), channel_id=1, source_target_pairs={{0,8},{4,12},{8,0},{12,4},{16,24},{20,28},{24,16},{28,20},{1,9},{5... | collective-permute-start | bytes 540680 | tf_op jit(solution)/shard_map/ppermute | solution.py:416
  7.2 1.6 %shard_map.121 = (bf16[256,256]{1,0:T(8,128)(2,1)S(1)}, bf16[608,256]{1,0:T(8,128)(2,1)S(1)}, bf16[256,256]{1,0:T(8,128)(2,1)S(1)}, bf16[608,256]{1,0:T(8,128)(2...) custom-call(bf16[256,2048]{1,0:T(8,128)(2,1)} %refs_5_.3, ...), custom_call_target="tpu_custom_call" | custom-call | flops 524288 | bytes 4194304 | tf_op jit(solution)/shard_map/pallas_call | solution.py:107
  8.8 0.1 collective-permute-start.4
  8.9 0.3 collective-permute-start.5
  9.2 0.4 collective-permute-start.6
  9.6 0.6 %collective-permute-done.refs_0_ = bf16[352,256]{1,0:T(8,128)(2,1)S(1)} collective-permute-done((bf16[352,256]{1,0:T(8,128)(2,1)S(1)}, bf16[352,256]{1,0:T(8,128)(2,1)S(1)}, u32[]{:S(2)}, u32[]{:S(2)}) %collective-permute-start) | collective-permute-done | bytes 180256 | tf_op jit(solution)/shard_map/ppermute | solution.py:416
  10.2 3.6 %collective-permute-start.2 = (bf16[352,256]{1,0:T(8,128)(2,1)S(1)}, bf16[352,256]{1,0:T(8,128)(2,1)S(1)}, u32[]{:S(2)}, u32[]{:S(2)}) collective-permute-start(bf16[352,256]{1,0:T(8,128)(2,1)S(1)} %get-tuple-element.50), channel_id=1, source_target_pairs={{0,24},{4,28},{8,16},{12,20},{16,8},{20,12},{24,0},{28,4},{1,25},{... | collective-permute-start | bytes 540680 | tf_op jit(solution)/shard_map/ppermute | solution.py:416
  13.8 0.0 collective-permute-done.1.refs_1_
  13.8 0.0 collective-permute-start.3
  13.8 10.3 %collective-permute-done.2.refs_2_ = bf16[352,256]{1,0:T(8,128)(2,1)S(1)} collective-permute-done((bf16[352,256]{1,0:T(8,128)(2,1)S(1)}, bf16[352,256]{1,0:T(8,128)(2,1)S(1)}, u32[]{:S(2)}, u32[]{:S(2)}) %collective-permute-start.2) | collective-permute-done | bytes 180256 | tf_op jit(solution)/shard_map/ppermute | solution.py:416
  24.2 0.4 collective-permute-start.10
  24.6 0.6 %collective-permute-done.3.refs_3_ = bf16[352,256]{1,0:T(8,128)(2,1)S(1)} collective-permute-done((bf16[352,256]{1,0:T(8,128)(2,1)S(1)}, bf16[352,256]{1,0:T(8,128)(2,1)S(1)}, u32[]{:S(2)}, u32[]{:S(2)}) %collective-permute-start.3) | collective-permute-done | bytes 180256 | tf_op jit(solution)/shard_map/ppermute | solution.py:416
  25.2 1.8 %collective-permute-start.7 = (bf16[256,256]{1,0:T(8,128)(2,1)S(1)}, bf16[256,256]{1,0:T(8,128)(2,1)S(1)}, u32[]{:S(2)}, u32[]{:S(2)}) collective-permute-start(bf16[256,256]{1,0:T(8,128)(2,1)S(1)} %get-tuple-element.61), channel_id=1, source_target_pairs={{0,8},{4,12},{8,0},{12,4},{16,24},{20,28},{24,16},{28,20},{1,9},{5... | collective-permute-start | bytes 393224 | tf_op jit(solution)/shard_map/ppermute | solution.py:416
  27.0 0.0 collective-permute-done.4.refs_4_.refs_0_
  27.0 1.7 %collective-permute-start.8 = (bf16[256,256]{1,0:T(8,128)(2,1)S(1)}, bf16[256,256]{1,0:T(8,128)(2,1)S(1)}, u32[]{:S(2)}, u32[]{:S(2)}) collective-permute-start(bf16[256,256]{1,0:T(8,128)(2,1)S(1)} %get-tuple-element.62), channel_id=1, source_target_pairs={{0,24},{4,28},{8,16},{12,20},{16,8},{20,12},{24,0},{28,4},{1,25},{... | collective-permute-start | bytes 393224 | tf_op jit(solution)/shard_map/ppermute | solution.py:416
  28.7 0.0 collective-permute-done.5.refs_5_.refs_1_
  28.7 0.9 %collective-permute-start.9 = (bf16[256,256]{1,0:T(8,128)(2,1)S(1)}, bf16[256,256]{1,0:T(8,128)(2,1)S(1)}, u32[]{:S(2)}, u32[]{:S(2)}) collective-permute-start(bf16[256,256]{1,0:T(8,128)(2,1)S(1)} %get-tuple-element.63), channel_id=1, source_target_pairs={{0,28},{4,24},{8,20},{12,16},{16,12},{20,8},{24,4},{28,0},{1,29},{... | collective-permute-start | bytes 393224 | tf_op jit(solution)/shard_map/ppermute | solution.py:416
  29.6 0.0 collective-permute-done.6.refs_6_.refs_2_
  29.6 0.0 copy-done.2
  29.6 0.0 copy-done.3
  29.6 0.0 copy-done.4
  29.6 4.1 %shard_map.122 = (bf16[8,256,256]{2,1,0:T(8,128)(2,1)S(1)}, f32[8,512,256]{2,1,0:T(8,128)S(1)}, bf16[256,256]{1,0:T(8,128)(2,1)S(1)}, bf16[256,256]{1,0:T(8,128)(2,1)S(1)}) custom-call(s32[16]{0:T(128)S(1)} %copy-done.4, bf16[512,256]{1,0:T(8,128)(2,1)S(1)} %copy-done.2, bf16[256,512]{1,0:T(8,128)(2,1)S(1)} %copy-done.3, ...), custom_call_target="tpu_custom_call" | custom-call | flops 1275068416 | bytes 7864384 | tf_op jit(solution)/shard_map/pallas_call | solution.py:271
  33.8 1.8 %collective-permute-start.13 = (bf16[256,256]{1,0:T(8,128)(2,1)S(1)}, bf16[256,256]{1,0:T(8,128)(2,1)S(1)}, u32[]{:S(2)}, u32[]{:S(2)}) collective-permute-start(bf16[256,256]{1,0:T(8,128)(2,1)S(1)} %get-tuple-element.70), channel_id=1, source_target_pairs={{0,28},{4,24},{8,20},{12,16},{16,12},{20,8},{24,4},{28,0},{1,29},{... | collective-permute-start | bytes 393224 | tf_op jit(solution)/shard_map/ppermute | solution.py:416
  35.5 0.0 collective-permute-done.10.refs_6_
  35.5 1.3 %collective-permute-start.18 = (bf16[256,256]{1,0:T(8,128)(2,1)S(1)}, bf16[256,256]{1,0:T(8,128)(2,1)S(1)}, u32[]{:S(2)}, u32[]{:S(2)}) collective-permute-start(bf16[256,256]{1,0:T(8,128)(2,1)S(1)} %get-tuple-element.80), channel_id=1, source_target_pairs={{0,24},{4,28},{8,16},{12,20},{16,8},{20,12},{24,0},{28,4},{1,25},{... | collective-permute-start | bytes 393224 | tf_op jit(solution)/shard_map/ppermute | solution.py:416
  36.8 0.0 collective-permute-done.7.refs_3_
  36.8 0.0 collective-permute-done.8.refs_4_
  36.8 1.0 %collective-permute-done.9.refs_5_ = bf16[256,256]{1,0:T(8,128)(2,1)S(1)} collective-permute-done((bf16[256,256]{1,0:T(8,128)(2,1)S(1)}, bf16[256,256]{1,0:T(8,128)(2,1)S(1)}, u32[]{:S(2)}, u32[]{:S(2)}) %collective-permute-start.9) | collective-permute-done | bytes 131104 | tf_op jit(solution)/shard_map/ppermute | solution.py:416
  37.8 0.0 copy-start.5
  37.8 0.0 copy-start.6
  37.8 4.1 %shard_map.123 = (bf16[352,256]{1,0:T(8,128)(2,1)S(1)}, bf16[352,256]{1,0:T(8,128)(2,1)S(1)}, bf16[352,256]{1,0:T(8,128)(2,1)S(1)}, bf16[352,256]{1,0:T(8,128)(2...) custom-call(s32[16]{0:T(128)S(1)} %copy-done.4, ...), custom_call_target="tpu_custom_call" | custom-call | flops 738197504 | bytes 8536128 | tf_op jit(solution)/shard_map/pallas_call | solution.py:271
  41.9 0.0 copy-start
  41.9 0.0 copy-start.1
  41.9 0.0 collective-permute-done.13.refs_4_
  41.9 1.3 %collective-permute-start.14 = (bf16[352,256]{1,0:T(8,128)(2,1)S(1)}, bf16[352,256]{1,0:T(8,128)(2,1)S(1)}, u32[]{:S(2)}, u32[]{:S(2)}) collective-permute-start(bf16[352,256]{1,0:T(8,128)(2,1)S(1)} %get-tuple-element.71), channel_id=1, source_target_pairs={{0,8},{4,12},{8,0},{12,4},{16,24},{20,28},{24,16},{28,20},{1,9},{5... | collective-permute-start | bytes 540680 | tf_op jit(solution)/shard_map/ppermute | solution.py:416
  43.2 0.6 %collective-permute-done.18.refs_3_ = bf16[256,256]{1,0:T(8,128)(2,1)S(1)} collective-permute-done((bf16[256,256]{1,0:T(8,128)(2,1)S(1)}, bf16[256,256]{1,0:T(8,128)(2,1)S(1)}, u32[]{:S(2)}, u32[]{:S(2)}) %collective-permute-start.18) | collective-permute-done | bytes 131104 | tf_op jit(solution)/shard_map/ppermute | solution.py:416
  43.8 0.9 %collective-permute-start.19 = (bf16[352,256]{1,0:T(8,128)(2,1)S(1)}, bf16[352,256]{1,0:T(8,128)(2,1)S(1)}, u32[]{:S(2)}, u32[]{:S(2)}) collective-permute-start(bf16[352,256]{1,0:T(8,128)(2,1)S(1)} %get-tuple-element.81), channel_id=1, source_target_pairs={{0,16},{4,20},{8,24},{12,28},{16,0},{20,4},{24,8},{28,12},{1,17},{... | collective-permute-start | bytes 540680 | tf_op jit(solution)/shard_map/ppermute | solution.py:416
  44.7 0.5 collective-permute-start.11
  45.2 1.6 %collective-permute-start.12 = (bf16[352,256]{1,0:T(8,128)(2,1)S(1)}, bf16[352,256]{1,0:T(8,128)(2,1)S(1)}, u32[]{:S(2)}, u32[]{:S(2)}) collective-permute-start(bf16[352,256]{1,0:T(8,128)(2,1)S(1)} %get-tuple-element.67), channel_id=1, source_target_pairs={{0,12},{4,8},{8,4},{12,0},{16,28},{20,24},{24,20},{28,16},{1,13},{... | collective-permute-start | bytes 540680 | tf_op jit(solution)/shard_map/ppermute | solution.py:416
  46.8 2.6 %collective-permute-done.14.refs_1_ = bf16[352,256]{1,0:T(8,128)(2,1)S(1)} collective-permute-done((bf16[352,256]{1,0:T(8,128)(2,1)S(1)}, bf16[352,256]{1,0:T(8,128)(2,1)S(1)}, u32[]{:S(2)}, u32[]{:S(2)}) %collective-permute-start.14) | collective-permute-done | bytes 180256 | tf_op jit(solution)/shard_map/ppermute | solution.py:416
  49.4 0.6 collective-permute-start.17
  49.9 1.9 %collective-permute-start.16 = (bf16[96,256]{1,0:T(8,128)(2,1)S(1)}, bf16[96,256]{1,0:T(8,128)(2,1)S(1)}, u32[]{:S(2)}, u32[]{:S(2)}) collective-permute-start(bf16[96,256]{1,0:T(8,128)(2,1)S(1)} %get-tuple-element.75), channel_id=1, source_target_pairs={{0,24},{4,28},{8,16},{12,20},{16,8},{20,12},{24,0},{28,4},{1,25},{... | collective-permute-start | bytes 147464 | tf_op jit(solution)/shard_map/ppermute | solution.py:416
  51.8 0.0 collective-permute-done.19.refs_0_
  51.8 0.3 collective-permute-start.15
  52.1 0.0 copy-done.5
  52.1 0.0 copy-done.6
  52.2 1.4 %multiply_convert_fusion = bf16[256,2048]{1,0:T(8,128)(2,1)} fusion(bf16[256,2048]{1,0:T(8,128)(2,1)S(1)} %copy-done.6, bf16[256,2048]{1,0:T(8,128)(2,1)S(1)} %copy-done.5), kind=kLoop, calls=%fused_computation | loop fusion | flops 2097152 | bytes 3145728 | tf_op jit(solution)/shard_map/convert_element_type | solution.py:430
  53.5 0.0 copy-done
  53.5 0.0 copy-done.1
  53.5 1.3 %shard_map.124 = (bf16[256,2048]{1,0:T(8,128)(2,1)}, bf16[256,2048]{1,0:T(8,128)(2,1)}, f32[96,2048]{1,0:T(8,128)}) custom-call(bf16[352,256]{1,0:T(8,128)(2,1)S(1)} %collective-permute-done.19.refs_0_, bf16[352,256]{1,0:T(8,128)(2,1)S(1)} %collective-permute-done.14.refs_1_, bf16[352,256]{1,0:T(8,128)(2,1)S(1)} %get-tuple-element.83.refs_2_, ...), custom_call_target="tpu_custom_call" | custom-call | flops 655360 | bytes 4014080 | tf_op jit(solution)/shard_map/pallas_call | solution.py:360
  54.8 0.0 collective-permute-done.11.refs_0_
  54.9 0.0 collective-permute-done.12.refs_1_
  54.9 0.0 collective-permute-done.17.refs_4_
  54.9 0.6 %collective-permute-done.16.refs_3_ = bf16[96,256]{1,0:T(8,128)(2,1)S(1)} collective-permute-done((bf16[96,256]{1,0:T(8,128)(2,1)S(1)}, bf16[96,256]{1,0:T(8,128)(2,1)S(1)}, u32[]{:S(2)}, u32[]{:S(2)}) %collective-permute-start.16) | collective-permute-done | bytes 49184 | tf_op jit(solution)/shard_map/ppermute | solution.py:416
  55.5 0.0 collective-permute-done.15.refs_2_
  55.5 1.2 %shard_map.125 = (bf16[256,2048]{1,0:T(8,128)(2,1)}, bf16[256,2048]{1,0:T(8,128)(2,1)}, f32[96,2048]{1,0:T(8,128)}) custom-call(bf16[352,256]{1,0:T(8,128)(2,1)S(1)} %collective-permute-done.11.refs_0_, bf16[352,256]{1,0:T(8,128)(2,1)S(1)} %collective-permute-done.12.refs_1_, ...), custom_call_target="tpu_custom_call", output_to_operand_aliasing={{0}: (7, {}), {1}: (8, {}), {2}: (9, {})} | custom-call | flops 655360 | bytes 4014080 | tf_op jit(solution)/shard_map/pallas_call | solution.py:360
Async XLA Ops:
  0.6 29.0 %copy-start.2 = (bf16[512,256]{1,0:T(8,128)(2,1)S(1)}, bf16[512,256]{1,0:T(8,128)(2,1)}, u32[]{:S(2)}) copy-start(bf16[512,256]{1,0:T(8,128)(2,1)} %constant.4.clone.forward_ref) | copy-start | bytes 786436
  0.6 29.0 %copy-start.3 = (bf16[256,512]{1,0:T(8,128)(2,1)S(1)}, bf16[256,512]{1,0:T(8,128)(2,1)}, u32[]{:S(2)}) copy-start(bf16[256,512]{1,0:T(8,128)(2,1)} %constant.5.clone.inverse_ref) | copy-start | bytes 786436
  0.7 29.0 %copy-start.4 = (s32[16]{0:T(128)S(1)}, s32[16]{0:T(128)}, u32[]{:S(2)}) copy-start(s32[16]{0:T(128)} %table_ref.3) | copy-start | bytes 196
  2.6 7.6 %collective-permute-start = (bf16[352,256]{1,0:T(8,128)(2,1)S(1)}, bf16[352,256]{1,0:T(8,128)(2,1)S(1)}, u32[]{:S(2)}, u32[]{:S(2)}) collective-permute-start(bf16[352,256]{1,0:T(8,128)(2,1)S(1)} %get-tuple-element.48), channel_id=1, source_target_pairs={{0,16},{4,20},{8,24},{12,28},{16,0},{20,4},{24,8},{28,12},{1,17},{... | collective-permute-start | bytes 540680 | tf_op jit(solution)/shard_map/ppermute | solution.py:416
  5.7 8.2 %collective-permute-start.1 = (bf16[352,256]{1,0:T(8,128)(2,1)S(1)}, bf16[352,256]{1,0:T(8,128)(2,1)S(1)}, u32[]{:S(2)}, u32[]{:S(2)}) collective-permute-start(bf16[352,256]{1,0:T(8,128)(2,1)S(1)} %get-tuple-element.49), channel_id=1, source_target_pairs={{0,8},{4,12},{8,0},{12,4},{16,24},{20,28},{24,16},{28,20},{1,9},{5... | collective-permute-start | bytes 540680 | tf_op jit(solution)/shard_map/ppermute | solution.py:416
  8.8 18.2 %collective-permute-start.4 = (bf16[608,256]{1,0:T(8,128)(2,1)S(1)}, bf16[608,256]{1,0:T(8,128)(2,1)S(1)}, u32[]{:S(2)}, u32[]{:S(2)}) collective-permute-start(bf16[608,256]{1,0:T(8,128)(2,1)S(1)} %get-tuple-element.55), channel_id=1, source_target_pairs={{0,20},{4,16},{8,28},{12,24},{16,4},{20,0},{24,12},{28,8},{1,21},{... | collective-permute-start | bytes 933896 | tf_op jit(solution)/shard_map/ppermute | solution.py:416
  8.9 19.8 %collective-permute-start.5 = (bf16[608,256]{1,0:T(8,128)(2,1)S(1)}, bf16[608,256]{1,0:T(8,128)(2,1)S(1)}, u32[]{:S(2)}, u32[]{:S(2)}) collective-permute-start(bf16[608,256]{1,0:T(8,128)(2,1)S(1)} %get-tuple-element.56), channel_id=1, source_target_pairs={{0,12},{4,8},{8,4},{12,0},{16,28},{20,24},{24,20},{28,16},{1,13},{... | collective-permute-start | bytes 933896 | tf_op jit(solution)/shard_map/ppermute | solution.py:416
  9.2 20.4 %collective-permute-start.6 = (bf16[608,256]{1,0:T(8,128)(2,1)S(1)}, bf16[608,256]{1,0:T(8,128)(2,1)S(1)}, u32[]{:S(2)}, u32[]{:S(2)}) collective-permute-start(bf16[608,256]{1,0:T(8,128)(2,1)S(1)} %get-tuple-element.57), channel_id=1, source_target_pairs={{0,4},{4,0},{8,12},{12,8},{16,20},{20,16},{24,28},{28,24},{1,5},{5... | collective-permute-start | bytes 933896 | tf_op jit(solution)/shard_map/ppermute | solution.py:416
  10.2 14.0 %collective-permute-start.2 = (bf16[352,256]{1,0:T(8,128)(2,1)S(1)}, bf16[352,256]{1,0:T(8,128)(2,1)S(1)}, u32[]{:S(2)}, u32[]{:S(2)}) collective-permute-start(bf16[352,256]{1,0:T(8,128)(2,1)S(1)} %get-tuple-element.50), channel_id=1, source_target_pairs={{0,24},{4,28},{8,16},{12,20},{16,8},{20,12},{24,0},{28,4},{1,25},{... | collective-permute-start | bytes 540680 | tf_op jit(solution)/shard_map/ppermute | solution.py:416
  13.8 11.4 %collective-permute-start.3 = (bf16[352,256]{1,0:T(8,128)(2,1)S(1)}, bf16[352,256]{1,0:T(8,128)(2,1)S(1)}, u32[]{:S(2)}, u32[]{:S(2)}) collective-permute-start(bf16[352,256]{1,0:T(8,128)(2,1)S(1)} %get-tuple-element.51), channel_id=1, source_target_pairs={{0,28},{4,24},{8,20},{12,16},{16,12},{20,8},{24,4},{28,0},{1,29},{... | collective-permute-start | bytes 540680 | tf_op jit(solution)/shard_map/ppermute | solution.py:416
  24.2 11.3 %collective-permute-start.10 = (bf16[256,256]{1,0:T(8,128)(2,1)S(1)}, bf16[256,256]{1,0:T(8,128)(2,1)S(1)}, u32[]{:S(2)}, u32[]{:S(2)}) collective-permute-start(bf16[256,256]{1,0:T(8,128)(2,1)S(1)} %get-tuple-element.64), channel_id=1, source_target_pairs={{0,16},{4,20},{8,24},{12,28},{16,0},{20,4},{24,8},{28,12},{1,17},{... | collective-permute-start | bytes 393224 | tf_op jit(solution)/shard_map/ppermute | solution.py:416
  25.2 11.6 %collective-permute-start.7 = (bf16[256,256]{1,0:T(8,128)(2,1)S(1)}, bf16[256,256]{1,0:T(8,128)(2,1)S(1)}, u32[]{:S(2)}, u32[]{:S(2)}) collective-permute-start(bf16[256,256]{1,0:T(8,128)(2,1)S(1)} %get-tuple-element.61), channel_id=1, source_target_pairs={{0,8},{4,12},{8,0},{12,4},{16,24},{20,28},{24,16},{28,20},{1,9},{5... | collective-permute-start | bytes 393224 | tf_op jit(solution)/shard_map/ppermute | solution.py:416
  27.0 9.8 %collective-permute-start.8 = (bf16[256,256]{1,0:T(8,128)(2,1)S(1)}, bf16[256,256]{1,0:T(8,128)(2,1)S(1)}, u32[]{:S(2)}, u32[]{:S(2)}) collective-permute-start(bf16[256,256]{1,0:T(8,128)(2,1)S(1)} %get-tuple-element.62), channel_id=1, source_target_pairs={{0,24},{4,28},{8,16},{12,20},{16,8},{20,12},{24,0},{28,4},{1,25},{... | collective-permute-start | bytes 393224 | tf_op jit(solution)/shard_map/ppermute | solution.py:416
  28.7 9.1 %collective-permute-start.9 = (bf16[256,256]{1,0:T(8,128)(2,1)S(1)}, bf16[256,256]{1,0:T(8,128)(2,1)S(1)}, u32[]{:S(2)}, u32[]{:S(2)}) collective-permute-start(bf16[256,256]{1,0:T(8,128)(2,1)S(1)} %get-tuple-element.63), channel_id=1, source_target_pairs={{0,28},{4,24},{8,20},{12,16},{16,12},{20,8},{24,4},{28,0},{1,29},{... | collective-permute-start | bytes 393224 | tf_op jit(solution)/shard_map/ppermute | solution.py:416
  33.8 8.1 %collective-permute-start.13 = (bf16[256,256]{1,0:T(8,128)(2,1)S(1)}, bf16[256,256]{1,0:T(8,128)(2,1)S(1)}, u32[]{:S(2)}, u32[]{:S(2)}) collective-permute-start(bf16[256,256]{1,0:T(8,128)(2,1)S(1)} %get-tuple-element.70), channel_id=1, source_target_pairs={{0,28},{4,24},{8,20},{12,16},{16,12},{20,8},{24,4},{28,0},{1,29},{... | collective-permute-start | bytes 393224 | tf_op jit(solution)/shard_map/ppermute | solution.py:416
  35.5 8.2 %collective-permute-start.18 = (bf16[256,256]{1,0:T(8,128)(2,1)S(1)}, bf16[256,256]{1,0:T(8,128)(2,1)S(1)}, u32[]{:S(2)}, u32[]{:S(2)}) collective-permute-start(bf16[256,256]{1,0:T(8,128)(2,1)S(1)} %get-tuple-element.80), channel_id=1, source_target_pairs={{0,24},{4,28},{8,16},{12,20},{16,8},{20,12},{24,0},{28,4},{1,25},{... | collective-permute-start | bytes 393224 | tf_op jit(solution)/shard_map/ppermute | solution.py:416
  37.8 14.4 %copy-start.5 = (bf16[256,2048]{1,0:T(8,128)(2,1)S(1)}, bf16[256,2048]{1,0:T(8,128)(2,1)}, u32[]{:S(2)}) copy-start(bf16[256,2048]{1,0:T(8,128)(2,1)} %refs_0_.2) | copy-start | bytes 3145732
  37.8 14.4 %copy-start.6 = (bf16[256,2048]{1,0:T(8,128)(2,1)S(1)}, bf16[256,2048]{1,0:T(8,128)(2,1)}, u32[]{:S(2)}) copy-start(bf16[256,2048]{1,0:T(8,128)(2,1)} %param.13) | copy-start | bytes 3145732
  41.9 11.7 %copy-start = (bf16[256,2048]{1,0:T(8,128)(2,1)S(1)}, bf16[256,2048]{1,0:T(8,128)(2,1)}, u32[]{:S(2)}) copy-start(bf16[256,2048]{1,0:T(8,128)(2,1)} %refs_5_.3) | copy-start | bytes 3145732
  41.9 11.7 %copy-start.1 = (bf16[256,2048]{1,0:T(8,128)(2,1)S(1)}, bf16[256,2048]{1,0:T(8,128)(2,1)}, u32[]{:S(2)}) copy-start(bf16[256,2048]{1,0:T(8,128)(2,1)} %refs_6_.3) | copy-start | bytes 3145732
  41.9 7.5 %collective-permute-start.14 = (bf16[352,256]{1,0:T(8,128)(2,1)S(1)}, bf16[352,256]{1,0:T(8,128)(2,1)S(1)}, u32[]{:S(2)}, u32[]{:S(2)}) collective-permute-start(bf16[352,256]{1,0:T(8,128)(2,1)S(1)} %get-tuple-element.71), channel_id=1, source_target_pairs={{0,8},{4,12},{8,0},{12,4},{16,24},{20,28},{24,16},{28,20},{1,9},{5... | collective-permute-start | bytes 540680 | tf_op jit(solution)/shard_map/ppermute | solution.py:416
  43.8 8.0 %collective-permute-start.19 = (bf16[352,256]{1,0:T(8,128)(2,1)S(1)}, bf16[352,256]{1,0:T(8,128)(2,1)S(1)}, u32[]{:S(2)}, u32[]{:S(2)}) collective-permute-start(bf16[352,256]{1,0:T(8,128)(2,1)S(1)} %get-tuple-element.81), channel_id=1, source_target_pairs={{0,16},{4,20},{8,24},{12,28},{16,0},{20,4},{24,8},{28,12},{1,17},{... | collective-permute-start | bytes 540680 | tf_op jit(solution)/shard_map/ppermute | solution.py:416
  44.7 10.2 %collective-permute-start.11 = (bf16[352,256]{1,0:T(8,128)(2,1)S(1)}, bf16[352,256]{1,0:T(8,128)(2,1)S(1)}, u32[]{:S(2)}, u32[]{:S(2)}) collective-permute-start(bf16[352,256]{1,0:T(8,128)(2,1)S(1)} %get-tuple-element.66), channel_id=1, source_target_pairs={{0,20},{4,16},{8,28},{12,24},{16,4},{20,0},{24,12},{28,8},{1,21},{... | collective-permute-start | bytes 540680 | tf_op jit(solution)/shard_map/ppermute | solution.py:416
  45.2 9.7 %collective-permute-start.12 = (bf16[352,256]{1,0:T(8,128)(2,1)S(1)}, bf16[352,256]{1,0:T(8,128)(2,1)S(1)}, u32[]{:S(2)}, u32[]{:S(2)}) collective-permute-start(bf16[352,256]{1,0:T(8,128)(2,1)S(1)} %get-tuple-element.67), channel_id=1, source_target_pairs={{0,12},{4,8},{8,4},{12,0},{16,28},{20,24},{24,20},{28,16},{1,13},{... | collective-permute-start | bytes 540680 | tf_op jit(solution)/shard_map/ppermute | solution.py:416
  49.4 5.5 %collective-permute-start.17 = (bf16[96,256]{1,0:T(8,128)(2,1)S(1)}, bf16[96,256]{1,0:T(8,128)(2,1)S(1)}, u32[]{:S(2)}, u32[]{:S(2)}) collective-permute-start(bf16[96,256]{1,0:T(8,128)(2,1)S(1)} %get-tuple-element.78), channel_id=1, source_target_pairs={{0,28},{4,24},{8,20},{12,16},{16,12},{20,8},{24,4},{28,0},{1,29},{... | collective-permute-start | bytes 147464 | tf_op jit(solution)/shard_map/ppermute | solution.py:416
  49.9 5.6 %collective-permute-start.16 = (bf16[96,256]{1,0:T(8,128)(2,1)S(1)}, bf16[96,256]{1,0:T(8,128)(2,1)S(1)}, u32[]{:S(2)}, u32[]{:S(2)}) collective-permute-start(bf16[96,256]{1,0:T(8,128)(2,1)S(1)} %get-tuple-element.75), channel_id=1, source_target_pairs={{0,24},{4,28},{8,16},{12,20},{16,8},{20,12},{24,0},{28,4},{1,25},{... | collective-permute-start | bytes 147464 | tf_op jit(solution)/shard_map/ppermute | solution.py:416
  51.8 3.7 %collective-permute-start.15 = (bf16[352,256]{1,0:T(8,128)(2,1)S(1)}, bf16[352,256]{1,0:T(8,128)(2,1)S(1)}, u32[]{:S(2)}, u32[]{:S(2)}) collective-permute-start(bf16[352,256]{1,0:T(8,128)(2,1)S(1)} %get-tuple-element.72), channel_id=1, source_target_pairs={{0,4},{4,0},{8,12},{12,8},{16,20},{20,16},{24,28},{28,24},{1,5},{5... | collective-permute-start | bytes 540680 | tf_op jit(solution)/shard_map/ppermute | solution.py:416
